TPU v7x, 256 devices: a whole 4x4x8 slice. The times are simulated.
256 devices in a mesh: rep: 32 (over x, z), own: 8 (over y, core).
Axes of the slice: x: 4, y: 4, z: 8, core: 2. Of those that a mesh axis runs over, the one named last changes fastest.
Arguments:
- grads: bfloat16 [32, 4096, 4096], P('rep', 'own'), may hold values from -1.1953125 to 1.1953125
- momentum: bfloat16 [8, 512, 8, 512], P(None, 'rep', 'own'), may hold values from -3 to 3
- second: float32 [8, 512, 8, 512], P(None, 'rep', 'own'), may hold values from 0.005 to 200
- left_roots: bfloat16 [8, 8, 512, 512], P(None, 'own', 'rep'), may hold values from -0.10606602 to 2, as said below
- right_roots: bfloat16 [8, 8, 512, 512], P(None, 'own'), may hold values from -0.10606602 to 2, as said below
Outputs:
- direction: bfloat16 [4096, 4096], P('own')
- new_momentum: bfloat16 [8, 512, 8, 512], P(None, 'rep', 'own')
- new_second: float32 [8, 512, 8, 512], P(None, 'rep', 'own')
Inputs may be any that keep to these rules, and one draw needn't show every extreme that they name: `left_roots`: each block is symmetric. `right_roots`: each block is symmetric.
All inputs are finite; a program needn't handle non-finite values.
Results may differ from a plain program's by a relative error of at most 0.024.
Values may be sent and summed in bfloat16 or wider, within the bound.
No kernel may reach another device: no remote copies, remote signals or barrier semaphores. Data moves between devices by JAX's collectives and lax.ppermute only.
A program may use at most 128 MiB of HBM per device.

v0:
```python
import jax
import jax.numpy as jnp
from jax import lax
from jax.sharding import PartitionSpec as P

BETA_ONE = 0.9
BETA_TWO = 0.95
CORRECT_ONE = 1.0 - 0.9**10
CORRECT_TWO = 1.0 - 0.95**10
ADAM_EPS = 1e-08
NORM_EPS = 1e-06


def on_device(grads, momentum, second, left_roots, right_roots):
    rep_count = lax.axis_size("rep")
    own_count = lax.axis_size("own")
    row_count = grads.shape[1]
    full_width = grads.shape[2]
    block_size = right_roots.shape[-1]
    dev_rows = left_roots.shape[2]
    slab_blocks = row_count // block_size
    col_blocks = right_roots.shape[1]
    replica_terms = (
        grads[0].astype(jnp.float32).reshape(slab_blocks, rep_count, dev_rows, full_width)
    )
    summed = lax.psum_scatter(
        replica_terms.astype(jnp.bfloat16), "rep", scatter_dimension=1, tiled=True
    ).astype(jnp.float32)
    regrouped = summed.reshape(slab_blocks, dev_rows, own_count, full_width // own_count)
    owner_layout = lax.all_to_all(
        regrouped.astype(jnp.bfloat16), "own", split_axis=2, concat_axis=0, tiled=True
    ).astype(regrouped.dtype)
    moment_f = BETA_ONE * momentum.astype(jnp.float32) + (1.0 - BETA_ONE) * owner_layout
    new_second = BETA_TWO * second + (1.0 - BETA_TWO) * owner_layout * owner_layout
    adam_step = moment_f / CORRECT_ONE / (jnp.sqrt(new_second / CORRECT_TWO) + ADAM_EPS)
    adam_sq = jnp.sum(adam_step * adam_step, axis=(1, 3))
    g_low = owner_layout.astype(jnp.bfloat16)
    right_product = jnp.einsum(
        "ikjl,ijlm->ikjm", g_low, right_roots, preferred_element_type=jnp.float32
    ).astype(jnp.bfloat16)
    shampoo = jnp.einsum(
        "ijkl,iljm->ikjm",
        left_roots,
        lax.all_gather(right_product, "rep", axis=1, tiled=True),
        preferred_element_type=jnp.float32,
    )
    shampoo_sq = jnp.sum(shampoo * shampoo, axis=(1, 3))
    adam_total, shampoo_total = lax.psum((adam_sq, shampoo_sq), "rep")
    graft_scale = jnp.sqrt((adam_total + NORM_EPS) / (shampoo_total + NORM_EPS))
    direction = (shampoo * graft_scale[:, None, :, None]).astype(jnp.bfloat16)
    full_rows = lax.all_gather(direction, "rep", axis=1, tiled=True)
    grouped = full_rows.reshape(own_count, slab_blocks, block_size, col_blocks, block_size)
    received = lax.all_to_all(grouped, "own", split_axis=0, concat_axis=3, tiled=True)
    assembled = received.reshape(row_count, full_width)
    return (assembled, moment_f.astype(jnp.bfloat16), new_second)


def solution(mesh):
    in_specs = (
        P("rep", "own", None),
        P(None, "rep", "own", None),
        P(None, "rep", "own", None),
        P(None, "own", "rep", None),
        P(None, "own", None, None),
    )
    out_specs = (P("own", None), P(None, "rep", "own", None), P(None, "rep", "own", None))
    return jax.shard_map(
        on_device, mesh=mesh, in_specs=in_specs, out_specs=out_specs, check_vma=False
    )
```

profile of v0, /device:TPU:96, one launch (start us, length us, event | category | flops | bytes accessed | tf_op | source)
XLA Modules:
  0.0 553.0 jit_solution(4485706091925957305)
XLA Ops:
  7.2 0.0 copy-start
  7.2 0.0 reduce-scatter.2.cloned.1.call-start
  7.2 0.0 copy-start.1
  7.2 0.0 copy-start.2
  7.2 0.7 reduce-scatter.2.cloned.1.call-update
  7.9 0.0 all-gather.3.cloned.1.call-start
  8.0 225.6 %reduce-scatter.2.cloned.1.call-done = bf16[1,1,16,4096]{3,2,1,0:T(8,128)(2,1)} async-done(((bf16[1,32,16,4096]{3,2,1,0:T(8,128)(2,1)}), bf16[1,1,16,4096]{3,2,1,0:T(8,128)(2,1)}) %reduce-scatter.2.cloned.1.call-update) | async-done | bytes 131088 | tf_op jit(solution)/shard_map/reduce_scatter | solution.py:26
  233.6 0.9 copy.27
  234.6 10.2 %all_to_all.30 = bf16[1,16,8,512]{3,1,0,2:T(8,128)(2,1)S(1)} all-to-all(bf16[1,16,8,512]{3,1,0,2:T(8,128)(2,1)S(1)} %copy.19), channel_id=1, replica_groups=mesh['rep'=32,'own'=8] {'own'}, dimensions={2} | all-to-all | bytes 262144 | tf_op jit(solution)/shard_map/all_to_all | solution.py:30
  244.8 3.5 fusion.10
  248.3 0.0 all-gather.3.cloned.1.call-update
  248.3 0.0 all-gather.5.cloned.1.call-start
  248.4 0.0 copy-done.1
  248.4 0.0 copy-done.2
  248.4 0.9 fusion.14
  249.3 78.3 %all-gather.3.cloned.1.call-done = bf16[8,512,1,512]{3,1,0,2:T(8,128)(2,1)} async-done(((bf16[8,16,1,512]{3,1,0,2:T(8,128)(2,1)}), bf16[8,512,1,512]{3,1,0,2:T(8,128)(2,1)}) %all-gather.3.cloned.1.call-update) | async-done | bytes 4194320 | tf_op jit(solution)/shard_map/all_gather | solution.py:44
  327.6 0.0 copy-done
  327.6 2.9 multiply_reduce_fusion
  330.5 65.9 %all-reduce = (f32[8,1]{0,1:T(1,128)S(1)}, f32[8,1]{0,1:T(1,128)S(1)}) all-reduce(f32[8,1]{0,1:T(1,128)S(1)} %bitcast.71, f32[8,1]{0,1:T(1,128)S(1)} %bitcast.70), channel_id=1, replica_groups=mesh['rep'=32,'own'=8] {'rep'}, use_global_device_ids=true, to_apply=%region_4.0 | all-reduce | flops 16 | bytes 128 | tf_op jit(solution)/shard_map/psum | solution.py:48
  396.5 0.8 fusion.17
  397.2 0.0 all-gather.5.cloned.1.call-update
  397.2 82.1 %all-gather.5.cloned.1.call-done = bf16[8,512,1,512]{3,1,0,2:T(8,128)(2,1)} async-done(((bf16[8,16,1,512]{3,1,0,2:T(8,128)(2,1)}), bf16[8,512,1,512]{3,1,0,2:T(8,128)(2,1)}) %all-gather.5.cloned.1.call-update) | async-done | bytes 4194320 | tf_op jit(solution)/shard_map/all_gather | solution.py:51
  479.4 4.5 all-to-all-start.1
  483.9 1.0 copy.26
  484.9 48.7 %all-to-all-done.1 = bf16[8,1,512,1,512]{4,2,3,1,0:T(8,128)(2,1)} async-done(((bf16[8,1,512,1,512]{4,2,3,1,0:T(8,128)(2,1)}), bf16[8,1,512,1,512]{4,2,3,1,0:T(8,128)(2,1)}, u32[]{:S(2)}, u32[]{:S(2)}) %all-to-all-start.1) | async-done | bytes 4194336 | tf_op jit(solution)/shard_map/all_to_all | solution.py:53
  533.6 6.5 %copy.23 = bf16[8,1,512,1,512]{2,4,0,3,1:T(8,128)(2,1)} copy(bf16[8,1,512,1,512]{4,2,3,1,0:T(8,128)(2,1)} %all-to-all-done.1) | data formatting | bytes 8388608 | tf_op jit(solution)/shard_map/all_to_all | solution.py:53
  540.1 6.3 %copy.24 = bf16[512,4096]{1,0:T(8,128)(2,1)} copy(bf16[512,4096]{0,1:T(8,128)(2,1)} %bitcast.65) | data formatting | bytes 8388608
  (2 shorter events, 0.1 us)
Async XLA Ops:
  7.2 320.4 %copy-start = (bf16[8,1,16,512]{3,2,1,0:T(8,128)(2,1)S(1)}, bf16[8,1,16,512]{3,2,1,0:T(8,128)(2,1)}, u32[]{:S(2)}) copy-start(bf16[8,1,16,512]{3,2,1,0:T(8,128)(2,1)} %param.8) | copy-start | bytes 393220
  7.2 226.4 %reduce-scatter.2.cloned.1.call-start = ((), (), s32[]{:S(2)}) async-start(), calls=%async_computation.3 | async-start | bytes 4325376 | tf_op jit(solution)/shard_map/reduce_scatter | solution.py:26
  7.2 241.2 %copy-start.1 = (f32[8,16,1,512]{3,2,1,0:T(1,128)S(1)}, f32[8,16,1,512]{3,2,1,0:T(1,128)}, u32[]{:S(2)}) copy-start(f32[8,16,1,512]{3,2,1,0:T(1,128)} %param.7) | copy-start | bytes 786436
  7.2 241.2 %copy-start.2 = (bf16[8,16,1,512]{3,1,2,0:T(8,128)(2,1)S(1)}, bf16[8,16,1,512]{3,1,2,0:T(8,128)(2,1)}, u32[]{:S(2)}) copy-start(bf16[8,16,1,512]{3,1,2,0:T(8,128)(2,1)} %param.6) | copy-start | bytes 393220
  7.9 319.6 %all-gather.3.cloned.1.call-start = ((), (), s32[]{:S(2)}) async-start(), calls=%async_computation.4 | async-start | bytes 4325376 | tf_op jit(solution)/shard_map/all_gather | solution.py:44
  248.3 231.0 %all-gather.5.cloned.1.call-start = ((), (), s32[]{:S(2)}) async-start(), calls=%async_computation.5 | async-start | bytes 4325376 | tf_op jit(solution)/shard_map/all_gather | solution.py:51
  479.4 54.2 %all-to-all-start.1 = ((bf16[8,1,512,1,512]{4,2,3,1,0:T(8,128)(2,1)}), bf16[8,1,512,1,512]{4,2,3,1,0:T(8,128)(2,1)}, u32[]{:S(2)}, u32[]{:S(2)}) async-start(bf16[8,1,512,1,512]{4,2,3,1,0:T(8,128)(2,1)} %bitcast.67), calls=%async_computation.2 | async-start | bytes 8388608 | tf_op jit(solution)/shard_map/all_to_all | solution.py:53
Sparse Core Ops, SparseCore 0:
  11.9 221.6 reduce-scatter.1
  248.5 79.0 all-gather.2
  397.4 81.9 all-gather.4
where the time goes:
time: 556 us; the launch traced here: 553 us
  waiting for transfers between devices  435 us (78%)
  blocking collectives  76.2 us (14%)
  local copies, waits for them, and re-layouts  14.8 us (3%)
  between operations  13.8 us (2%)
  matrix products  6.44 us (1%)
    reduce_scatter x1, waiting for transfers between devices, on_device(): lax.psum_scatter(replica_terms.astype(jnp.bfloat16), 'rep', scatter_dimen...  226 us
    all_gather x1, waiting for transfers between devices, on_device(): full_rows = lax.all_gather(direction, 'rep', axis=1, tiled=True)  82.1 us
    all_gather x1, waiting for transfers between devices, on_device(): lax.all_gather(right_product, 'rep', axis=1, tiled=True)  78.3 us
    psum x1, blocking collectives, on_device(): adam_total, shampoo_total = lax.psum((adam_sq, shampoo_sq), 'rep')  65.9 us
    all_to_all x1, waiting for transfers between devices, on_device(): lax.all_to_all(grouped, 'own', split_axis=0, concat_axis=3, tiled=True)  48.7 us
  transfers between devices with their start and end apart: 4, of which 4 were waited for; matrix products, arithmetic and copies ran while one was open for 0% of the time, Pallas kernels for 0%

commit v1 on v0

v1 whole, which is shorter than its diff:
```python
import functools

import jax
import jax.numpy as jnp
from jax import lax
from jax.experimental import pallas as pl
from jax.experimental.pallas import tpu as pltpu
from jax.sharding import Mesh, PartitionSpec as P

BETA_ONE = 0.9
BETA_TWO = 0.95
CORRECT_ONE = 1.0 - 0.9**10
CORRECT_TWO = 1.0 - 0.95**10
ADAM_EPS = 1e-08
NORM_EPS = 1e-06

NX, NZ, NY, NC = 4, 8, 4, 2
OWN = ("y", "core")
BS = 512
QROWS = BS // NX
DROWS = QROWS // NZ
HROWS = BS // 2
SHIFTS = (0, 1, 3, 2)
SUMS = 16
HALF = NZ * BS // 2
VMEM = 40 * 1024 * 1024
PARAMS = pltpu.CompilerParams(vmem_limit_bytes=VMEM)
ALL_VMEM = pltpu.CompilerParams(vmem_limit_bytes=57 * 1024 * 1024)
F32, BF16 = jnp.float32, jnp.bfloat16


def cost(flops, nbytes):
    return pl.CostEstimate(flops=flops, bytes_accessed=nbytes, transcendentals=0)


def moments(g, m, v):
    moment = BETA_ONE * m.astype(F32) + (1.0 - BETA_ONE) * g
    second = BETA_TWO * v.astype(F32) + (1.0 - BETA_TWO) * g * g
    return moment, second


def staged(loads, stores, sems):
    for k, (src, dst) in enumerate(loads):
        pltpu.make_async_copy(src, dst, sems.at[0, k]).start()
    for k, (src, dst) in enumerate(loads):
        pltpu.make_async_copy(src, dst, sems.at[0, k]).wait()
        if k < len(stores):
            pltpu.make_async_copy(*stores[k], sems.at[1, k]).start()
    for k, (src, dst) in enumerate(stores):
        pltpu.make_async_copy(src, dst, sems.at[1, k]).wait()


def pick_kernel(x_ref, src_ref, left_ref, right_ref, hold_ref, sems):
    loads, stores = [], []
    for half, out_ref in enumerate((left_ref, right_ref)):
        for k, bits in enumerate(((1, 2), (3, 2))[half]):
            cols = pl.ds(half * HALF, HALF)
            held = hold_ref.at[2 * half + k]
            loads.append((src_ref.at[x_ref[0] ^ bits, :, cols], held))
            stores.append((held, out_ref.at[k]))
    staged(loads, stores, sems)


def pick(grads, x):
    anywhere = pl.BlockSpec(memory_space=pl.ANY)
    return pl.pallas_call(
        pick_kernel,
        in_specs=[pl.BlockSpec(memory_space=pltpu.SMEM), anywhere],
        out_specs=(anywhere, anywhere),
        out_shape=(jax.ShapeDtypeStruct((2, QROWS, HALF), BF16),) * 2,
        scratch_shapes=[pltpu.VMEM((4, QROWS, HALF), BF16), pltpu.SemaphoreType.DMA((2, 4))],
        compiler_params=ALL_VMEM,
        cost_estimate=cost(0, 4 << 20),
    )(x, grads)


def pack_kernel(x_ref, z_ref, after_ref, right_ref, *refs):
    out_ref, hold_ref, sems = refs[-3:]
    row = pl.multiple_of(x_ref[0] * QROWS + z_ref[0] * DROWS, DROWS)
    parts = [right_ref.at[:, pl.ds(row, DROWS)], *refs[:-3]]
    loads = [
        (part, hold_ref.at[:, pl.ds(k * DROWS, DROWS)]) for k, part in enumerate(parts)
    ]
    staged(loads[:-1], [], sems)
    staged(loads[-1:], [(hold_ref, out_ref)], sems)


def pack(x, z, after, right, *states):
    anywhere = pl.BlockSpec(memory_space=pl.ANY)
    smem = pl.BlockSpec(memory_space=pltpu.SMEM)
    shape = (NZ, (1 + len(states)) * DROWS, BS)
    return pl.pallas_call(
        pack_kernel,
        in_specs=[smem, smem] + [anywhere] * (2 + len(states)),
        out_specs=anywhere,
        out_shape=jax.ShapeDtypeStruct(shape, BF16),
        scratch_shapes=[pltpu.VMEM(shape, BF16), pltpu.SemaphoreType.DMA((2, 4))],
        compiler_params=ALL_VMEM,
        cost_estimate=cost(0, 1 << 20),
    )(x, z, after, right, *states)


def add_kernel(where_ref, src_ref, got_ref, out_ref):
    out_ref[...] = (src_ref[0].astype(F32) + got_ref[0].astype(F32)).astype(BF16)


def add_quarter(grads, got, quarter, half):
    return pl.pallas_call(
        add_kernel,
        grid_spec=pltpu.PrefetchScalarGridSpec(
            num_scalar_prefetch=1,
            grid=(2,),
            in_specs=[
                pl.BlockSpec((1, QROWS, HALF // 2), lambda c, where: (where[0], 0, 2 * half + c)),
                pl.BlockSpec((1, QROWS, HALF // 2), lambda c, where: (1, 0, c)),
            ],
            out_specs=pl.BlockSpec((QROWS, HALF // 2), lambda c, where: (0, c)),
        ),
        out_shape=jax.ShapeDtypeStruct((QROWS, HALF), BF16),
        compiler_params=PARAMS,
        cost_estimate=cost(1 << 19, 3 << 19),
    )(quarter, grads, got)


def sum_kernel(where_ref, *refs):
    out_ref = refs[-1]
    for half in range(2):
        mine_ref, first_ref, second_ref = refs[3 * half : 3 * half + 3]
        total = mine_ref[0].astype(F32) + first_ref[0].astype(F32) + second_ref[...].astype(F32)
        out_ref[half, 0] = total.astype(BF16)


def sum_quarter(grads, firsts, seconds, quarter):
    specs, args = [], []
    for half in range(2):
        specs += [
            pl.BlockSpec((1, QROWS, BS), lambda j, where, half=half: (where[0], 0, 4 * half + j)),
            pl.BlockSpec((1, QROWS, BS), lambda j, where: (0, 0, j)),
            pl.BlockSpec((QROWS, BS), lambda j, where: (0, j)),
        ]
        args += [grads, firsts[half], seconds[half]]
    total = pl.pallas_call(
        sum_kernel,
        grid_spec=pltpu.PrefetchScalarGridSpec(
            num_scalar_prefetch=1,
            grid=(NZ // 2,),
            in_specs=specs,
            out_specs=pl.BlockSpec((2, 1, QROWS, BS), lambda j, where: (0, j, 0, 0)),
        ),
        out_shape=jax.ShapeDtypeStruct((2, NZ // 2, QROWS, BS), BF16),
        compiler_params=PARAMS,
        cost_estimate=cost(1 << 20, 28 << 20),
    )(quarter, *args)
    return total.reshape(NZ, QROWS, BS)


def right_kernel(x_ref, parts_ref, pre_ref, *refs):
    roots, (low_ref, prod_ref) = refs[:NX], refs[NX:]
    g = parts_ref[0].astype(F32)
    for k in range(1, NZ):
        g += parts_ref[k].astype(F32)
    low_ref[...] = g.astype(BF16)
    prod = None
    for by, root_ref in zip(SHIFTS, roots):
        col = pl.multiple_of(lax.rem(x_ref[0] + NX - by, NX) * QROWS, QROWS)
        right = root_ref[:, :DROWS].reshape(QROWS, BS)
        term = jnp.dot(low_ref[:, pl.ds(col, QROWS)], right, preferred_element_type=F32)
        prod = term if prod is None else prod + term
    prod_ref[:QROWS] = prod.astype(BF16)
    m = pre_ref[:, 2 * DROWS : 3 * DROWS].reshape(QROWS, BS)
    v = pre_ref[:, 3 * DROWS :].reshape(QROWS, BS)
    moment, second = moments(g, m, v)
    step = moment / CORRECT_ONE / (jnp.sqrt(second / CORRECT_TWO) + ADAM_EPS)
    total = jnp.full((SUMS, BS), jnp.sum(step * step), F32)
    high = total.astype(BF16).astype(F32)
    first = lax.broadcasted_iota(jnp.int32, (SUMS, BS), 0) == 0
    prod_ref[QROWS:] = jnp.where(first, high, total - high).astype(BF16)


def right_stage(x, parts, pre, roots):
    full = pl.BlockSpec(memory_space=pltpu.VMEM)
    return pl.pallas_call(
        right_kernel,
        in_specs=[pl.BlockSpec(memory_space=pltpu.SMEM)] + [full] * (2 + NX),
        out_shape=(
            jax.ShapeDtypeStruct((QROWS, BS), BF16),
            jax.ShapeDtypeStruct((QROWS + SUMS, BS), BF16),
        ),
        compiler_params=PARAMS,
        cost_estimate=cost(1 << 26, 2 << 20),
    )(x, parts, pre, *roots)


def left_kernel(x_ref, *refs):
    prods, roots, (out_ref, up_ref, down_ref) = refs[:NX], refs[NX : 2 * NX], refs[2 * NX :]
    shampoo, adam_sq = None, None
    for prod_ref, root_ref in zip(prods, roots):
        term = lax.dot_general(
            root_ref[:, DROWS:].reshape(QROWS, BS),
            prod_ref[:QROWS],
            (((0,), (0,)), ((), ())),
            preferred_element_type=F32,
        )
        sums = prod_ref[QROWS:].astype(F32)
        part = sums[0:1, 0:1] + sums[1:2, 0:1]
        shampoo = term if shampoo is None else shampoo + term
        adam_sq = part if adam_sq is None else adam_sq + part
    scale = jnp.sqrt((adam_sq + NORM_EPS) / (jnp.sum(shampoo * shampoo) + NORM_EPS))
    out_ref[...] = (shampoo * scale).astype(BF16)
    up_ref[...] = out_ref[pl.ds(pl.multiple_of((x_ref[0] & 1) * HROWS, HROWS), HROWS)]
    down_ref[...] = out_ref[pl.ds(pl.multiple_of((x_ref[0] >> 1) * HROWS, HROWS), HROWS)]


def left_stage(x, prods, roots):
    full = pl.BlockSpec(memory_space=pltpu.VMEM)
    return pl.pallas_call(
        left_kernel,
        in_specs=[pl.BlockSpec(memory_space=pltpu.SMEM)] + [full] * (2 * NX),
        out_shape=(
            jax.ShapeDtypeStruct((BS, BS), BF16),
            jax.ShapeDtypeStruct((HROWS, BS), BF16),
            jax.ShapeDtypeStruct((HROWS, BS), BF16),
        ),
        compiler_params=PARAMS,
        cost_estimate=cost(1 << 28, 3 << 19),
    )(x, *prods, *roots)


def place_kernel(spots, x_ref, z_ref, *refs):
    srcs, out_ref, sems = refs[:-2], refs[-2], refs[-1]
    halves = {"up": x_ref[0] & 1, "down": x_ref[0] >> 1}
    copies = []
    for k, (src, ring, other, quarter, by) in enumerate(zip(srcs, *zip(*spots))):
        half = 0 if ring is None else (1 - halves[ring] if other else halves[ring])
        row = pl.multiple_of(half * HROWS + quarter * QROWS, QROWS)
        col = pl.multiple_of(lax.rem(z_ref[0] + by, NZ) * BS, BS)
        dst = out_ref.at[pl.ds(row, src.shape[0]), pl.ds(col, BS)]
        copies.append(pltpu.make_async_copy(src, dst, sems.at[k]))
        copies[-1].start()
    for copy in copies:
        copy.wait()


def place(x, z, pieces):
    srcs, spots = [piece[0] for piece in pieces], [piece[1:] for piece in pieces]
    anywhere = pl.BlockSpec(memory_space=pl.ANY)
    smem = pl.BlockSpec(memory_space=pltpu.SMEM)
    return pl.pallas_call(
        functools.partial(place_kernel, spots),
        in_specs=[smem, smem] + [pl.BlockSpec(memory_space=pltpu.VMEM)] * len(srcs),
        out_specs=anywhere,
        out_shape=jax.ShapeDtypeStruct((BS, NZ * BS), BF16),
        scratch_shapes=[pltpu.SemaphoreType.DMA((len(pieces),))],
        compiler_params=PARAMS,
        cost_estimate=cost(0, 4 * sum(src.size for src in srcs)),
    )(x, z, *srcs)


def shift(value, axis, size, by):
    return lax.ppermute(value, axis, [(k, (k + by) % size) for k in range(size)])


def partner(value, bits):
    return lax.ppermute(value, "x", [(k, k ^ bits) for k in range(NX)])


def swap_z_own(value):
    pairs = [(i * NZ + j, j * NZ + i) for i in range(NZ) for j in range(NZ)]
    return lax.ppermute(value, ("z", *OWN), pairs)


def gather_x(value):
    return [value] + [shift(value, "x", NX, by) for by in SHIFTS[1:]]


def exchange(value, axis):
    return lax.all_to_all(value, axis, split_axis=0, concat_axis=0, tiled=True)


def after(value, *others):
    return lax.optimization_barrier((value, *others))[0]


def on_device(grads, momentum, second, left_roots, right_roots):
    x, z = lax.axis_index("x").reshape(1), lax.axis_index("z").reshape(1)
    quarters = grads[0].reshape(NX, QROWS, grads.shape[2])

    steps = (1, 3)
    sends = pick(quarters, x)
    firsts = [partner(sends[h], steps[h]) for h in range(2)]

    low_second = after(second, sends[1])[:, :, 0].astype(BF16)
    pre = pack(
        x, z, sends[1], right_roots[:, 0], left_roots[:, 0], momentum[:, :, 0], low_second
    )
    pre = exchange(after(exchange(pre, OWN), *firsts), "z")
    roots = gather_x(pre[:, : 2 * DROWS])

    seconds = [
        partner(add_quarter(quarters, firsts[h], x ^ steps[1 - h], h), steps[1 - h])
        for h in range(2)
    ]
    over_z = exchange(sum_quarter(quarters, firsts, seconds, x), "z")
    g_low, prod = right_stage(x, over_z, pre, roots)
    block, up, down = left_stage(x, gather_x(prod), roots)

    pieces = [(block, None, False, 0, 0)]
    g_state = swap_z_own(g_low)
    waits, last = (), (g_state,)
    for step in range(1, NZ // 2):
        up, down = (after(half, *waits) for half in (up, down))
        up, down = shift(up, "z", NZ, 1), shift(down, "z", NZ, NZ - 1)
        others = [partner(up, 1), partner(down, 3)]
        pieces += [
            (up, "up", False, 0, NZ - step),
            (down, "down", False, 0, step),
            (others[0], "up", True, 0, NZ - step),
            (others[1], "down", True, 0, step),
        ]
        waits, last = last, others
    up, down = (after(half, *waits) for half in (up, down))
    up, down = shift(up[:QROWS], "z", NZ, 1), shift(down[QROWS:], "z", NZ, NZ - 1)
    pieces += [
        (up, "up", False, 0, NZ // 2),
        (down, "down", False, 1, NZ // 2),
        (partner(up, 1), "up", True, 0, NZ // 2),
        (partner(down, 3), "down", True, 1, NZ // 2),
    ]

    g = exchange(after(g_state, *waits).reshape(NZ, DROWS, BS), "z").astype(F32)[:, :, None]
    new_moment, new_second = moments(g, momentum, second)
    return place(x, z, pieces), new_moment.astype(BF16), new_second


def solution(mesh):
    named = Mesh(mesh.devices.reshape(NX, NZ, NY, NC), ("x", "z", "y", "core"))
    rep = ("x", "z")
    in_specs = (
        P(rep, OWN, None),
        P(None, rep, OWN, None),
        P(None, rep, OWN, None),
        P(None, OWN, rep, None),
        P(None, OWN, None, None),
    )
    out_specs = (P(OWN, None), P(None, rep, OWN, None), P(None, rep, OWN, None))
    return jax.shard_map(
        on_device, mesh=named, in_specs=in_specs, out_specs=out_specs, check_vma=False
    )
```

time: 556 us -> 159 us (0.29)
  waiting for transfers between devices: 435 us -> 63.5 us
  blocking collectives: 76.2 us -> 15 us
  starting transfers between devices: 4.66 us -> 59 us
  between operations: 13.8 us -> 0.95 us
  Pallas kernels: 0 us -> 12.8 us
  local copies, waits for them, and re-layouts: 14.8 us -> 2.91 us
  matrix products: 6.44 us -> 0 us
    reduce_scatter x1 -> x0, waiting for transfers between devices: 226 us -> none  [on_device(): lax.psum_scatter(replica_terms.astype(jnp.bfloat16), 'rep', scatter_dimen...]
    all_gather x2 -> x0, waiting for transfers between devices: 160 us -> none  [the longest x1 82.1 us: on_device(): full_rows = lax.all_gather(direction, 'rep', axis=1, tiled=True)]
    psum x1 -> x0, blocking collectives: 65.9 us -> none  [on_device(): adam_total, shampoo_total = lax.psum((adam_sq, shampoo_sq), 'rep')]
    ppermute x0 -> x27, waiting for transfers between devices: none -> 53.8 us  [the longest x14 26.1 us: shift(): lax.ppermute(value, axis, [(k, (k + by) % size) for k in range(size)])]
    all_to_all x1 -> x3, waiting for transfers between devices: 48.7 us -> 9.69 us  [exchange(): return lax.all_to_all(value, axis, split_axis=0, concat_axis=0, tiled=True)]
    ppermute x0 -> x27, starting transfers between devices: none -> 35.8 us  [the longest x14 21.6 us: shift(): lax.ppermute(value, axis, [(k, (k + by) % size) for k in range(size)])]
    all_to_all x1 -> x3, starting transfers between devices: 4.54 us -> 23.2 us  [exchange(): return lax.all_to_all(value, axis, split_axis=0, concat_axis=0, tiled=True)]
    pallas_call x0 -> x8, Pallas kernels: none -> 12.8 us  [the longest x1 3.25 us: place(): pl.pallas_call(functools.partial(place_kernel, spots), in_specs=[smem, sm...]
  transfers between devices with their start and end apart: 4 -> 30, of which waited for: 4 -> 17; matrix products, arithmetic and copies ran while one was open for 0% -> 3% of each run, Pallas kernels for 0% -> 3%
where the time goes in v1:
time: 159 us
  waiting for transfers between devices  63.5 us (40%)
  starting transfers between devices  59 us (37%)
  blocking collectives  15 us (9%)
  Pallas kernels  12.8 us (8%)
  other arithmetic  4.62 us (3%)
  local copies, waits for them, and re-layouts  2.91 us (2%)
    ppermute x14, waiting for transfers between devices, shift(): lax.ppermute(value, axis, [(k, (k + by) % size) for k in range(size)])  26.1 us
    all_to_all x3, starting transfers between devices, exchange(): return lax.all_to_all(value, axis, split_axis=0, concat_axis=0, tiled=True)  23.2 us
    ppermute x14, starting transfers between devices, shift(): lax.ppermute(value, axis, [(k, (k + by) % size) for k in range(size)])  21.6 us
    ppermute x12, waiting for transfers between devices, partner(): return lax.ppermute(value, 'x', [(k, k ^ bits) for k in range(NX)])  20.8 us
    all_to_all x1, blocking collectives, exchange(): return lax.all_to_all(value, axis, split_axis=0, concat_axis=0, tiled=True)  15 us
    ppermute x12, starting transfers between devices, partner(): return lax.ppermute(value, 'x', [(k, k ^ bits) for k in range(NX)])  11.4 us
    all_to_all x3, waiting for transfers between devices, exchange(): return lax.all_to_all(value, axis, split_axis=0, concat_axis=0, tiled=True)  9.69 us
    ppermute x1, waiting for transfers between devices, swap_z_own(): return lax.ppermute(value, ('z', *OWN), pairs)  6.93 us
  transfers between devices with their start and end apart: 30, of which 17 were waited for; matrix products, arithmetic and copies ran while one was open for 3% of the time, Pallas kernels for 3%

profile of v1, /device:TPU:96, one launch (start us, length us, event | category | flops | bytes accessed | tf_op | source)
XLA Modules:
  0.0 158.7 jit_solution(10711437147485412492)
XLA Ops:
  0.6 2.5 %shard_map.76 = (bf16[2,128,2048]{2,1,0:T(8,128)(2,1)}, bf16[2,128,2048]{2,1,0:T(8,128)(2,1)}) custom-call(s32[1]{0:T(128)} %bitcast.x_ref.where_ref, bf16[4,128,4096]{2,1,0:T(8,128)(2,1)} %bitcast.23), custom_call_target="tpu_custom_call" | custom-call | bytes 4194304 | tf_op jit(solution)/shard_map/pallas_call | solution.py:66
  3.1 1.6 collective-permute-start
  4.7 2.1 %collective-permute-start.2 = (bf16[2,128,2048]{2,1,0:T(8,128)(2,1)}, bf16[2,128,2048]{2,1,0:T(8,128)(2,1)S(1)}, u32[]{:S(2)}, u32[]{:S(2)}) collective-permute-start(bf16[2,128,2048]{2,1,0:T(8,128)(2,1)} %get-tuple-element.20.after_ref), channel_id=1, source_target_pairs={{0,192},{64,128},{128,64},{192,0},{1,193},{65,129},{129,65},{193,1... | collective-permute-start | bytes 3145736 | tf_op jit(solution)/shard_map/ppermute | solution.py:264
  6.8 0.7 copy.14
  7.5 2.8 %shard_map.80 = bf16[8,64,512]{2,1,0:T(8,128)(2,1)} custom-call(s32[1]{0:T(128)} %bitcast.x_ref.where_ref, s32[1]{0:T(128)} %bitcast.1.z_ref, bf16[2,128,2048]{2,1,0:T(8,128)(2,1)} %get-tuple-element.20.after_ref, bf16[8,512,512]{2,1,0:T(8,128)(2,1)} %bitcast.28, bf16[8,16,512]{2,1,0:T(8,128)(2,1)} %bitcast.31, bf16[8,16,512]{2,1,0:T(8,128)(2,1)} %bitcast.29, ...), custom_call_target="tpu_custom_call" | custom-call | bytes 1048576 | tf_op jit(solution)/shard_map/pallas_call | solution.py:92
  10.3 15.0 %all_to_all.20 = bf16[8,64,512]{2,1,0:T(8,128)(2,1)} all-to-all(bf16[8,64,512]{2,1,0:T(8,128)(2,1)} %shard_map.80), channel_id=1, replica_groups=mesh['x'=4,'z'=8,'y'=4,'core'=2] {'y','core'}, dimensions={0} | all-to-all | bytes 1048576 | tf_op jit(solution)/shard_map/all_to_all | solution.py:277
  25.3 3.1 %collective-permute-done.got_ref.refs_1_ = bf16[2,128,2048]{2,1,0:T(8,128)(2,1)S(1)} collective-permute-done((bf16[2,128,2048]{2,1,0:T(8,128)(2,1)}, bf16[2,128,2048]{2,1,0:T(8,128)(2,1)S(1)}, u32[]{:S(2)}, u32[]{:S(2)}) %collective-permute-start) | collective-permute-done | bytes 1048608 | tf_op jit(solution)/shard_map/ppermute | solution.py:264
  28.3 2.4 %collective-permute-done.2.got_ref.refs_4_ = bf16[2,128,2048]{2,1,0:T(8,128)(2,1)S(1)} collective-permute-done((bf16[2,128,2048]{2,1,0:T(8,128)(2,1)}, bf16[2,128,2048]{2,1,0:T(8,128)(2,1)S(1)}, u32[]{:S(2)}, u32[]{:S(2)}) %collective-permute-start.2) | collective-permute-done | bytes 1048608 | tf_op jit(solution)/shard_map/ppermute | solution.py:264
  30.7 7.7 %all-to-all-start.2 = ((bf16[8,64,512]{2,1,0:T(8,128)(2,1)}), bf16[8,64,512]{2,1,0:T(8,128)(2,1)S(1)}, u32[]{:S(2)}, u32[]{:S(2)}) async-start(bf16[8,64,512]{2,1,0:T(8,128)(2,1)} %all_to_all.20), calls=%async_computation.2 | async-start | bytes 1048576 | tf_op jit(solution)/shard_map/all_to_all | solution.py:277
  38.4 2.2 %copy-done = bf16[1,512,4096]{2,1,0:T(8,128)(2,1)S(1)} copy-done((bf16[1,512,4096]{2,1,0:T(8,128)(2,1)S(1)}, bf16[1,512,4096]{2,1,0:T(8,128)(2,1)}, u32[]{:S(2)}) %copy-start) | copy-done | bytes 4194328
  40.9 2.2 %collective-permute-start.1 = (bf16[128,2048]{1,0:T(8,128)(2,1)S(1)}, bf16[128,2048]{1,0:T(8,128)(2,1)S(1)}, u32[]{:S(2)}, u32[]{:S(2)}) collective-permute-start(bf16[128,2048]{1,0:T(8,128)(2,1)S(1)} %shard_map.77), channel_id=1, source_target_pairs={{0,192},{64,128},{128,64},{192,0},{1,193},{65,129},{129,65},{193,1... | collective-permute-start | bytes 1572872 | tf_op jit(solution)/shard_map/ppermute | solution.py:264
  43.5 10.6 %collective-permute-done.1.refs_2_ = bf16[128,2048]{1,0:T(8,128)(2,1)S(1)} collective-permute-done((bf16[128,2048]{1,0:T(8,128)(2,1)S(1)}, bf16[128,2048]{1,0:T(8,128)(2,1)S(1)}, u32[]{:S(2)}, u32[]{:S(2)}) %collective-permute-start.1) | collective-permute-done | bytes 524320 | tf_op jit(solution)/shard_map/ppermute | solution.py:264
  54.1 1.0 collective-permute-done.3.refs_5_
  55.1 2.0 %shard_map.79 = bf16[2,4,128,512]{3,2,1,0:T(8,128)(2,1)} custom-call(s32[1]{0:T(128)} %bitcast.x_ref.where_ref, bf16[4,128,4096]{2,1,0:T(8,128)(2,1)S(1)} %bitcast.26, bf16[2,128,2048]{2,1,0:T(8,128)(2,1)S(1)} %collective-permute-done.got_ref.refs_1_, bf16[128,2048]{1,0:T(8,128)(2,1)S(1)} %collective-permute-done.1.refs_2_, ...), custom_call_target="tpu_custom_call" | custom-call | flops 1048576 | bytes 29360128 | tf_op jit(solution)/shard_map/pallas_call | solution.py:142
  57.1 7.2 %all-to-all-start = ((bf16[8,128,512]{2,1,0:T(8,128)(2,1)}), bf16[8,128,512]{2,1,0:T(8,128)(2,1)S(1)}, u32[]{:S(2)}, u32[]{:S(2)}) async-start(bf16[8,128,512]{2,1,0:T(8,128)(2,1)} %bitcast.3), calls=%async_computation | async-start | bytes 2097152 | tf_op jit(solution)/shard_map/all_to_all | solution.py:277
  64.7 3.0 %collective-permute-start.5 = (bf16[8,32,512]{2,1,0:T(8,128)(2,1)S(1)}, bf16[8,32,512]{2,1,0:T(8,128)(2,1)S(1)}, u32[]{:S(2)}, u32[]{:S(2)}) collective-permute-start(bf16[8,32,512]{2,1,0:T(8,128)(2,1)S(1)} %slice.12.refs_0_.refs_4_), channel_id=1, source_target_pairs={{0,192},{64,0},{128,64},{192,128},{1,193},{65,1},{129,65},{193,129... | collective-permute-start | bytes 786440 | tf_op jit(solution)/shard_map/ppermute | solution.py:260
  67.6 8.6 %collective-permute-done.4.refs_1_.refs_5_ = bf16[8,32,512]{2,1,0:T(8,128)(2,1)S(1)} collective-permute-done((bf16[8,32,512]{2,1,0:T(8,128)(2,1)S(1)}, bf16[8,32,512]{2,1,0:T(8,128)(2,1)S(1)}, u32[]{:S(2)}, u32[]{:S(2)}) %collective-permute-start.4) | collective-permute-done | bytes 262176 | tf_op jit(solution)/shard_map/ppermute | solution.py:260
  76.2 9.7 %all-to-all-done.parts_ref = bf16[8,128,512]{2,1,0:T(8,128)(2,1)S(1)} async-done(((bf16[8,128,512]{2,1,0:T(8,128)(2,1)}), bf16[8,128,512]{2,1,0:T(8,128)(2,1)S(1)}, u32[]{:S(2)}, u32[]{:S(2)}) %all-to-all-start) | async-done | bytes 1048608 | tf_op jit(solution)/shard_map/all_to_all | solution.py:277
  85.9 0.5 shard_map.81
  86.4 0.6 collective-permute-start.7
  87.0 2.8 %collective-permute-start.8 = (bf16[144,512]{1,0:T(8,128)(2,1)S(1)}, bf16[144,512]{1,0:T(8,128)(2,1)S(1)}, u32[]{:S(2)}, u32[]{:S(2)}) collective-permute-start(bf16[144,512]{1,0:T(8,128)(2,1)S(1)} %get-tuple-element.23.refs_0_), channel_id=1, source_target_pairs={{0,192},{64,0},{128,64},{192,128},{1,193},{65,1},{129,65},{193,129... | collective-permute-start | bytes 442376 | tf_op jit(solution)/shard_map/ppermute | solution.py:260
  89.8 3.1 %collective-permute-done.7.refs_1_ = bf16[144,512]{1,0:T(8,128)(2,1)S(1)} collective-permute-done((bf16[144,512]{1,0:T(8,128)(2,1)S(1)}, bf16[144,512]{1,0:T(8,128)(2,1)S(1)}, u32[]{:S(2)}, u32[]{:S(2)}) %collective-permute-start.7) | collective-permute-done | bytes 147488 | tf_op jit(solution)/shard_map/ppermute | solution.py:260
  92.9 1.2 collective-permute-done.8.refs_2_
  94.0 2.4 %collective-permute-done.9.refs_3_ = bf16[144,512]{1,0:T(8,128)(2,1)S(1)} collective-permute-done((bf16[144,512]{1,0:T(8,128)(2,1)S(1)}, bf16[144,512]{1,0:T(8,128)(2,1)S(1)}, u32[]{:S(2)}, u32[]{:S(2)}) %collective-permute-start.9) | collective-permute-done | bytes 147488 | tf_op jit(solution)/shard_map/ppermute | solution.py:260
  96.4 1.2 shard_map.82
  97.6 1.5 collective-permute-start.10
  99.1 0.6 collective-permute-start.11
  99.7 2.7 %collective-permute-start.14 = (bf16[128,512]{1,0:T(8,128)(2,1)S(1)}, bf16[128,512]{1,0:T(8,128)(2,1)}, u32[]{:S(2)}, u32[]{:S(2)}) collective-permute-start(bf16[128,512]{1,0:T(8,128)(2,1)S(1)} %get-tuple-element.27), channel_id=1, source_target_pairs={{0,0},{1,8},{2,16},{3,24},{4,32},{5,40},{6,48},{7,56},{8,1},{9,9},... | collective-permute-start | bytes 393224 | tf_op jit(solution)/shard_map/ppermute | solution.py:269
  102.5 6.9 %collective-permute-done.14 = bf16[128,512]{1,0:T(8,128)(2,1)} collective-permute-done((bf16[128,512]{1,0:T(8,128)(2,1)S(1)}, bf16[128,512]{1,0:T(8,128)(2,1)}, u32[]{:S(2)}, u32[]{:S(2)}) %collective-permute-start.14) | collective-permute-done | bytes 131104 | tf_op jit(solution)/shard_map/ppermute | solution.py:269
  109.4 6.7 %collective-permute-start.15 = (bf16[256,512]{1,0:T(8,128)(2,1)S(1)}, bf16[256,512]{1,0:T(8,128)(2,1)S(1)}, u32[]{:S(2)}, u32[]{:S(2)}) collective-permute-start(bf16[256,512]{1,0:T(8,128)(2,1)S(1)} %collective-permute-done.10.refs_1_), channel_id=1, source_target_pairs={{0,8},{8,16},{16,24},{24,32},{32,40},{40,48},{48,56},{56,0},{1,9},... | collective-permute-start | bytes 786440 | tf_op jit(solution)/shard_map/ppermute | solution.py:260
  116.2 1.4 collective-permute-start.13
  117.5 2.5 %collective-permute-done.15.refs_5_ = bf16[256,512]{1,0:T(8,128)(2,1)S(1)} collective-permute-done((bf16[256,512]{1,0:T(8,128)(2,1)S(1)}, bf16[256,512]{1,0:T(8,128)(2,1)S(1)}, u32[]{:S(2)}, u32[]{:S(2)}) %collective-permute-start.15) | collective-permute-done | bytes 262176 | tf_op jit(solution)/shard_map/ppermute | solution.py:260
  120.0 3.7 %collective-permute-done.16.refs_6_ = bf16[256,512]{1,0:T(8,128)(2,1)S(1)} collective-permute-done((bf16[256,512]{1,0:T(8,128)(2,1)S(1)}, bf16[256,512]{1,0:T(8,128)(2,1)S(1)}, u32[]{:S(2)}, u32[]{:S(2)}) %collective-permute-start.16) | collective-permute-done | bytes 262176 | tf_op jit(solution)/shard_map/ppermute | solution.py:260
  123.7 1.3 collective-permute-start.18
  125.0 3.3 %collective-permute-start.19 = (bf16[256,512]{1,0:T(8,128)(2,1)S(1)}, bf16[256,512]{1,0:T(8,128)(2,1)S(1)}, u32[]{:S(2)}, u32[]{:S(2)}) collective-permute-start(bf16[256,512]{1,0:T(8,128)(2,1)S(1)} %collective-permute-done.15.refs_5_), channel_id=1, source_target_pairs={{0,8},{8,16},{16,24},{24,32},{32,40},{40,48},{48,56},{56,0},{1,9},... | collective-permute-start | bytes 786440 | tf_op jit(solution)/shard_map/ppermute | solution.py:260
  128.3 0.8 collective-permute-done.17.refs_7_
  129.1 2.2 %collective-permute-done.18.refs_8_ = bf16[256,512]{1,0:T(8,128)(2,1)S(1)} collective-permute-done((bf16[256,512]{1,0:T(8,128)(2,1)S(1)}, bf16[256,512]{1,0:T(8,128)(2,1)S(1)}, u32[]{:S(2)}, u32[]{:S(2)}) %collective-permute-start.18) | collective-permute-done | bytes 262176 | tf_op jit(solution)/shard_map/ppermute | solution.py:264
  131.3 8.3 %all-to-all-start.3 = ((bf16[8,16,512]{2,1,0:T(8,128)(2,1)}), bf16[8,16,512]{2,1,0:T(8,128)(2,1)}, u32[]{:S(2)}, u32[]{:S(2)}) async-start(bf16[8,16,512]{2,1,0:T(8,128)(2,1)} %bitcast.9), calls=%async_computation.3 | async-start | bytes 262144 | tf_op jit(solution)/shard_map/all_to_all | solution.py:277
  139.7 2.8 %collective-permute-start.23 = (bf16[128,512]{1,0:T(8,128)(2,1)S(1)}, bf16[128,512]{1,0:T(8,128)(2,1)S(1)}, u32[]{:S(2)}, u32[]{:S(2)}) collective-permute-start(bf16[128,512]{1,0:T(8,128)(2,1)S(1)} %slice.10), channel_id=1, source_target_pairs={{0,8},{8,16},{16,24},{24,32},{32,40},{40,48},{48,56},{56,0},{1,9},... | collective-permute-start | bytes 393224 | tf_op jit(solution)/shard_map/ppermute | solution.py:260
  142.6 1.3 collective-permute-start.22
  143.9 1.1 collective-permute-done.23.refs_13_
  145.2 3.6 %collective-permute-done.24.refs_14_ = bf16[128,512]{1,0:T(8,128)(2,1)} collective-permute-done((bf16[128,512]{1,0:T(8,128)(2,1)S(1)}, bf16[128,512]{1,0:T(8,128)(2,1)}, u32[]{:S(2)}, u32[]{:S(2)}) %collective-permute-start.24) | collective-permute-done | bytes 131104 | tf_op jit(solution)/shard_map/ppermute | solution.py:260
  148.8 1.2 collective-permute-start.26
  150.0 0.9 multiply_multiply_fusion
  150.9 2.0 %reshape_add_fusion = f32[8,16,1,512]{3,2,1,0:T(1,128)} fusion(f32[8,16,512]{2,1,0:T(8,128)S(1)} %multiply_multiply_fusion, f32[8,16,1,512]{3,2,1,0:T(1,128)} %param.7), kind=kLoop, calls=%fused_computation.6 | loop fusion | flops 131072 | bytes 786432 | tf_op jit(solution)/shard_map/add | solution.py:38
  152.9 1.7 %fusion.4 = bf16[8,16,1,512]{3,1,2,0:T(8,128)(2,1)} fusion(bf16[8,16,512]{2,1,0:T(8,128)(2,1)} %all-to-all-done.3, bf16[8,16,1,512]{3,1,2,0:T(8,128)(2,1)} %param.6), kind=kLoop, calls=%fused_computation.8 | loop fusion | flops 393216 | bytes 393216
  154.6 0.7 collective-permute-done.26.refs_16_
  155.3 3.3 %shard_map.83 = bf16[512,4096]{1,0:T(8,128)(2,1)} custom-call(s32[1]{0:T(128)} %bitcast.x_ref.where_ref, s32[1]{0:T(128)} %bitcast.1.z_ref, bf16[512,512]{1,0:T(8,128)(2,1)S(1)} %get-tuple-element.24.refs_0_, bf16[256,512]{1,0:T(8,128)(2,1)S(1)} %collective-permute-done.10.refs_1_, bf16[256,512]{1,0:T(8,128)(2,1)S(1)} %collective-permute-done.11.refs_2_, ...), custom_call_target="tpu_custom_call" | custom-call | bytes 8388608 | tf_op jit(solution)/shard_map/pallas_call | solution.py:248
  (34 shorter events, 1.6 us)
Async XLA Ops:
  0.6 6.2 %copy-start.2 = (f32[8,16,1,512]{3,2,1,0:T(1,128)S(1)}, f32[8,16,1,512]{3,2,1,0:T(1,128)}, u32[]{:S(2)}) copy-start(f32[8,16,1,512]{3,2,1,0:T(1,128)} %param.7) | copy-start | bytes 786436
  3.1 25.2 %collective-permute-start = (bf16[2,128,2048]{2,1,0:T(8,128)(2,1)}, bf16[2,128,2048]{2,1,0:T(8,128)(2,1)S(1)}, u32[]{:S(2)}, u32[]{:S(2)}) collective-permute-start(bf16[2,128,2048]{2,1,0:T(8,128)(2,1)} %get-tuple-element.19), channel_id=1, source_target_pairs={{0,64},{64,0},{128,192},{192,128},{1,65},{65,1},{129,193},{193,129... | collective-permute-start | bytes 3145736 | tf_op jit(solution)/shard_map/ppermute | solution.py:264
  4.7 26.0 %collective-permute-start.2 = (bf16[2,128,2048]{2,1,0:T(8,128)(2,1)}, bf16[2,128,2048]{2,1,0:T(8,128)(2,1)S(1)}, u32[]{:S(2)}, u32[]{:S(2)}) collective-permute-start(bf16[2,128,2048]{2,1,0:T(8,128)(2,1)} %get-tuple-element.20.after_ref), channel_id=1, source_target_pairs={{0,192},{64,128},{128,64},{192,0},{1,193},{65,129},{129,65},{193,1... | collective-permute-start | bytes 3145736 | tf_op jit(solution)/shard_map/ppermute | solution.py:264
  30.7 26.3 %all-to-all-start.2 = ((bf16[8,64,512]{2,1,0:T(8,128)(2,1)}), bf16[8,64,512]{2,1,0:T(8,128)(2,1)S(1)}, u32[]{:S(2)}, u32[]{:S(2)}) async-start(bf16[8,64,512]{2,1,0:T(8,128)(2,1)} %all_to_all.20), calls=%async_computation.2 | async-start | bytes 1048576 | tf_op jit(solution)/shard_map/all_to_all | solution.py:277
  38.4 2.2 %copy-start = (bf16[1,512,4096]{2,1,0:T(8,128)(2,1)S(1)}, bf16[1,512,4096]{2,1,0:T(8,128)(2,1)}, u32[]{:S(2)}) copy-start(bf16[1,512,4096]{2,1,0:T(8,128)(2,1)} %param.5) | copy-start | bytes 12582916
  40.9 14.2 %copy-start.1 = (bf16[1,512,4096]{2,1,0:T(8,128)(2,1)S(1)}, bf16[1,512,4096]{2,1,0:T(8,128)(2,1)}, u32[]{:S(2)}) copy-start(bf16[1,512,4096]{2,1,0:T(8,128)(2,1)} %param.5) | copy-start | bytes 12582916
  40.9 13.2 %collective-permute-start.1 = (bf16[128,2048]{1,0:T(8,128)(2,1)S(1)}, bf16[128,2048]{1,0:T(8,128)(2,1)S(1)}, u32[]{:S(2)}, u32[]{:S(2)}) collective-permute-start(bf16[128,2048]{1,0:T(8,128)(2,1)S(1)} %shard_map.77), channel_id=1, source_target_pairs={{0,192},{64,128},{128,64},{192,0},{1,193},{65,129},{129,65},{193,1... | collective-permute-start | bytes 1572872 | tf_op jit(solution)/shard_map/ppermute | solution.py:264
  43.4 11.7 %collective-permute-start.3 = (bf16[128,2048]{1,0:T(8,128)(2,1)S(1)}, bf16[128,2048]{1,0:T(8,128)(2,1)S(1)}, u32[]{:S(2)}, u32[]{:S(2)}) collective-permute-start(bf16[128,2048]{1,0:T(8,128)(2,1)S(1)} %shard_map.78), channel_id=1, source_target_pairs={{0,64},{64,0},{128,192},{192,128},{1,65},{65,1},{129,193},{193,129... | collective-permute-start | bytes 1572872 | tf_op jit(solution)/shard_map/ppermute | solution.py:264
  57.1 28.8 %all-to-all-start = ((bf16[8,128,512]{2,1,0:T(8,128)(2,1)}), bf16[8,128,512]{2,1,0:T(8,128)(2,1)S(1)}, u32[]{:S(2)}, u32[]{:S(2)}) async-start(bf16[8,128,512]{2,1,0:T(8,128)(2,1)} %bitcast.3), calls=%async_computation | async-start | bytes 2097152 | tf_op jit(solution)/shard_map/all_to_all | solution.py:277
  64.3 11.9 %collective-permute-start.4 = (bf16[8,32,512]{2,1,0:T(8,128)(2,1)S(1)}, bf16[8,32,512]{2,1,0:T(8,128)(2,1)S(1)}, u32[]{:S(2)}, u32[]{:S(2)}) collective-permute-start(bf16[8,32,512]{2,1,0:T(8,128)(2,1)S(1)} %slice.12.refs_0_.refs_4_), channel_id=1, source_target_pairs={{0,64},{64,128},{128,192},{192,0},{1,65},{65,129},{129,193},{193,1... | collective-permute-start | bytes 786440 | tf_op jit(solution)/shard_map/ppermute | solution.py:260
  64.7 11.6 %collective-permute-start.5 = (bf16[8,32,512]{2,1,0:T(8,128)(2,1)S(1)}, bf16[8,32,512]{2,1,0:T(8,128)(2,1)S(1)}, u32[]{:S(2)}, u32[]{:S(2)}) collective-permute-start(bf16[8,32,512]{2,1,0:T(8,128)(2,1)S(1)} %slice.12.refs_0_.refs_4_), channel_id=1, source_target_pairs={{0,192},{64,0},{128,64},{192,128},{1,193},{65,1},{129,65},{193,129... | collective-permute-start | bytes 786440 | tf_op jit(solution)/shard_map/ppermute | solution.py:260
  67.6 8.6 %collective-permute-start.6 = (bf16[8,32,512]{2,1,0:T(8,128)(2,1)S(1)}, bf16[8,32,512]{2,1,0:T(8,128)(2,1)S(1)}, u32[]{:S(2)}, u32[]{:S(2)}) collective-permute-start(bf16[8,32,512]{2,1,0:T(8,128)(2,1)S(1)} %slice.12.refs_0_.refs_4_), channel_id=1, source_target_pairs={{0,128},{64,192},{128,0},{192,64},{1,129},{65,193},{129,1},{193,65... | collective-permute-start | bytes 786440 | tf_op jit(solution)/shard_map/ppermute | solution.py:260
  86.4 6.4 %collective-permute-start.7 = (bf16[144,512]{1,0:T(8,128)(2,1)S(1)}, bf16[144,512]{1,0:T(8,128)(2,1)S(1)}, u32[]{:S(2)}, u32[]{:S(2)}) collective-permute-start(bf16[144,512]{1,0:T(8,128)(2,1)S(1)} %get-tuple-element.23.refs_0_), channel_id=1, source_target_pairs={{0,64},{64,128},{128,192},{192,0},{1,65},{65,129},{129,193},{193,1... | collective-permute-start | bytes 442376 | tf_op jit(solution)/shard_map/ppermute | solution.py:260
  87.0 7.0 %collective-permute-start.8 = (bf16[144,512]{1,0:T(8,128)(2,1)S(1)}, bf16[144,512]{1,0:T(8,128)(2,1)S(1)}, u32[]{:S(2)}, u32[]{:S(2)}) collective-permute-start(bf16[144,512]{1,0:T(8,128)(2,1)S(1)} %get-tuple-element.23.refs_0_), channel_id=1, source_target_pairs={{0,192},{64,0},{128,64},{192,128},{1,193},{65,1},{129,65},{193,129... | collective-permute-start | bytes 442376 | tf_op jit(solution)/shard_map/ppermute | solution.py:260
  89.8 6.6 %collective-permute-start.9 = (bf16[144,512]{1,0:T(8,128)(2,1)S(1)}, bf16[144,512]{1,0:T(8,128)(2,1)S(1)}, u32[]{:S(2)}, u32[]{:S(2)}) collective-permute-start(bf16[144,512]{1,0:T(8,128)(2,1)S(1)} %get-tuple-element.23.refs_0_), channel_id=1, source_target_pairs={{0,128},{64,192},{128,0},{192,64},{1,129},{65,193},{129,1},{193,65... | collective-permute-start | bytes 442376 | tf_op jit(solution)/shard_map/ppermute | solution.py:260
  97.6 11.8 %collective-permute-start.10 = (bf16[256,512]{1,0:T(8,128)(2,1)S(1)}, bf16[256,512]{1,0:T(8,128)(2,1)S(1)}, u32[]{:S(2)}, u32[]{:S(2)}) collective-permute-start(bf16[256,512]{1,0:T(8,128)(2,1)S(1)} %get-tuple-element.25), channel_id=1, source_target_pairs={{0,8},{8,16},{16,24},{24,32},{32,40},{40,48},{48,56},{56,0},{1,9},... | collective-permute-start | bytes 786440 | tf_op jit(solution)/shard_map/ppermute | solution.py:260
  99.1 17.0 %collective-permute-start.11 = (bf16[256,512]{1,0:T(8,128)(2,1)S(1)}, bf16[256,512]{1,0:T(8,128)(2,1)S(1)}, u32[]{:S(2)}, u32[]{:S(2)}) collective-permute-start(bf16[256,512]{1,0:T(8,128)(2,1)S(1)} %get-tuple-element.26), channel_id=1, source_target_pairs={{0,56},{8,0},{16,8},{24,16},{32,24},{40,32},{48,40},{56,48},{1,57}... | collective-permute-start | bytes 786440 | tf_op jit(solution)/shard_map/ppermute | solution.py:260
  99.7 9.7 %collective-permute-start.14 = (bf16[128,512]{1,0:T(8,128)(2,1)S(1)}, bf16[128,512]{1,0:T(8,128)(2,1)}, u32[]{:S(2)}, u32[]{:S(2)}) collective-permute-start(bf16[128,512]{1,0:T(8,128)(2,1)S(1)} %get-tuple-element.27), channel_id=1, source_target_pairs={{0,0},{1,8},{2,16},{3,24},{4,32},{5,40},{6,48},{7,56},{8,1},{9,9},... | collective-permute-start | bytes 393224 | tf_op jit(solution)/shard_map/ppermute | solution.py:269
  109.4 10.6 %collective-permute-start.15 = (bf16[256,512]{1,0:T(8,128)(2,1)S(1)}, bf16[256,512]{1,0:T(8,128)(2,1)S(1)}, u32[]{:S(2)}, u32[]{:S(2)}) collective-permute-start(bf16[256,512]{1,0:T(8,128)(2,1)S(1)} %collective-permute-done.10.refs_1_), channel_id=1, source_target_pairs={{0,8},{8,16},{16,24},{24,32},{32,40},{40,48},{48,56},{56,0},{1,9},... | collective-permute-start | bytes 786440 | tf_op jit(solution)/shard_map/ppermute | solution.py:260
  116.1 7.6 %collective-permute-start.16 = (bf16[256,512]{1,0:T(8,128)(2,1)S(1)}, bf16[256,512]{1,0:T(8,128)(2,1)S(1)}, u32[]{:S(2)}, u32[]{:S(2)}) collective-permute-start(bf16[256,512]{1,0:T(8,128)(2,1)S(1)} %collective-permute-done.11.refs_2_), channel_id=1, source_target_pairs={{0,56},{8,0},{16,8},{24,16},{32,24},{40,32},{48,40},{56,48},{1,57}... | collective-permute-start | bytes 786440 | tf_op jit(solution)/shard_map/ppermute | solution.py:260
  116.2 8.9 %collective-permute-start.12 = (bf16[256,512]{1,0:T(8,128)(2,1)S(1)}, bf16[256,512]{1,0:T(8,128)(2,1)S(1)}, u32[]{:S(2)}, u32[]{:S(2)}) collective-permute-start(bf16[256,512]{1,0:T(8,128)(2,1)S(1)} %collective-permute-done.10.refs_1_), channel_id=1, source_target_pairs={{0,64},{64,0},{128,192},{192,128},{1,65},{65,1},{129,193},{193,129... | collective-permute-start | bytes 786440 | tf_op jit(solution)/shard_map/ppermute | solution.py:264
  116.2 8.9 %collective-permute-start.13 = (bf16[256,512]{1,0:T(8,128)(2,1)S(1)}, bf16[256,512]{1,0:T(8,128)(2,1)S(1)}, u32[]{:S(2)}, u32[]{:S(2)}) collective-permute-start(bf16[256,512]{1,0:T(8,128)(2,1)S(1)} %collective-permute-done.11.refs_2_), channel_id=1, source_target_pairs={{0,192},{64,128},{128,64},{192,0},{1,193},{65,129},{129,65},{193,1... | collective-permute-start | bytes 786440 | tf_op jit(solution)/shard_map/ppermute | solution.py:264
  120.0 9.1 %collective-permute-start.17 = (bf16[256,512]{1,0:T(8,128)(2,1)S(1)}, bf16[256,512]{1,0:T(8,128)(2,1)S(1)}, u32[]{:S(2)}, u32[]{:S(2)}) collective-permute-start(bf16[256,512]{1,0:T(8,128)(2,1)S(1)} %collective-permute-done.15.refs_5_), channel_id=1, source_target_pairs={{0,64},{64,0},{128,192},{192,128},{1,65},{65,1},{129,193},{193,129... | collective-permute-start | bytes 786440 | tf_op jit(solution)/shard_map/ppermute | solution.py:264
  123.7 7.6 %collective-permute-start.18 = (bf16[256,512]{1,0:T(8,128)(2,1)S(1)}, bf16[256,512]{1,0:T(8,128)(2,1)S(1)}, u32[]{:S(2)}, u32[]{:S(2)}) collective-permute-start(bf16[256,512]{1,0:T(8,128)(2,1)S(1)} %collective-permute-done.16.refs_6_), channel_id=1, source_target_pairs={{0,192},{64,128},{128,64},{192,0},{1,193},{65,129},{129,65},{193,1... | collective-permute-start | bytes 786440 | tf_op jit(solution)/shard_map/ppermute | solution.py:264
  125.0 14.6 %collective-permute-start.19 = (bf16[256,512]{1,0:T(8,128)(2,1)S(1)}, bf16[256,512]{1,0:T(8,128)(2,1)S(1)}, u32[]{:S(2)}, u32[]{:S(2)}) collective-permute-start(bf16[256,512]{1,0:T(8,128)(2,1)S(1)} %collective-permute-done.15.refs_5_), channel_id=1, source_target_pairs={{0,8},{8,16},{16,24},{24,32},{32,40},{40,48},{48,56},{56,0},{1,9},... | collective-permute-start | bytes 786440 | tf_op jit(solution)/shard_map/ppermute | solution.py:260
  128.3 14.1 %collective-permute-start.20 = (bf16[256,512]{1,0:T(8,128)(2,1)S(1)}, bf16[256,512]{1,0:T(8,128)(2,1)S(1)}, u32[]{:S(2)}, u32[]{:S(2)}) collective-permute-start(bf16[256,512]{1,0:T(8,128)(2,1)S(1)} %collective-permute-done.16.refs_6_), channel_id=1, source_target_pairs={{0,56},{8,0},{16,8},{24,16},{32,24},{40,32},{48,40},{56,48},{1,57}... | collective-permute-start | bytes 786440 | tf_op jit(solution)/shard_map/ppermute | solution.py:260
  131.3 18.6 %all-to-all-start.3 = ((bf16[8,16,512]{2,1,0:T(8,128)(2,1)}), bf16[8,16,512]{2,1,0:T(8,128)(2,1)}, u32[]{:S(2)}, u32[]{:S(2)}) async-start(bf16[8,16,512]{2,1,0:T(8,128)(2,1)} %bitcast.9), calls=%async_computation.3 | async-start | bytes 262144 | tf_op jit(solution)/shard_map/all_to_all | solution.py:277
  139.7 5.3 %collective-permute-start.23 = (bf16[128,512]{1,0:T(8,128)(2,1)S(1)}, bf16[128,512]{1,0:T(8,128)(2,1)S(1)}, u32[]{:S(2)}, u32[]{:S(2)}) collective-permute-start(bf16[128,512]{1,0:T(8,128)(2,1)S(1)} %slice.10), channel_id=1, source_target_pairs={{0,8},{8,16},{16,24},{24,32},{32,40},{40,48},{48,56},{56,0},{1,9},... | collective-permute-start | bytes 393224 | tf_op jit(solution)/shard_map/ppermute | solution.py:260
  142.4 6.4 %collective-permute-start.24 = (bf16[128,512]{1,0:T(8,128)(2,1)S(1)}, bf16[128,512]{1,0:T(8,128)(2,1)}, u32[]{:S(2)}, u32[]{:S(2)}) collective-permute-start(bf16[128,512]{1,0:T(8,128)(2,1)S(1)} %slice.11), channel_id=1, source_target_pairs={{0,56},{8,0},{16,8},{24,16},{32,24},{40,32},{48,40},{56,48},{1,57}... | collective-permute-start | bytes 393224 | tf_op jit(solution)/shard_map/ppermute | solution.py:260
  142.5 12.1 %collective-permute-start.21 = (bf16[256,512]{1,0:T(8,128)(2,1)S(1)}, bf16[256,512]{1,0:T(8,128)(2,1)S(1)}, u32[]{:S(2)}, u32[]{:S(2)}) collective-permute-start(bf16[256,512]{1,0:T(8,128)(2,1)S(1)} %collective-permute-done.19.refs_9_), channel_id=1, source_target_pairs={{0,64},{64,0},{128,192},{192,128},{1,65},{65,1},{129,193},{193,129... | collective-permute-start | bytes 786440 | tf_op jit(solution)/shard_map/ppermute | solution.py:264
  142.6 12.0 %collective-permute-start.22 = (bf16[256,512]{1,0:T(8,128)(2,1)S(1)}, bf16[256,512]{1,0:T(8,128)(2,1)}, u32[]{:S(2)}, u32[]{:S(2)}) collective-permute-start(bf16[256,512]{1,0:T(8,128)(2,1)S(1)} %collective-permute-done.20.refs_10_), channel_id=1, source_target_pairs={{0,192},{64,128},{128,64},{192,0},{1,193},{65,129},{129,65},{193,1... | collective-permute-start | bytes 786440 | tf_op jit(solution)/shard_map/ppermute | solution.py:264
  144.9 9.7 %collective-permute-start.25 = (bf16[128,512]{1,0:T(8,128)(2,1)S(1)}, bf16[128,512]{1,0:T(8,128)(2,1)}, u32[]{:S(2)}, u32[]{:S(2)}) collective-permute-start(bf16[128,512]{1,0:T(8,128)(2,1)S(1)} %collective-permute-done.23.refs_13_), channel_id=1, source_target_pairs={{0,64},{64,0},{128,192},{192,128},{1,65},{65,1},{129,193},{193,129... | collective-permute-start | bytes 393224 | tf_op jit(solution)/shard_map/ppermute | solution.py:264
  148.8 6.5 %collective-permute-start.26 = (bf16[128,512]{1,0:T(8,128)(2,1)}, bf16[128,512]{1,0:T(8,128)(2,1)}, u32[]{:S(2)}, u32[]{:S(2)}) collective-permute-start(bf16[128,512]{1,0:T(8,128)(2,1)} %collective-permute-done.24.refs_14_), channel_id=1, source_target_pairs={{0,192},{64,128},{128,64},{192,0},{1,193},{65,129},{129,65},{193,1... | collective-permute-start | bytes 393224 | tf_op jit(solution)/shard_map/ppermute | solution.py:264

commit v2 on v1

--- a/solution.py
+++ b/solution.py
@@ -20,7 +20,6 @@
 QROWS = BS // NX
 DROWS = QROWS // NZ
 HROWS = BS // 2
-SHIFTS = (0, 1, 3, 2)
 SUMS = 16
 HALF = NZ * BS // 2
 VMEM = 40 * 1024 * 1024
@@ -74,30 +73,51 @@
     )(x, grads)
 
 
-def pack_kernel(x_ref, z_ref, after_ref, right_ref, *refs):
-    out_ref, hold_ref, sems = refs[-3:]
-    row = pl.multiple_of(x_ref[0] * QROWS + z_ref[0] * DROWS, DROWS)
-    parts = [right_ref.at[:, pl.ds(row, DROWS)], *refs[:-3]]
+def pack_kernel(z_ref, own_ref, after_ref, right_ref, *refs):
+    states, (out_ref, root_ref, hold_ref, hold_root_ref, sems) = refs[:-5], refs[-5:]
+    root = pltpu.make_async_copy(
+        right_ref.at[lax.rem(z_ref[0] + NZ - own_ref[0], NZ)], hold_root_ref, sems.at[0, NZ]
+    )
     loads = [
-        (part, hold_ref.at[:, pl.ds(k * DROWS, DROWS)]) for k, part in enumerate(parts)
+        pltpu.make_async_copy(ref, hold_ref.at[:, pl.ds(k * DROWS, DROWS)], sems.at[0, k])
+        for k, ref in enumerate(states)
     ]
-    staged(loads[:-1], [], sems)
-    staged(loads[-1:], [(hold_ref, out_ref)], sems)
-
-
-def pack(x, z, after, right, *states):
+    for copy in (*loads, root):
+        copy.start()
+    for copy in loads:
+        copy.wait()
+    stores = [
+        pltpu.make_async_copy(
+            hold_ref.at[i], out_ref.at[lax.rem(own_ref[0] + i, NZ)], sems.at[1, i]
+        )
+        for i in range(NZ)
+    ]
+    for copy in stores:
+        copy.start()
+    root.wait()
+    stores.append(pltpu.make_async_copy(hold_root_ref, root_ref, sems.at[1, NZ]))
+    stores[-1].start()
+    for copy in stores:
+        copy.wait()
+
+
+def pack(z, own, after, right, *states):
     anywhere = pl.BlockSpec(memory_space=pl.ANY)
     smem = pl.BlockSpec(memory_space=pltpu.SMEM)
-    shape = (NZ, (1 + len(states)) * DROWS, BS)
+    shape = (NZ, len(states) * DROWS, BS)
     return pl.pallas_call(
         pack_kernel,
         in_specs=[smem, smem] + [anywhere] * (2 + len(states)),
-        out_specs=anywhere,
-        out_shape=jax.ShapeDtypeStruct(shape, BF16),
-        scratch_shapes=[pltpu.VMEM(shape, BF16), pltpu.SemaphoreType.DMA((2, 4))],
+        out_specs=(anywhere, anywhere),
+        out_shape=(jax.ShapeDtypeStruct(shape, BF16), jax.ShapeDtypeStruct((BS, BS), BF16)),
+        scratch_shapes=[
+            pltpu.VMEM(shape, BF16),
+            pltpu.VMEM((BS, BS), BF16),
+            pltpu.SemaphoreType.DMA((2, NZ + 1)),
+        ],
         compiler_params=ALL_VMEM,
-        cost_estimate=cost(0, 1 << 20),
-    )(x, z, after, right, *states)
+        cost_estimate=cost(0, 2 << 20),
+    )(z, own, after, right, *states)
 
 
 def add_kernel(where_ref, src_ref, got_ref, out_ref):
@@ -122,53 +142,46 @@
     )(quarter, grads, got)
 
 
-def sum_kernel(where_ref, *refs):
-    out_ref = refs[-1]
+def sum_kernel(x_ref, own_ref, *refs):
+    out_ref, j = refs[-1], pl.program_id(0)
     for half in range(2):
         mine_ref, first_ref, second_ref = refs[3 * half : 3 * half + 3]
         total = mine_ref[0].astype(F32) + first_ref[0].astype(F32) + second_ref[...].astype(F32)
-        out_ref[half, 0] = total.astype(BF16)
-
-
-def sum_quarter(grads, firsts, seconds, quarter):
+        out_ref[lax.rem(own_ref[0] + half * (NZ // 2) + j, NZ)] = total.astype(BF16)
+
+
+def sum_quarter(grads, firsts, seconds, x, own):
     specs, args = [], []
     for half in range(2):
         specs += [
-            pl.BlockSpec((1, QROWS, BS), lambda j, where, half=half: (where[0], 0, 4 * half + j)),
-            pl.BlockSpec((1, QROWS, BS), lambda j, where: (0, 0, j)),
-            pl.BlockSpec((QROWS, BS), lambda j, where: (0, j)),
+            pl.BlockSpec((1, QROWS, BS), lambda j, x, own, half=half: (x[0], 0, 4 * half + j)),
+            pl.BlockSpec((1, QROWS, BS), lambda j, x, own: (0, 0, j)),
+            pl.BlockSpec((QROWS, BS), lambda j, x, own: (0, j)),
         ]
         args += [grads, firsts[half], seconds[half]]
-    total = pl.pallas_call(
+    return pl.pallas_call(
         sum_kernel,
         grid_spec=pltpu.PrefetchScalarGridSpec(
-            num_scalar_prefetch=1,
+            num_scalar_prefetch=2,
             grid=(NZ // 2,),
             in_specs=specs,
-            out_specs=pl.BlockSpec((2, 1, QROWS, BS), lambda j, where: (0, j, 0, 0)),
+            out_specs=pl.BlockSpec((NZ, QROWS, BS), lambda j, x, own: (0, 0, 0)),
         ),
-        out_shape=jax.ShapeDtypeStruct((2, NZ // 2, QROWS, BS), BF16),
-        compiler_params=PARAMS,
-        cost_estimate=cost(1 << 20, 28 << 20),
-    )(quarter, *args)
-    return total.reshape(NZ, QROWS, BS)
-
-
-def right_kernel(x_ref, parts_ref, pre_ref, *refs):
-    roots, (low_ref, prod_ref) = refs[:NX], refs[NX:]
+        out_shape=jax.ShapeDtypeStruct((NZ, QROWS, BS), BF16),
+        compiler_params=PARAMS,
+        cost_estimate=cost(1 << 20, 4 << 20),
+    )(x, own, *args)
+
+
+def right_kernel(parts_ref, pre_ref, root_ref, low_ref, prod_ref):
     g = parts_ref[0].astype(F32)
     for k in range(1, NZ):
         g += parts_ref[k].astype(F32)
-    low_ref[...] = g.astype(BF16)
-    prod = None
-    for by, root_ref in zip(SHIFTS, roots):
-        col = pl.multiple_of(lax.rem(x_ref[0] + NX - by, NX) * QROWS, QROWS)
-        right = root_ref[:, :DROWS].reshape(QROWS, BS)
-        term = jnp.dot(low_ref[:, pl.ds(col, QROWS)], right, preferred_element_type=F32)
-        prod = term if prod is None else prod + term
-    prod_ref[:QROWS] = prod.astype(BF16)
-    m = pre_ref[:, 2 * DROWS : 3 * DROWS].reshape(QROWS, BS)
-    v = pre_ref[:, 3 * DROWS :].reshape(QROWS, BS)
+    low = g.astype(BF16)
+    low_ref[...] = low
+    prod_ref[:QROWS] = jnp.dot(low, root_ref[...], preferred_element_type=F32).astype(BF16)
+    m = pre_ref[:, DROWS : 2 * DROWS].reshape(QROWS, BS)
+    v = pre_ref[:, 2 * DROWS :].reshape(QROWS, BS)
     moment, second = moments(g, m, v)
     step = moment / CORRECT_ONE / (jnp.sqrt(second / CORRECT_TWO) + ADAM_EPS)
     total = jnp.full((SUMS, BS), jnp.sum(step * step), F32)
@@ -177,18 +190,33 @@
     prod_ref[QROWS:] = jnp.where(first, high, total - high).astype(BF16)
 
 
-def right_stage(x, parts, pre, roots):
-    full = pl.BlockSpec(memory_space=pltpu.VMEM)
+def right_stage(parts, pre, root):
     return pl.pallas_call(
         right_kernel,
-        in_specs=[pl.BlockSpec(memory_space=pltpu.SMEM)] + [full] * (2 + NX),
         out_shape=(
             jax.ShapeDtypeStruct((QROWS, BS), BF16),
             jax.ShapeDtypeStruct((QROWS + SUMS, BS), BF16),
         ),
         compiler_params=PARAMS,
         cost_estimate=cost(1 << 26, 2 << 20),
-    )(x, parts, pre, *roots)
+    )(parts, pre, root)
+
+
+def order_kernel(own_ref, src_ref, out_ref):
+    for k in range(NZ):
+        out_ref[lax.rem(k + NZ - own_ref[0], NZ)] = src_ref[k]
+
+
+def in_order(own, parts):
+    full, smem = pl.BlockSpec(memory_space=pltpu.VMEM), pl.BlockSpec(memory_space=pltpu.SMEM)
+    return pl.pallas_call(
+        order_kernel,
+        in_specs=[smem, full],
+        out_specs=full,
+        out_shape=jax.ShapeDtypeStruct(parts.shape, BF16),
+        compiler_params=PARAMS,
+        cost_estimate=cost(0, 1 << 18),
+    )(own, parts)
 
 
 def left_kernel(x_ref, *refs):
@@ -196,7 +224,7 @@
     shampoo, adam_sq = None, None
     for prod_ref, root_ref in zip(prods, roots):
         term = lax.dot_general(
-            root_ref[:, DROWS:].reshape(QROWS, BS),
+            root_ref[...],
             prod_ref[:QROWS],
             (((0,), (0,)), ((), ())),
             preferred_element_type=F32,
@@ -226,14 +254,14 @@
     )(x, *prods, *roots)
 
 
-def place_kernel(spots, x_ref, z_ref, *refs):
+def place_kernel(spots, x_ref, z_ref, own_ref, *refs):
     srcs, out_ref, sems = refs[:-2], refs[-2], refs[-1]
     halves = {"up": x_ref[0] & 1, "down": x_ref[0] >> 1}
     copies = []
     for k, (src, ring, other, quarter, by) in enumerate(zip(srcs, *zip(*spots))):
         half = 0 if ring is None else (1 - halves[ring] if other else halves[ring])
         row = pl.multiple_of(half * HROWS + quarter * QROWS, QROWS)
-        col = pl.multiple_of(lax.rem(z_ref[0] + by, NZ) * BS, BS)
+        col = pl.multiple_of(lax.rem(z_ref[0] + NZ - own_ref[0] + by, NZ) * BS, BS)
         dst = out_ref.at[pl.ds(row, src.shape[0]), pl.ds(col, BS)]
         copies.append(pltpu.make_async_copy(src, dst, sems.at[k]))
         copies[-1].start()
@@ -241,19 +269,19 @@
         copy.wait()
 
 
-def place(x, z, pieces):
+def place(x, z, own, pieces):
     srcs, spots = [piece[0] for piece in pieces], [piece[1:] for piece in pieces]
     anywhere = pl.BlockSpec(memory_space=pl.ANY)
     smem = pl.BlockSpec(memory_space=pltpu.SMEM)
     return pl.pallas_call(
         functools.partial(place_kernel, spots),
-        in_specs=[smem, smem] + [pl.BlockSpec(memory_space=pltpu.VMEM)] * len(srcs),
+        in_specs=[smem] * 3 + [pl.BlockSpec(memory_space=pltpu.VMEM)] * len(srcs),
         out_specs=anywhere,
         out_shape=jax.ShapeDtypeStruct((BS, NZ * BS), BF16),
         scratch_shapes=[pltpu.SemaphoreType.DMA((len(pieces),))],
         compiler_params=PARAMS,
         cost_estimate=cost(0, 4 * sum(src.size for src in srcs)),
-    )(x, z, *srcs)
+    )(x, z, own, *srcs)
 
 
 def shift(value, axis, size, by):
@@ -264,13 +292,13 @@
     return lax.ppermute(value, "x", [(k, k ^ bits) for k in range(NX)])
 
 
-def swap_z_own(value):
-    pairs = [(i * NZ + j, j * NZ + i) for i in range(NZ) for j in range(NZ)]
+def mirror(value):
+    pairs = [(z * NZ + own, z * NZ + (z - own) % NZ) for z in range(NZ) for own in range(NZ)]
     return lax.ppermute(value, ("z", *OWN), pairs)
 
 
 def gather_x(value):
-    return [value] + [shift(value, "x", NX, by) for by in SHIFTS[1:]]
+    return [value] + [shift(value, "x", NX, by) for by in (1, 3, 2)]
 
 
 def exchange(value, axis):
@@ -282,7 +310,7 @@
 
 
 def on_device(grads, momentum, second, left_roots, right_roots):
-    x, z = lax.axis_index("x").reshape(1), lax.axis_index("z").reshape(1)
+    x, z, own = (lax.axis_index(name).reshape(1) for name in ("x", "z", OWN))
     quarters = grads[0].reshape(NX, QROWS, grads.shape[2])
 
     steps = (1, 3)
@@ -290,22 +318,24 @@
     firsts = [partner(sends[h], steps[h]) for h in range(2)]
 
     low_second = after(second, sends[1])[:, :, 0].astype(BF16)
-    pre = pack(
-        x, z, sends[1], right_roots[:, 0], left_roots[:, 0], momentum[:, :, 0], low_second
+    pre, root = pack(
+        z, own, sends[1], right_roots[:, 0], left_roots[:, 0], momentum[:, :, 0], low_second
     )
-    pre = exchange(after(exchange(pre, OWN), *firsts), "z")
-    roots = gather_x(pre[:, : 2 * DROWS])
+    pre = exchange(pre, "z")
+    firsts = [after(first, pre) for first in firsts]
+    pre, root = mirror(pre), mirror(root)
+    roots = gather_x(pre[:, :DROWS].reshape(QROWS, BS))
 
     seconds = [
         partner(add_quarter(quarters, firsts[h], x ^ steps[1 - h], h), steps[1 - h])
         for h in range(2)
     ]
-    over_z = exchange(sum_quarter(quarters, firsts, seconds, x), "z")
-    g_low, prod = right_stage(x, over_z, pre, roots)
+    over_z = exchange(sum_quarter(quarters, firsts, seconds, x, own), "z")
+    g_low, prod = right_stage(over_z, pre, after(root, *roots))
     block, up, down = left_stage(x, gather_x(prod), roots)
 
     pieces = [(block, None, False, 0, 0)]
-    g_state = swap_z_own(g_low)
+    g_state = mirror(g_low)
     waits, last = (), (g_state,)
     for step in range(1, NZ // 2):
         up, down = (after(half, *waits) for half in (up, down))
@@ -327,9 +357,10 @@
         (partner(down, 3), "down", True, 1, NZ // 2),
     ]
 
-    g = exchange(after(g_state, *waits).reshape(NZ, DROWS, BS), "z").astype(F32)[:, :, None]
+    g = exchange(after(g_state, *waits).reshape(NZ, DROWS, BS), "z")
+    g = in_order(own, g).astype(F32)[:, :, None]
     new_moment, new_second = moments(g, momentum, second)
-    return place(x, z, pieces), new_moment.astype(BF16), new_second
+    return place(x, z, own, pieces), new_moment.astype(BF16), new_second
 
 
 def solution(mesh):

time: 159 us -> 149 us (0.937)
  blocking collectives: 15 us -> 0 us
  waiting for transfers between devices: 63.5 us -> 67.4 us
  starting transfers between devices: 59 us -> 62 us
  other arithmetic: 4.62 us -> 1.73 us
    all_to_all x1 -> x0, blocking collectives: 15 us -> none  [exchange(): return lax.all_to_all(value, axis, split_axis=0, concat_axis=0, tiled=True)]
    ppermute x1 -> x3, waiting for transfers between devices: 6.93 us -> 19.9 us  [mirror(): return lax.ppermute(value, ('z', *OWN), pairs)]
    ppermute x14, waiting for transfers between devices: 26.1 us -> 17.2 us  [shift(): lax.ppermute(value, axis, [(k, (k + by) % size) for k in range(size)])]
    ppermute x1 -> x3, starting transfers between devices: 2.74 us -> 7.46 us  [mirror(): return lax.ppermute(value, ('z', *OWN), pairs)]
    unnamed x1 -> x0, other arithmetic: 1.67 us -> none
    all_to_all x3, starting transfers between devices: 23.2 us -> 21.5 us  [exchange(): return lax.all_to_all(value, axis, split_axis=0, concat_axis=0, tiled=True)]
    pallas_call x2 -> x3, Pallas kernels: 3.8 us -> 3.81 us  [the longest x1 3.29 us: place(): pl.pallas_call(functools.partial(place_kernel, spots), in_specs=[smem] *...]
  transfers between devices with their start and end apart: 30 -> 32, of which waited for: 17 -> 14; matrix products, arithmetic and copies ran while one was open for 3% -> 2% of each run, Pallas kernels for 3% -> 2%
where the time goes in v2:
time: 149 us; the launch traced here: 148 us
  waiting for transfers between devices  67.4 us (45%)
  starting transfers between devices  62 us (42%)
  Pallas kernels  11.9 us (8%)
  local copies, waits for them, and re-layouts  3.88 us (3%)
  other arithmetic  1.73 us (1%)
    all_to_all x3, starting transfers between devices, exchange(): return lax.all_to_all(value, axis, split_axis=0, concat_axis=0, tiled=True)  21.5 us
    ppermute x14, starting transfers between devices, shift(): lax.ppermute(value, axis, [(k, (k + by) % size) for k in range(size)])  20.4 us
    ppermute x3, waiting for transfers between devices, mirror(): return lax.ppermute(value, ('z', *OWN), pairs)  19.9 us
    ppermute x12, waiting for transfers between devices, partner(): return lax.ppermute(value, 'x', [(k, k ^ bits) for k in range(NX)])  19.8 us
    ppermute x14, waiting for transfers between devices, shift(): lax.ppermute(value, axis, [(k, (k + by) % size) for k in range(size)])  17.2 us
    ppermute x12, starting transfers between devices, partner(): return lax.ppermute(value, 'x', [(k, k ^ bits) for k in range(NX)])  12.6 us
    all_to_all x3, waiting for transfers between devices, exchange(): return lax.all_to_all(value, axis, split_axis=0, concat_axis=0, tiled=True)  10.5 us
    ppermute x3, starting transfers between devices, mirror(): return lax.ppermute(value, ('z', *OWN), pairs)  7.46 us
  transfers between devices with their start and end apart: 32, of which 14 were waited for; matrix products, arithmetic and copies ran while one was open for 2% of the time, Pallas kernels for 2%

profile of v2, /device:TPU:96, one launch (start us, length us, event | category | flops | bytes accessed | tf_op | source)
XLA Modules:
  0.0 147.9 jit_solution(7998673349989650530)
XLA Ops:
  0.6 2.5 %shard_map.76 = (bf16[2,128,2048]{2,1,0:T(8,128)(2,1)}, bf16[2,128,2048]{2,1,0:T(8,128)(2,1)}) custom-call(s32[1]{0:T(128)} %bitcast.x_ref, bf16[4,128,4096]{2,1,0:T(8,128)(2,1)} %bitcast.28), custom_call_target="tpu_custom_call" | custom-call | bytes 4194304 | tf_op jit(solution)/shard_map/pallas_call | solution.py:65
  3.1 1.6 %collective-permute-start = (bf16[2,128,2048]{2,1,0:T(8,128)(2,1)}, bf16[2,128,2048]{2,1,0:T(8,128)(2,1)S(1)}, u32[]{:S(2)}, u32[]{:S(2)}) collective-permute-start(bf16[2,128,2048]{2,1,0:T(8,128)(2,1)} %get-tuple-element.23), channel_id=1, source_target_pairs={{0,64},{64,0},{128,192},{192,128},{1,65},{65,1},{129,193},{193,129... | collective-permute-start | bytes 3145736 | tf_op jit(solution)/shard_map/ppermute | solution.py:292
  4.7 2.1 %collective-permute-start.2 = (bf16[2,128,2048]{2,1,0:T(8,128)(2,1)}, bf16[2,128,2048]{2,1,0:T(8,128)(2,1)S(1)}, u32[]{:S(2)}, u32[]{:S(2)}) collective-permute-start(bf16[2,128,2048]{2,1,0:T(8,128)(2,1)} %get-tuple-element.24.after_ref), channel_id=1, source_target_pairs={{0,192},{64,128},{128,64},{192,0},{1,193},{65,129},{129,65},{193,1... | collective-permute-start | bytes 3145736 | tf_op jit(solution)/shard_map/ppermute | solution.py:292
  6.8 0.7 copy.19
  7.5 2.2 %shard_map.77 = (bf16[8,48,512]{2,1,0:T(8,128)(2,1)}, bf16[512,512]{1,0:T(8,128)(2,1)}) custom-call(s32[1]{0:T(128)} %bitcast.1.z_ref, s32[1]{0:T(128)} %bitcast.2.own_ref, bf16[2,128,2048]{2,1,0:T(8,128)(2,1)} %get-tuple-element.24.after_ref, bf16[8,512,512]{2,1,0:T(8,128)(2,1)} %bitcast.37, bf16[8,16,512]{2,1,0:T(8,128)(2,1)} %bitcast.40, ...), custom_call_target="tpu_custom_call" | custom-call | bytes 2097152 | tf_op jit(solution)/shard_map/pallas_call | solution.py:108
  9.7 7.7 %all-to-all-start = ((bf16[8,48,512]{2,1,0:T(8,128)(2,1)}), bf16[8,48,512]{2,1,0:T(8,128)(2,1)S(1)}, u32[]{:S(2)}, u32[]{:S(2)}) async-start(bf16[8,48,512]{2,1,0:T(8,128)(2,1)} %get-tuple-element.26), calls=%async_computation | async-start | bytes 786432 | tf_op jit(solution)/shard_map/all_to_all | solution.py:305
  17.4 10.4 %all-to-all-done = bf16[8,48,512]{2,1,0:T(8,128)(2,1)S(1)} async-done(((bf16[8,48,512]{2,1,0:T(8,128)(2,1)}), bf16[8,48,512]{2,1,0:T(8,128)(2,1)S(1)}, u32[]{:S(2)}, u32[]{:S(2)}) %all-to-all-start) | async-done | bytes 393248 | tf_op jit(solution)/shard_map/all_to_all | solution.py:305
  27.8 0.5 collective-permute-done.got_ref.refs_1_
  28.3 2.2 %copy-done = bf16[1,512,4096]{2,1,0:T(8,128)(2,1)S(1)} copy-done((bf16[1,512,4096]{2,1,0:T(8,128)(2,1)S(1)}, bf16[1,512,4096]{2,1,0:T(8,128)(2,1)}, u32[]{:S(2)}) %copy-start) | copy-done | bytes 4194328
  30.8 2.8 %collective-permute-start.1 = (bf16[128,2048]{1,0:T(8,128)(2,1)S(1)}, bf16[128,2048]{1,0:T(8,128)(2,1)S(1)}, u32[]{:S(2)}, u32[]{:S(2)}) collective-permute-start(bf16[128,2048]{1,0:T(8,128)(2,1)S(1)} %shard_map.78), channel_id=1, source_target_pairs={{0,192},{64,128},{128,64},{192,0},{1,193},{65,129},{129,65},{193,1... | collective-permute-start | bytes 1572872 | tf_op jit(solution)/shard_map/ppermute | solution.py:292
  34.0 0.3 collective-permute-start.3
  34.3 10.6 %collective-permute-done.1.refs_2_ = bf16[128,2048]{1,0:T(8,128)(2,1)S(1)} collective-permute-done((bf16[128,2048]{1,0:T(8,128)(2,1)S(1)}, bf16[128,2048]{1,0:T(8,128)(2,1)S(1)}, u32[]{:S(2)}, u32[]{:S(2)}) %collective-permute-start.1) | collective-permute-done | bytes 524320 | tf_op jit(solution)/shard_map/ppermute | solution.py:292
  44.9 1.7 %collective-permute-done.3.refs_5_ = bf16[128,2048]{1,0:T(8,128)(2,1)S(1)} collective-permute-done((bf16[128,2048]{1,0:T(8,128)(2,1)S(1)}, bf16[128,2048]{1,0:T(8,128)(2,1)S(1)}, u32[]{:S(2)}, u32[]{:S(2)}) %collective-permute-start.3) | collective-permute-done | bytes 524320 | tf_op jit(solution)/shard_map/ppermute | solution.py:292
  46.6 1.7 %shard_map.80 = bf16[8,128,512]{2,1,0:T(8,128)(2,1)} custom-call(s32[1]{0:T(128)} %bitcast.x_ref, s32[1]{0:T(128)} %bitcast.2.own_ref, bf16[4,128,4096]{2,1,0:T(8,128)(2,1)S(1)} %bitcast.31, bf16[2,128,2048]{2,1,0:T(8,128)(2,1)S(1)} %collective-permute-done.got_ref.refs_1_, bf16[128,2048]{1,0:T(8,128)(2,1)S(1)} %collective-permute-done.1.refs_2_, ...), custom_call_target="tpu_custom_call" | custom-call | flops 1048576 | bytes 4194304 | tf_op jit(solution)/shard_map/pallas_call | solution.py:162
  48.3 7.7 %all-to-all-start.1 = ((bf16[8,128,512]{2,1,0:T(8,128)(2,1)}), bf16[8,128,512]{2,1,0:T(8,128)(2,1)S(1)}, u32[]{:S(2)}, u32[]{:S(2)}) async-start(bf16[8,128,512]{2,1,0:T(8,128)(2,1)} %shard_map.80), calls=%async_computation.1 | async-start | bytes 2097152 | tf_op jit(solution)/shard_map/all_to_all | solution.py:305
  56.0 1.9 %collective-permute-start.4 = (bf16[8,48,512]{2,1,0:T(8,128)(2,1)S(1)}, bf16[8,48,512]{2,1,0:T(8,128)(2,1)S(1)}, u32[]{:S(2)}, u32[]{:S(2)}) collective-permute-start(bf16[8,48,512]{2,1,0:T(8,128)(2,1)S(1)} %all-to-all-done), channel_id=1, source_target_pairs={{0,0},{1,7},{2,6},{3,5},{4,4},{5,3},{6,2},{7,1},{8,9},{9,8},{10,15... | collective-permute-start | bytes 1179656 | tf_op jit(solution)/shard_map/ppermute | solution.py:297
  57.9 3.6 %collective-permute-start.5 = (bf16[512,512]{1,0:T(8,128)(2,1)S(1)}, bf16[512,512]{1,0:T(8,128)(2,1)S(1)}, u32[]{:S(2)}, u32[]{:S(2)}) collective-permute-start(bf16[512,512]{1,0:T(8,128)(2,1)S(1)} %copy-done.3), channel_id=1, source_target_pairs={{0,0},{1,7},{2,6},{3,5},{4,4},{5,3},{6,2},{7,1},{8,9},{9,8},{10,15... | collective-permute-start | bytes 1572872 | tf_op jit(solution)/shard_map/ppermute | solution.py:297
  61.5 7.6 %collective-permute-done.4.pre_ref = bf16[8,48,512]{2,1,0:T(8,128)(2,1)S(1)} collective-permute-done((bf16[8,48,512]{2,1,0:T(8,128)(2,1)S(1)}, bf16[8,48,512]{2,1,0:T(8,128)(2,1)S(1)}, u32[]{:S(2)}, u32[]{:S(2)}) %collective-permute-start.4) | collective-permute-done | bytes 393248 | tf_op jit(solution)/shard_map/ppermute | solution.py:297
  69.1 0.4 collective-permute-start.6
  69.5 3.0 %collective-permute-start.7 = (bf16[128,512]{1,0:T(8,128)(2,1)S(1)}, bf16[128,512]{1,0:T(8,128)(2,1)S(1)}, u32[]{:S(2)}, u32[]{:S(2)}) collective-permute-start(bf16[128,512]{1,0:T(8,128)(2,1)S(1)} %bitcast.34), channel_id=1, source_target_pairs={{0,192},{64,0},{128,64},{192,128},{1,193},{65,1},{129,65},{193,129... | collective-permute-start | bytes 393224 | tf_op jit(solution)/shard_map/ppermute | solution.py:288
  72.4 7.9 %collective-permute-done.5.root_ref = bf16[512,512]{1,0:T(8,128)(2,1)S(1)} collective-permute-done((bf16[512,512]{1,0:T(8,128)(2,1)S(1)}, bf16[512,512]{1,0:T(8,128)(2,1)S(1)}, u32[]{:S(2)}, u32[]{:S(2)}) %collective-permute-start.5) | collective-permute-done | bytes 524320 | tf_op jit(solution)/shard_map/ppermute | solution.py:297
  80.4 0.5 shard_map.81
  80.9 0.4 collective-permute-start.9
  81.2 3.0 %collective-permute-start.10 = (bf16[144,512]{1,0:T(8,128)(2,1)S(1)}, bf16[144,512]{1,0:T(8,128)(2,1)S(1)}, u32[]{:S(2)}, u32[]{:S(2)}) collective-permute-start(bf16[144,512]{1,0:T(8,128)(2,1)S(1)} %get-tuple-element.31.refs_0_), channel_id=1, source_target_pairs={{0,192},{64,0},{128,64},{192,128},{1,193},{65,1},{129,65},{193,129... | collective-permute-start | bytes 442376 | tf_op jit(solution)/shard_map/ppermute | solution.py:288
  84.2 7.0 %collective-permute-done.9.refs_1_ = bf16[144,512]{1,0:T(8,128)(2,1)S(1)} collective-permute-done((bf16[144,512]{1,0:T(8,128)(2,1)S(1)}, bf16[144,512]{1,0:T(8,128)(2,1)S(1)}, u32[]{:S(2)}, u32[]{:S(2)}) %collective-permute-start.9) | collective-permute-done | bytes 147488 | tf_op jit(solution)/shard_map/ppermute | solution.py:288
  91.2 1.2 shard_map.82
  92.4 3.4 %collective-permute-start.12 = (bf16[256,512]{1,0:T(8,128)(2,1)S(1)}, bf16[256,512]{1,0:T(8,128)(2,1)S(1)}, u32[]{:S(2)}, u32[]{:S(2)}) collective-permute-start(bf16[256,512]{1,0:T(8,128)(2,1)S(1)} %get-tuple-element.33), channel_id=1, source_target_pairs={{0,8},{8,16},{16,24},{24,32},{32,40},{40,48},{48,56},{56,0},{1,9},... | collective-permute-start | bytes 786440 | tf_op jit(solution)/shard_map/ppermute | solution.py:288
  95.8 1.9 %collective-permute-start.16 = (bf16[128,512]{1,0:T(8,128)(2,1)S(1)}, bf16[128,512]{1,0:T(8,128)(2,1)}, u32[]{:S(2)}, u32[]{:S(2)}) collective-permute-start(bf16[128,512]{1,0:T(8,128)(2,1)S(1)} %get-tuple-element.35), channel_id=1, source_target_pairs={{0,0},{1,7},{2,6},{3,5},{4,4},{5,3},{6,2},{7,1},{8,9},{9,8},{10,15... | collective-permute-start | bytes 393224 | tf_op jit(solution)/shard_map/ppermute | solution.py:297
  97.7 4.5 %collective-permute-done.16 = bf16[128,512]{1,0:T(8,128)(2,1)} collective-permute-done((bf16[128,512]{1,0:T(8,128)(2,1)S(1)}, bf16[128,512]{1,0:T(8,128)(2,1)}, u32[]{:S(2)}, u32[]{:S(2)}) %collective-permute-start.16) | collective-permute-done | bytes 131104 | tf_op jit(solution)/shard_map/ppermute | solution.py:297
  102.2 5.3 %collective-permute-start.17 = (bf16[256,512]{1,0:T(8,128)(2,1)S(1)}, bf16[256,512]{1,0:T(8,128)(2,1)S(1)}, u32[]{:S(2)}, u32[]{:S(2)}) collective-permute-start(bf16[256,512]{1,0:T(8,128)(2,1)S(1)} %collective-permute-done.12.refs_1_), channel_id=1, source_target_pairs={{0,8},{8,16},{16,24},{24,32},{32,40},{40,48},{48,56},{56,0},{1,9},... | collective-permute-start | bytes 786440 | tf_op jit(solution)/shard_map/ppermute | solution.py:288
  107.5 1.4 collective-permute-start.15
  108.9 2.5 %collective-permute-done.17.refs_5_ = bf16[256,512]{1,0:T(8,128)(2,1)S(1)} collective-permute-done((bf16[256,512]{1,0:T(8,128)(2,1)S(1)}, bf16[256,512]{1,0:T(8,128)(2,1)S(1)}, u32[]{:S(2)}, u32[]{:S(2)}) %collective-permute-start.17) | collective-permute-done | bytes 262176 | tf_op jit(solution)/shard_map/ppermute | solution.py:288
  111.4 3.7 %collective-permute-done.18.refs_6_ = bf16[256,512]{1,0:T(8,128)(2,1)S(1)} collective-permute-done((bf16[256,512]{1,0:T(8,128)(2,1)S(1)}, bf16[256,512]{1,0:T(8,128)(2,1)S(1)}, u32[]{:S(2)}, u32[]{:S(2)}) %collective-permute-start.18) | collective-permute-done | bytes 262176 | tf_op jit(solution)/shard_map/ppermute | solution.py:288
  115.1 1.3 collective-permute-start.20
  116.4 2.2 %collective-permute-start.21 = (bf16[256,512]{1,0:T(8,128)(2,1)S(1)}, bf16[256,512]{1,0:T(8,128)(2,1)S(1)}, u32[]{:S(2)}, u32[]{:S(2)}) collective-permute-start(bf16[256,512]{1,0:T(8,128)(2,1)S(1)} %collective-permute-done.17.refs_5_), channel_id=1, source_target_pairs={{0,8},{8,16},{16,24},{24,32},{32,40},{40,48},{48,56},{56,0},{1,9},... | collective-permute-start | bytes 786440 | tf_op jit(solution)/shard_map/ppermute | solution.py:288
  118.6 4.1 %collective-permute-done.20.refs_8_ = bf16[256,512]{1,0:T(8,128)(2,1)S(1)} collective-permute-done((bf16[256,512]{1,0:T(8,128)(2,1)S(1)}, bf16[256,512]{1,0:T(8,128)(2,1)S(1)}, u32[]{:S(2)}, u32[]{:S(2)}) %collective-permute-start.20) | collective-permute-done | bytes 262176 | tf_op jit(solution)/shard_map/ppermute | solution.py:292
  122.7 6.2 %all-to-all-start.2 = ((bf16[8,16,512]{2,1,0:T(8,128)(2,1)}), bf16[8,16,512]{2,1,0:T(8,128)(2,1)S(1)}, u32[]{:S(2)}, u32[]{:S(2)}) async-start(bf16[8,16,512]{2,1,0:T(8,128)(2,1)} %bitcast.10), calls=%async_computation.2 | async-start | bytes 262144 | tf_op jit(solution)/shard_map/all_to_all | solution.py:305
  128.9 2.8 %collective-permute-start.25 = (bf16[128,512]{1,0:T(8,128)(2,1)S(1)}, bf16[128,512]{1,0:T(8,128)(2,1)}, u32[]{:S(2)}, u32[]{:S(2)}) collective-permute-start(bf16[128,512]{1,0:T(8,128)(2,1)S(1)} %slice.10), channel_id=1, source_target_pairs={{0,8},{8,16},{16,24},{24,32},{32,40},{40,48},{48,56},{56,0},{1,9},... | collective-permute-start | bytes 393224 | tf_op jit(solution)/shard_map/ppermute | solution.py:288
  131.7 0.5 collective-permute-start.23
  132.2 1.3 collective-permute-start.24
  133.5 0.6 collective-permute-done.25.refs_13_
  134.1 0.4 collective-permute-start.27
  134.6 3.4 %collective-permute-done.26.refs_14_ = bf16[128,512]{1,0:T(8,128)(2,1)} collective-permute-done((bf16[128,512]{1,0:T(8,128)(2,1)S(1)}, bf16[128,512]{1,0:T(8,128)(2,1)}, u32[]{:S(2)}, u32[]{:S(2)}) %collective-permute-start.26) | collective-permute-done | bytes 131104 | tf_op jit(solution)/shard_map/ppermute | solution.py:288
  138.0 0.9 collective-permute-start.28
  138.9 1.7 %fusion.4 = (f32[8,16,1,512]{3,1,0,2:T(8,128)S(1)}, bf16[8,16,1,512]{3,1,2,0:T(8,128)(2,1)}) fusion(bf16[8,16,512]{2,1,0:T(8,128)(2,1)S(1)} %shard_map.84, f32[8,16,1,512]{3,2,1,0:T(1,128)} %param.7, bf16[8,16,1,512]{3,1,2,0:T(8,128)(2,1)} %param.6), kind=kLoop, calls=%fused_computation.6 | loop fusion | flops 655360 | bytes 917504 | tf_op jit(solution)/shard_map/add | solution.py:37
  140.7 1.0 copy.12
  141.6 2.8 %collective-permute-done.28.refs_16_ = bf16[128,512]{1,0:T(8,128)(2,1)} collective-permute-done((bf16[128,512]{1,0:T(8,128)(2,1)}, bf16[128,512]{1,0:T(8,128)(2,1)}, u32[]{:S(2)}, u32[]{:S(2)}) %collective-permute-start.28) | collective-permute-done | bytes 131104 | tf_op jit(solution)/shard_map/ppermute | solution.py:292
  144.5 3.3 %shard_map.83 = bf16[512,4096]{1,0:T(8,128)(2,1)} custom-call(s32[1]{0:T(128)} %bitcast.x_ref, s32[1]{0:T(128)} %bitcast.1.z_ref, s32[1]{0:T(128)} %bitcast.2.own_ref, bf16[512,512]{1,0:T(8,128)(2,1)S(1)} %get-tuple-element.32.refs_0_, bf16[256,512]{1,0:T(8,128)(2,1)S(1)} %collective-permute-done.12.refs_1_, ...), custom_call_target="tpu_custom_call" | custom-call | bytes 8388608 | tf_op jit(solution)/shard_map/pallas_call | solution.py:276
  (39 shorter events, 0.8 us)
Async XLA Ops:
  0.6 6.2 %copy-start.2 = (f32[8,16,1,512]{3,2,1,0:T(1,128)S(1)}, f32[8,16,1,512]{3,2,1,0:T(1,128)}, u32[]{:S(2)}) copy-start(f32[8,16,1,512]{3,2,1,0:T(1,128)} %param.7) | copy-start | bytes 786436
  3.1 25.2 %collective-permute-start = (bf16[2,128,2048]{2,1,0:T(8,128)(2,1)}, bf16[2,128,2048]{2,1,0:T(8,128)(2,1)S(1)}, u32[]{:S(2)}, u32[]{:S(2)}) collective-permute-start(bf16[2,128,2048]{2,1,0:T(8,128)(2,1)} %get-tuple-element.23), channel_id=1, source_target_pairs={{0,64},{64,0},{128,192},{192,128},{1,65},{65,1},{129,193},{193,129... | collective-permute-start | bytes 3145736 | tf_op jit(solution)/shard_map/ppermute | solution.py:292
  4.7 29.0 %collective-permute-start.2 = (bf16[2,128,2048]{2,1,0:T(8,128)(2,1)}, bf16[2,128,2048]{2,1,0:T(8,128)(2,1)S(1)}, u32[]{:S(2)}, u32[]{:S(2)}) collective-permute-start(bf16[2,128,2048]{2,1,0:T(8,128)(2,1)} %get-tuple-element.24.after_ref), channel_id=1, source_target_pairs={{0,192},{64,128},{128,64},{192,0},{1,193},{65,129},{129,65},{193,1... | collective-permute-start | bytes 3145736 | tf_op jit(solution)/shard_map/ppermute | solution.py:292
  9.7 18.1 %all-to-all-start = ((bf16[8,48,512]{2,1,0:T(8,128)(2,1)}), bf16[8,48,512]{2,1,0:T(8,128)(2,1)S(1)}, u32[]{:S(2)}, u32[]{:S(2)}) async-start(bf16[8,48,512]{2,1,0:T(8,128)(2,1)} %get-tuple-element.26), calls=%async_computation | async-start | bytes 786432 | tf_op jit(solution)/shard_map/all_to_all | solution.py:305
  28.3 2.2 %copy-start = (bf16[1,512,4096]{2,1,0:T(8,128)(2,1)S(1)}, bf16[1,512,4096]{2,1,0:T(8,128)(2,1)}, u32[]{:S(2)}) copy-start(bf16[1,512,4096]{2,1,0:T(8,128)(2,1)} %param.5) | copy-start | bytes 12582916
  30.8 15.8 %copy-start.1 = (bf16[1,512,4096]{2,1,0:T(8,128)(2,1)S(1)}, bf16[1,512,4096]{2,1,0:T(8,128)(2,1)}, u32[]{:S(2)}) copy-start(bf16[1,512,4096]{2,1,0:T(8,128)(2,1)} %param.5) | copy-start | bytes 12582916
  30.8 14.1 %collective-permute-start.1 = (bf16[128,2048]{1,0:T(8,128)(2,1)S(1)}, bf16[128,2048]{1,0:T(8,128)(2,1)S(1)}, u32[]{:S(2)}, u32[]{:S(2)}) collective-permute-start(bf16[128,2048]{1,0:T(8,128)(2,1)S(1)} %shard_map.78), channel_id=1, source_target_pairs={{0,192},{64,128},{128,64},{192,0},{1,193},{65,129},{129,65},{193,1... | collective-permute-start | bytes 1572872 | tf_op jit(solution)/shard_map/ppermute | solution.py:292
  34.0 23.9 %copy-start.3 = (bf16[512,512]{1,0:T(8,128)(2,1)S(1)}, bf16[512,512]{1,0:T(8,128)(2,1)}, u32[]{:S(2)}) copy-start(bf16[512,512]{1,0:T(8,128)(2,1)} %get-tuple-element.29) | copy-start | bytes 1572868
  34.0 12.6 %collective-permute-start.3 = (bf16[128,2048]{1,0:T(8,128)(2,1)S(1)}, bf16[128,2048]{1,0:T(8,128)(2,1)S(1)}, u32[]{:S(2)}, u32[]{:S(2)}) collective-permute-start(bf16[128,2048]{1,0:T(8,128)(2,1)S(1)} %shard_map.79), channel_id=1, source_target_pairs={{0,64},{64,0},{128,192},{192,128},{1,65},{65,1},{129,193},{193,129... | collective-permute-start | bytes 1572872 | tf_op jit(solution)/shard_map/ppermute | solution.py:292
  48.3 32.1 %all-to-all-start.1 = ((bf16[8,128,512]{2,1,0:T(8,128)(2,1)}), bf16[8,128,512]{2,1,0:T(8,128)(2,1)S(1)}, u32[]{:S(2)}, u32[]{:S(2)}) async-start(bf16[8,128,512]{2,1,0:T(8,128)(2,1)} %shard_map.80), calls=%async_computation.1 | async-start | bytes 2097152 | tf_op jit(solution)/shard_map/all_to_all | solution.py:305
  56.0 13.2 %collective-permute-start.4 = (bf16[8,48,512]{2,1,0:T(8,128)(2,1)S(1)}, bf16[8,48,512]{2,1,0:T(8,128)(2,1)S(1)}, u32[]{:S(2)}, u32[]{:S(2)}) collective-permute-start(bf16[8,48,512]{2,1,0:T(8,128)(2,1)S(1)} %all-to-all-done), channel_id=1, source_target_pairs={{0,0},{1,7},{2,6},{3,5},{4,4},{5,3},{6,2},{7,1},{8,9},{9,8},{10,15... | collective-permute-start | bytes 1179656 | tf_op jit(solution)/shard_map/ppermute | solution.py:297
  57.9 22.5 %collective-permute-start.5 = (bf16[512,512]{1,0:T(8,128)(2,1)S(1)}, bf16[512,512]{1,0:T(8,128)(2,1)S(1)}, u32[]{:S(2)}, u32[]{:S(2)}) collective-permute-start(bf16[512,512]{1,0:T(8,128)(2,1)S(1)} %copy-done.3), channel_id=1, source_target_pairs={{0,0},{1,7},{2,6},{3,5},{4,4},{5,3},{6,2},{7,1},{8,9},{9,8},{10,15... | collective-permute-start | bytes 1572872 | tf_op jit(solution)/shard_map/ppermute | solution.py:297
  69.1 11.2 %collective-permute-start.6 = (bf16[128,512]{1,0:T(8,128)(2,1)S(1)}, bf16[128,512]{1,0:T(8,128)(2,1)S(1)}, u32[]{:S(2)}, u32[]{:S(2)}) collective-permute-start(bf16[128,512]{1,0:T(8,128)(2,1)S(1)} %bitcast.33), channel_id=1, source_target_pairs={{0,64},{64,128},{128,192},{192,0},{1,65},{65,129},{129,193},{193,1... | collective-permute-start | bytes 393224 | tf_op jit(solution)/shard_map/ppermute | solution.py:288
  69.5 10.9 %collective-permute-start.7 = (bf16[128,512]{1,0:T(8,128)(2,1)S(1)}, bf16[128,512]{1,0:T(8,128)(2,1)S(1)}, u32[]{:S(2)}, u32[]{:S(2)}) collective-permute-start(bf16[128,512]{1,0:T(8,128)(2,1)S(1)} %bitcast.34), channel_id=1, source_target_pairs={{0,192},{64,0},{128,64},{192,128},{1,193},{65,1},{129,65},{193,129... | collective-permute-start | bytes 393224 | tf_op jit(solution)/shard_map/ppermute | solution.py:288
  72.4 7.9 %collective-permute-start.8 = (bf16[128,512]{1,0:T(8,128)(2,1)S(1)}, bf16[128,512]{1,0:T(8,128)(2,1)S(1)}, u32[]{:S(2)}, u32[]{:S(2)}) collective-permute-start(bf16[128,512]{1,0:T(8,128)(2,1)S(1)} %bitcast.35), channel_id=1, source_target_pairs={{0,128},{64,192},{128,0},{192,64},{1,129},{65,193},{129,1},{193,65... | collective-permute-start | bytes 393224 | tf_op jit(solution)/shard_map/ppermute | solution.py:288
  80.9 10.3 %collective-permute-start.9 = (bf16[144,512]{1,0:T(8,128)(2,1)S(1)}, bf16[144,512]{1,0:T(8,128)(2,1)S(1)}, u32[]{:S(2)}, u32[]{:S(2)}) collective-permute-start(bf16[144,512]{1,0:T(8,128)(2,1)S(1)} %get-tuple-element.31.refs_0_), channel_id=1, source_target_pairs={{0,64},{64,128},{128,192},{192,0},{1,65},{65,129},{129,193},{193,1... | collective-permute-start | bytes 442376 | tf_op jit(solution)/shard_map/ppermute | solution.py:288
  81.2 10.0 %collective-permute-start.10 = (bf16[144,512]{1,0:T(8,128)(2,1)S(1)}, bf16[144,512]{1,0:T(8,128)(2,1)S(1)}, u32[]{:S(2)}, u32[]{:S(2)}) collective-permute-start(bf16[144,512]{1,0:T(8,128)(2,1)S(1)} %get-tuple-element.31.refs_0_), channel_id=1, source_target_pairs={{0,192},{64,0},{128,64},{192,128},{1,193},{65,1},{129,65},{193,129... | collective-permute-start | bytes 442376 | tf_op jit(solution)/shard_map/ppermute | solution.py:288
  84.2 7.0 %collective-permute-start.11 = (bf16[144,512]{1,0:T(8,128)(2,1)S(1)}, bf16[144,512]{1,0:T(8,128)(2,1)S(1)}, u32[]{:S(2)}, u32[]{:S(2)}) collective-permute-start(bf16[144,512]{1,0:T(8,128)(2,1)S(1)} %get-tuple-element.31.refs_0_), channel_id=1, source_target_pairs={{0,128},{64,192},{128,0},{192,64},{1,129},{65,193},{129,1},{193,65... | collective-permute-start | bytes 442376 | tf_op jit(solution)/shard_map/ppermute | solution.py:288
  92.4 9.8 %collective-permute-start.12 = (bf16[256,512]{1,0:T(8,128)(2,1)S(1)}, bf16[256,512]{1,0:T(8,128)(2,1)S(1)}, u32[]{:S(2)}, u32[]{:S(2)}) collective-permute-start(bf16[256,512]{1,0:T(8,128)(2,1)S(1)} %get-tuple-element.33), channel_id=1, source_target_pairs={{0,8},{8,16},{16,24},{24,32},{32,40},{40,48},{48,56},{56,0},{1,9},... | collective-permute-start | bytes 786440 | tf_op jit(solution)/shard_map/ppermute | solution.py:288
  95.8 11.7 %collective-permute-start.13 = (bf16[256,512]{1,0:T(8,128)(2,1)S(1)}, bf16[256,512]{1,0:T(8,128)(2,1)S(1)}, u32[]{:S(2)}, u32[]{:S(2)}) collective-permute-start(bf16[256,512]{1,0:T(8,128)(2,1)S(1)} %get-tuple-element.34), channel_id=1, source_target_pairs={{0,56},{8,0},{16,8},{24,16},{32,24},{40,32},{48,40},{56,48},{1,57}... | collective-permute-start | bytes 786440 | tf_op jit(solution)/shard_map/ppermute | solution.py:288
  95.8 6.4 %collective-permute-start.16 = (bf16[128,512]{1,0:T(8,128)(2,1)S(1)}, bf16[128,512]{1,0:T(8,128)(2,1)}, u32[]{:S(2)}, u32[]{:S(2)}) collective-permute-start(bf16[128,512]{1,0:T(8,128)(2,1)S(1)} %get-tuple-element.35), channel_id=1, source_target_pairs={{0,0},{1,7},{2,6},{3,5},{4,4},{5,3},{6,2},{7,1},{8,9},{9,8},{10,15... | collective-permute-start | bytes 393224 | tf_op jit(solution)/shard_map/ppermute | solution.py:297
  102.2 9.2 %collective-permute-start.17 = (bf16[256,512]{1,0:T(8,128)(2,1)S(1)}, bf16[256,512]{1,0:T(8,128)(2,1)S(1)}, u32[]{:S(2)}, u32[]{:S(2)}) collective-permute-start(bf16[256,512]{1,0:T(8,128)(2,1)S(1)} %collective-permute-done.12.refs_1_), channel_id=1, source_target_pairs={{0,8},{8,16},{16,24},{24,32},{32,40},{40,48},{48,56},{56,0},{1,9},... | collective-permute-start | bytes 786440 | tf_op jit(solution)/shard_map/ppermute | solution.py:288
  107.5 7.6 %collective-permute-start.18 = (bf16[256,512]{1,0:T(8,128)(2,1)S(1)}, bf16[256,512]{1,0:T(8,128)(2,1)S(1)}, u32[]{:S(2)}, u32[]{:S(2)}) collective-permute-start(bf16[256,512]{1,0:T(8,128)(2,1)S(1)} %collective-permute-done.13.refs_2_), channel_id=1, source_target_pairs={{0,56},{8,0},{16,8},{24,16},{32,24},{40,32},{48,40},{56,48},{1,57}... | collective-permute-start | bytes 786440 | tf_op jit(solution)/shard_map/ppermute | solution.py:288
  107.5 8.9 %collective-permute-start.14 = (bf16[256,512]{1,0:T(8,128)(2,1)S(1)}, bf16[256,512]{1,0:T(8,128)(2,1)S(1)}, u32[]{:S(2)}, u32[]{:S(2)}) collective-permute-start(bf16[256,512]{1,0:T(8,128)(2,1)S(1)} %collective-permute-done.12.refs_1_), channel_id=1, source_target_pairs={{0,64},{64,0},{128,192},{192,128},{1,65},{65,1},{129,193},{193,129... | collective-permute-start | bytes 786440 | tf_op jit(solution)/shard_map/ppermute | solution.py:292
  107.5 8.9 %collective-permute-start.15 = (bf16[256,512]{1,0:T(8,128)(2,1)S(1)}, bf16[256,512]{1,0:T(8,128)(2,1)S(1)}, u32[]{:S(2)}, u32[]{:S(2)}) collective-permute-start(bf16[256,512]{1,0:T(8,128)(2,1)S(1)} %collective-permute-done.13.refs_2_), channel_id=1, source_target_pairs={{0,192},{64,128},{128,64},{192,0},{1,193},{65,129},{129,65},{193,1... | collective-permute-start | bytes 786440 | tf_op jit(solution)/shard_map/ppermute | solution.py:292
  111.4 7.2 %collective-permute-start.19 = (bf16[256,512]{1,0:T(8,128)(2,1)S(1)}, bf16[256,512]{1,0:T(8,128)(2,1)S(1)}, u32[]{:S(2)}, u32[]{:S(2)}) collective-permute-start(bf16[256,512]{1,0:T(8,128)(2,1)S(1)} %collective-permute-done.17.refs_5_), channel_id=1, source_target_pairs={{0,64},{64,0},{128,192},{192,128},{1,65},{65,1},{129,193},{193,129... | collective-permute-start | bytes 786440 | tf_op jit(solution)/shard_map/ppermute | solution.py:292
  115.1 7.6 %collective-permute-start.20 = (bf16[256,512]{1,0:T(8,128)(2,1)S(1)}, bf16[256,512]{1,0:T(8,128)(2,1)S(1)}, u32[]{:S(2)}, u32[]{:S(2)}) collective-permute-start(bf16[256,512]{1,0:T(8,128)(2,1)S(1)} %collective-permute-done.18.refs_6_), channel_id=1, source_target_pairs={{0,192},{64,128},{128,64},{192,0},{1,193},{65,129},{129,65},{193,1... | collective-permute-start | bytes 786440 | tf_op jit(solution)/shard_map/ppermute | solution.py:292
  116.4 12.5 %collective-permute-start.21 = (bf16[256,512]{1,0:T(8,128)(2,1)S(1)}, bf16[256,512]{1,0:T(8,128)(2,1)S(1)}, u32[]{:S(2)}, u32[]{:S(2)}) collective-permute-start(bf16[256,512]{1,0:T(8,128)(2,1)S(1)} %collective-permute-done.17.refs_5_), channel_id=1, source_target_pairs={{0,8},{8,16},{16,24},{24,32},{32,40},{40,48},{48,56},{56,0},{1,9},... | collective-permute-start | bytes 786440 | tf_op jit(solution)/shard_map/ppermute | solution.py:288
  118.6 13.1 %collective-permute-start.22 = (bf16[256,512]{1,0:T(8,128)(2,1)S(1)}, bf16[256,512]{1,0:T(8,128)(2,1)S(1)}, u32[]{:S(2)}, u32[]{:S(2)}) collective-permute-start(bf16[256,512]{1,0:T(8,128)(2,1)S(1)} %collective-permute-done.18.refs_6_), channel_id=1, source_target_pairs={{0,56},{8,0},{16,8},{24,16},{32,24},{40,32},{48,40},{56,48},{1,57}... | collective-permute-start | bytes 786440 | tf_op jit(solution)/shard_map/ppermute | solution.py:288
  122.7 16.2 %all-to-all-start.2 = ((bf16[8,16,512]{2,1,0:T(8,128)(2,1)}), bf16[8,16,512]{2,1,0:T(8,128)(2,1)S(1)}, u32[]{:S(2)}, u32[]{:S(2)}) async-start(bf16[8,16,512]{2,1,0:T(8,128)(2,1)} %bitcast.10), calls=%async_computation.2 | async-start | bytes 262144 | tf_op jit(solution)/shard_map/all_to_all | solution.py:305
  128.9 5.3 %collective-permute-start.25 = (bf16[128,512]{1,0:T(8,128)(2,1)S(1)}, bf16[128,512]{1,0:T(8,128)(2,1)}, u32[]{:S(2)}, u32[]{:S(2)}) collective-permute-start(bf16[128,512]{1,0:T(8,128)(2,1)S(1)} %slice.10), channel_id=1, source_target_pairs={{0,8},{8,16},{16,24},{24,32},{32,40},{40,48},{48,56},{56,0},{1,9},... | collective-permute-start | bytes 393224 | tf_op jit(solution)/shard_map/ppermute | solution.py:288
  131.6 6.4 %collective-permute-start.26 = (bf16[128,512]{1,0:T(8,128)(2,1)S(1)}, bf16[128,512]{1,0:T(8,128)(2,1)}, u32[]{:S(2)}, u32[]{:S(2)}) collective-permute-start(bf16[128,512]{1,0:T(8,128)(2,1)S(1)} %slice.11), channel_id=1, source_target_pairs={{0,56},{8,0},{16,8},{24,16},{32,24},{40,32},{48,40},{56,48},{1,57}... | collective-permute-start | bytes 393224 | tf_op jit(solution)/shard_map/ppermute | solution.py:288
  131.7 9.9 %collective-permute-start.23 = (bf16[256,512]{1,0:T(8,128)(2,1)S(1)}, bf16[256,512]{1,0:T(8,128)(2,1)S(1)}, u32[]{:S(2)}, u32[]{:S(2)}) collective-permute-start(bf16[256,512]{1,0:T(8,128)(2,1)S(1)} %collective-permute-done.21.refs_9_), channel_id=1, source_target_pairs={{0,64},{64,0},{128,192},{192,128},{1,65},{65,1},{129,193},{193,129... | collective-permute-start | bytes 786440 | tf_op jit(solution)/shard_map/ppermute | solution.py:292
  132.2 9.4 %collective-permute-start.24 = (bf16[256,512]{1,0:T(8,128)(2,1)S(1)}, bf16[256,512]{1,0:T(8,128)(2,1)}, u32[]{:S(2)}, u32[]{:S(2)}) collective-permute-start(bf16[256,512]{1,0:T(8,128)(2,1)S(1)} %collective-permute-done.22.refs_10_), channel_id=1, source_target_pairs={{0,192},{64,128},{128,64},{192,0},{1,193},{65,129},{129,65},{193,1... | collective-permute-start | bytes 786440 | tf_op jit(solution)/shard_map/ppermute | solution.py:292
  134.1 7.5 %collective-permute-start.27 = (bf16[128,512]{1,0:T(8,128)(2,1)}, bf16[128,512]{1,0:T(8,128)(2,1)}, u32[]{:S(2)}, u32[]{:S(2)}) collective-permute-start(bf16[128,512]{1,0:T(8,128)(2,1)} %collective-permute-done.25.refs_13_), channel_id=1, source_target_pairs={{0,64},{64,0},{128,192},{192,128},{1,65},{65,1},{129,193},{193,129... | collective-permute-start | bytes 393224 | tf_op jit(solution)/shard_map/ppermute | solution.py:292
  138.0 6.5 %collective-permute-start.28 = (bf16[128,512]{1,0:T(8,128)(2,1)}, bf16[128,512]{1,0:T(8,128)(2,1)}, u32[]{:S(2)}, u32[]{:S(2)}) collective-permute-start(bf16[128,512]{1,0:T(8,128)(2,1)} %collective-permute-done.26.refs_14_), channel_id=1, source_target_pairs={{0,192},{64,128},{128,64},{192,0},{1,193},{65,129},{129,65},{193,1... | collective-permute-start | bytes 393224 | tf_op jit(solution)/shard_map/ppermute | solution.py:292

commit v3 on v2

--- a/solution.py
+++ b/solution.py
@@ -73,73 +73,83 @@
     )(x, grads)
 
 
-def pack_kernel(z_ref, own_ref, after_ref, right_ref, *refs):
-    states, (out_ref, root_ref, hold_ref, hold_root_ref, sems) = refs[:-5], refs[-5:]
-    root = pltpu.make_async_copy(
-        right_ref.at[lax.rem(z_ref[0] + NZ - own_ref[0], NZ)], hold_root_ref, sems.at[0, NZ]
-    )
+def pack_kernel(x_ref, z_ref, own_ref, after_ref, grads_ref, right_ref, *refs):
+    states, (out_ref, root_ref, left_ref, rest_ref) = refs[:-8], refs[-8:-4]
+    hold_ref, hold_root_ref, hold_kept_ref, sems = refs[-4:]
     loads = [
         pltpu.make_async_copy(ref, hold_ref.at[:, pl.ds(k * DROWS, DROWS)], sems.at[0, k])
         for k, ref in enumerate(states)
     ]
-    for copy in (*loads, root):
-        copy.start()
-    for copy in loads:
-        copy.wait()
     stores = [
         pltpu.make_async_copy(
             hold_ref.at[i], out_ref.at[lax.rem(own_ref[0] + i, NZ)], sems.at[1, i]
         )
         for i in range(NZ)
     ]
+    root = right_ref.at[lax.rem(z_ref[0] + NZ - own_ref[0], NZ)]
+    others = [(root, hold_root_ref, root_ref)]
+    for half, bits, kept_ref in ((0, 3, left_ref), (1, 1, rest_ref)):
+        src = grads_ref.at[x_ref[0] ^ bits, :, pl.ds(half * HALF, HALF)]
+        others.append((src, hold_kept_ref.at[half], kept_ref))
+    more = [
+        (
+            pltpu.make_async_copy(src, hold, sems.at[0, NZ + k]),
+            pltpu.make_async_copy(hold, dst, sems.at[1, NZ + k]),
+        )
+        for k, (src, hold, dst) in enumerate(others)
+    ]
+    for copy in loads:
+        copy.start()
+    for load, _ in more:
+        load.start()
+    for copy in loads:
+        copy.wait()
     for copy in stores:
         copy.start()
-    root.wait()
-    stores.append(pltpu.make_async_copy(hold_root_ref, root_ref, sems.at[1, NZ]))
-    stores[-1].start()
+    for load, store in more:
+        load.wait()
+        store.start()
     for copy in stores:
         copy.wait()
-
-
-def pack(z, own, after, right, *states):
+    for _, store in more:
+        store.wait()
+
+
+def pack(x, z, own, after, grads, right, *states):
     anywhere = pl.BlockSpec(memory_space=pl.ANY)
     smem = pl.BlockSpec(memory_space=pltpu.SMEM)
-    shape = (NZ, len(states) * DROWS, BS)
+    shapes = [(NZ, len(states) * DROWS, BS), (BS, BS), (QROWS, HALF), (QROWS, HALF)]
     return pl.pallas_call(
         pack_kernel,
-        in_specs=[smem, smem] + [anywhere] * (2 + len(states)),
-        out_specs=(anywhere, anywhere),
-        out_shape=(jax.ShapeDtypeStruct(shape, BF16), jax.ShapeDtypeStruct((BS, BS), BF16)),
+        in_specs=[smem] * 3 + [anywhere] * (3 + len(states)),
+        out_specs=(anywhere,) * 4,
+        out_shape=tuple(jax.ShapeDtypeStruct(shape, BF16) for shape in shapes),
         scratch_shapes=[
-            pltpu.VMEM(shape, BF16),
-            pltpu.VMEM((BS, BS), BF16),
-            pltpu.SemaphoreType.DMA((2, NZ + 1)),
+            pltpu.VMEM(shapes[0], BF16),
+            pltpu.VMEM(shapes[1], BF16),
+            pltpu.VMEM((2, QROWS, HALF), BF16),
+            pltpu.SemaphoreType.DMA((2, NZ + 3)),
         ],
         compiler_params=ALL_VMEM,
-        cost_estimate=cost(0, 2 << 20),
-    )(z, own, after, right, *states)
-
-
-def add_kernel(where_ref, src_ref, got_ref, out_ref):
-    out_ref[...] = (src_ref[0].astype(F32) + got_ref[0].astype(F32)).astype(BF16)
-
-
-def add_quarter(grads, got, quarter, half):
+        cost_estimate=cost(0, 4 << 20),
+    )(x, z, own, after, grads, right, *states)
+
+
+def add_kernel(kept_ref, got_ref, out_ref):
+    out_ref[...] = (kept_ref[...].astype(F32) + got_ref[0].astype(F32)).astype(BF16)
+
+
+def add_quarter(kept, got):
+    spec = pl.BlockSpec((QROWS, HALF // 2), lambda c: (0, c))
     return pl.pallas_call(
         add_kernel,
-        grid_spec=pltpu.PrefetchScalarGridSpec(
-            num_scalar_prefetch=1,
-            grid=(2,),
-            in_specs=[
-                pl.BlockSpec((1, QROWS, HALF // 2), lambda c, where: (where[0], 0, 2 * half + c)),
-                pl.BlockSpec((1, QROWS, HALF // 2), lambda c, where: (1, 0, c)),
-            ],
-            out_specs=pl.BlockSpec((QROWS, HALF // 2), lambda c, where: (0, c)),
-        ),
+        grid=(2,),
+        in_specs=[spec, pl.BlockSpec((1, QROWS, HALF // 2), lambda c: (1, 0, c))],
+        out_specs=spec,
         out_shape=jax.ShapeDtypeStruct((QROWS, HALF), BF16),
         compiler_params=PARAMS,
         cost_estimate=cost(1 << 19, 3 << 19),
-    )(quarter, grads, got)
+    )(kept, got)
 
 
 def sum_kernel(x_ref, own_ref, *refs):
@@ -236,7 +246,7 @@
     scale = jnp.sqrt((adam_sq + NORM_EPS) / (jnp.sum(shampoo * shampoo) + NORM_EPS))
     out_ref[...] = (shampoo * scale).astype(BF16)
     up_ref[...] = out_ref[pl.ds(pl.multiple_of((x_ref[0] & 1) * HROWS, HROWS), HROWS)]
-    down_ref[...] = out_ref[pl.ds(pl.multiple_of((x_ref[0] >> 1) * HROWS, HROWS), HROWS)]
+    down_ref[...] = out_ref[pl.ds(pl.multiple_of((1 - (x_ref[0] & 1)) * HROWS, HROWS), HROWS)]
 
 
 def left_stage(x, prods, roots):
@@ -256,7 +266,7 @@
 
 def place_kernel(spots, x_ref, z_ref, own_ref, *refs):
     srcs, out_ref, sems = refs[:-2], refs[-2], refs[-1]
-    halves = {"up": x_ref[0] & 1, "down": x_ref[0] >> 1}
+    halves = {"up": x_ref[0] & 1, "down": 1 - (x_ref[0] & 1)}
     copies = []
     for k, (src, ring, other, quarter, by) in enumerate(zip(srcs, *zip(*spots))):
         half = 0 if ring is None else (1 - halves[ring] if other else halves[ring])
@@ -318,17 +328,15 @@
     firsts = [partner(sends[h], steps[h]) for h in range(2)]
 
     low_second = after(second, sends[1])[:, :, 0].astype(BF16)
-    pre, root = pack(
-        z, own, sends[1], right_roots[:, 0], left_roots[:, 0], momentum[:, :, 0], low_second
-    )
+    states = left_roots[:, 0], momentum[:, :, 0], low_second
+    pre, root, *kept = pack(x, z, own, sends[1], quarters, right_roots[:, 0], *states)
     pre = exchange(pre, "z")
     firsts = [after(first, pre) for first in firsts]
     pre, root = mirror(pre), mirror(root)
     roots = gather_x(pre[:, :DROWS].reshape(QROWS, BS))
 
     seconds = [
-        partner(add_quarter(quarters, firsts[h], x ^ steps[1 - h], h), steps[1 - h])
-        for h in range(2)
+        partner(add_quarter(kept[h], firsts[h]), steps[1 - h]) for h in range(2)
     ]
     over_z = exchange(sum_quarter(quarters, firsts, seconds, x, own), "z")
     g_low, prod = right_stage(over_z, pre, after(root, *roots))
@@ -349,13 +357,8 @@
         ]
         waits, last = last, others
     up, down = (after(half, *waits) for half in (up, down))
-    up, down = shift(up[:QROWS], "z", NZ, 1), shift(down[QROWS:], "z", NZ, NZ - 1)
-    pieces += [
-        (up, "up", False, 0, NZ // 2),
-        (down, "down", False, 1, NZ // 2),
-        (partner(up, 1), "up", True, 0, NZ // 2),
-        (partner(down, 3), "down", True, 1, NZ // 2),
-    ]
+    up, down = shift(up, "z", NZ, 1), shift(down, "z", NZ, NZ - 1)
+    pieces += [(up, "up", False, 0, NZ // 2), (down, "down", False, 0, NZ // 2)]
 
     g = exchange(after(g_state, *waits).reshape(NZ, DROWS, BS), "z")
     g = in_order(own, g).astype(F32)[:, :, None]

time: 149 us -> 145 us (0.973)
  blocking collectives: 0 us -> 18.6 us
  waiting for transfers between devices: 67.4 us -> 54.6 us
  starting transfers between devices: 62 us -> 52.2 us
    all_to_all x0 -> x1, blocking collectives: none -> 18.6 us  [exchange(): return lax.all_to_all(value, axis, split_axis=0, concat_axis=0, tiled=True)]
    all_to_all x3 -> x2, waiting for transfers between devices: 10.5 us -> 1.78 us  [exchange(): return lax.all_to_all(value, axis, split_axis=0, concat_axis=0, tiled=True)]
    all_to_all x3 -> x2, starting transfers between devices: 21.5 us -> 13.9 us  [exchange(): return lax.all_to_all(value, axis, split_axis=0, concat_axis=0, tiled=True)]
    ppermute x14, waiting for transfers between devices: 17.2 us -> 14.5 us  [shift(): lax.ppermute(value, axis, [(k, (k + by) % size) for k in range(size)])]
    ppermute x12 -> x10, starting transfers between devices: 12.6 us -> 10.7 us  [partner(): return lax.ppermute(value, 'x', [(k, k ^ bits) for k in range(NX)])]
    ppermute x12 -> x10, waiting for transfers between devices: 19.8 us -> 18.4 us  [partner(): return lax.ppermute(value, 'x', [(k, k ^ bits) for k in range(NX)])]
    unnamed x9 -> x11, local copies, waits for them, and re-layouts: 3.18 us -> 3.07 us
  transfers between devices with their start and end apart: 32 -> 29, of which waited for: 14 -> 13; matrix products, arithmetic and copies ran while one was open for 2% -> 2% of each run, Pallas kernels for 2% -> 2%
where the time goes in v3:
time: 145 us; the launch traced here: 144 us
  waiting for transfers between devices  54.6 us (38%)
  starting transfers between devices  52.2 us (36%)
  blocking collectives  18.6 us (13%)
  Pallas kernels  12.3 us (8%)
  local copies, waits for them, and re-layouts  3.76 us (3%)
  other arithmetic  1.73 us (1%)
    ppermute x14, starting transfers between devices, shift(): lax.ppermute(value, axis, [(k, (k + by) % size) for k in range(size)])  20.1 us
    ppermute x3, waiting for transfers between devices, mirror(): return lax.ppermute(value, ('z', *OWN), pairs)  19.9 us
    all_to_all x1, blocking collectives, exchange(): return lax.all_to_all(value, axis, split_axis=0, concat_axis=0, tiled=True)  18.6 us
    ppermute x10, waiting for transfers between devices, partner(): return lax.ppermute(value, 'x', [(k, k ^ bits) for k in range(NX)])  18.4 us
    ppermute x14, waiting for transfers between devices, shift(): lax.ppermute(value, axis, [(k, (k + by) % size) for k in range(size)])  14.5 us
    all_to_all x2, starting transfers between devices, exchange(): return lax.all_to_all(value, axis, split_axis=0, concat_axis=0, tiled=True)  13.9 us
    ppermute x10, starting transfers between devices, partner(): return lax.ppermute(value, 'x', [(k, k ^ bits) for k in range(NX)])  10.7 us
    ppermute x3, starting transfers between devices, mirror(): return lax.ppermute(value, ('z', *OWN), pairs)  7.46 us
  transfers between devices with their start and end apart: 29, of which 13 were waited for; matrix products, arithmetic and copies ran while one was open for 2% of the time, Pallas kernels for 2%

profile of v3, /device:TPU:96, one launch (start us, length us, event | category | flops | bytes accessed | tf_op | source)
XLA Modules:
  0.0 144.1 jit_solution(1395501514217495960)
XLA Ops:
  0.6 2.5 %shard_map.76 = (bf16[2,128,2048]{2,1,0:T(8,128)(2,1)}, bf16[2,128,2048]{2,1,0:T(8,128)(2,1)}) custom-call(s32[1]{0:T(128)} %bitcast.x_ref, bf16[4,128,4096]{2,1,0:T(8,128)(2,1)} %bitcast.28), custom_call_target="tpu_custom_call" | custom-call | bytes 4194304 | tf_op jit(solution)/shard_map/pallas_call | solution.py:65
  3.1 1.6 %collective-permute-start = (bf16[2,128,2048]{2,1,0:T(8,128)(2,1)}, bf16[2,128,2048]{2,1,0:T(8,128)(2,1)S(1)}, u32[]{:S(2)}, u32[]{:S(2)}) collective-permute-start(bf16[2,128,2048]{2,1,0:T(8,128)(2,1)} %get-tuple-element.25), channel_id=1, source_target_pairs={{0,64},{64,0},{128,192},{192,128},{1,65},{65,1},{129,193},{193,129... | collective-permute-start | bytes 3145736 | tf_op jit(solution)/shard_map/ppermute | solution.py:302
  4.7 2.1 %collective-permute-start.2 = (bf16[2,128,2048]{2,1,0:T(8,128)(2,1)}, bf16[2,128,2048]{2,1,0:T(8,128)(2,1)S(1)}, u32[]{:S(2)}, u32[]{:S(2)}) collective-permute-start(bf16[2,128,2048]{2,1,0:T(8,128)(2,1)} %get-tuple-element.26.after_ref), channel_id=1, source_target_pairs={{0,192},{64,128},{128,64},{192,0},{1,193},{65,129},{129,65},{193,1... | collective-permute-start | bytes 3145736 | tf_op jit(solution)/shard_map/ppermute | solution.py:302
  6.8 0.7 copy.19
  7.5 2.6 %shard_map.77 = (bf16[8,48,512]{2,1,0:T(8,128)(2,1)}, bf16[512,512]{1,0:T(8,128)(2,1)}, bf16[128,2048]{1,0:T(8,128)(2,1)}, bf16[128,2048]{1,0:T(8,128)(2,1)}) custom-call(s32[1]{0:T(128)} %bitcast.x_ref, s32[1]{0:T(128)} %bitcast.1.z_ref, s32[1]{0:T(128)} %bitcast.2.own_ref, bf16[2,128,2048]{2,1,0:T(8,128)(2,1)} %get-tuple-element.26.after_ref, ...), custom_call_target="tpu_custom_call" | custom-call | bytes 4194304 | tf_op jit(solution)/shard_map/pallas_call | solution.py:122
  10.1 18.6 %all_to_all.15 = bf16[8,48,512]{2,1,0:T(8,128)(2,1)S(1)} all-to-all(bf16[8,48,512]{2,1,0:T(8,128)(2,1)} %get-tuple-element.28), channel_id=1, replica_groups=mesh['x'=4,'z'=8,'y'=4,'core'=2] {'z'}, dimensions={0} | all-to-all | bytes 786432 | tf_op jit(solution)/shard_map/all_to_all | solution.py:315
  28.7 1.0 copy-done.2
  29.8 0.3 shard_map.78
  30.1 2.4 %collective-permute-start.1 = (bf16[128,2048]{1,0:T(8,128)(2,1)S(1)}, bf16[128,2048]{1,0:T(8,128)(2,1)S(1)}, u32[]{:S(2)}, u32[]{:S(2)}) collective-permute-start(bf16[128,2048]{1,0:T(8,128)(2,1)S(1)} %shard_map.78), channel_id=1, source_target_pairs={{0,192},{64,128},{128,64},{192,0},{1,193},{65,129},{129,65},{193,1... | collective-permute-start | bytes 1572872 | tf_op jit(solution)/shard_map/ppermute | solution.py:302
  32.5 1.0 copy-done.1
  33.5 0.3 shard_map.79
  33.8 0.3 collective-permute-start.3
  34.2 9.6 %collective-permute-done.1.refs_2_ = bf16[128,2048]{1,0:T(8,128)(2,1)S(1)} collective-permute-done((bf16[128,2048]{1,0:T(8,128)(2,1)S(1)}, bf16[128,2048]{1,0:T(8,128)(2,1)S(1)}, u32[]{:S(2)}, u32[]{:S(2)}) %collective-permute-start.1) | collective-permute-done | bytes 524320 | tf_op jit(solution)/shard_map/ppermute | solution.py:302
  43.7 2.7 %collective-permute-done.3.refs_5_ = bf16[128,2048]{1,0:T(8,128)(2,1)S(1)} collective-permute-done((bf16[128,2048]{1,0:T(8,128)(2,1)S(1)}, bf16[128,2048]{1,0:T(8,128)(2,1)S(1)}, u32[]{:S(2)}, u32[]{:S(2)}) %collective-permute-start.3) | collective-permute-done | bytes 524320 | tf_op jit(solution)/shard_map/ppermute | solution.py:302
  46.4 1.7 %shard_map.80 = bf16[8,128,512]{2,1,0:T(8,128)(2,1)} custom-call(s32[1]{0:T(128)} %bitcast.x_ref, s32[1]{0:T(128)} %bitcast.2.own_ref, bf16[4,128,4096]{2,1,0:T(8,128)(2,1)S(1)} %bitcast.30, bf16[2,128,2048]{2,1,0:T(8,128)(2,1)S(1)} %collective-permute-done.got_ref.refs_1_, bf16[128,2048]{1,0:T(8,128)(2,1)S(1)} %collective-permute-done.1.refs_2_, ...), custom_call_target="tpu_custom_call" | custom-call | flops 1048576 | bytes 4194304 | tf_op jit(solution)/shard_map/pallas_call | solution.py:172
  48.2 7.7 %all-to-all-start.1 = ((bf16[8,128,512]{2,1,0:T(8,128)(2,1)}), bf16[8,128,512]{2,1,0:T(8,128)(2,1)S(1)}, u32[]{:S(2)}, u32[]{:S(2)}) async-start(bf16[8,128,512]{2,1,0:T(8,128)(2,1)} %shard_map.80), calls=%async_computation.1 | async-start | bytes 2097152 | tf_op jit(solution)/shard_map/all_to_all | solution.py:315
  55.8 1.9 %collective-permute-start.4 = (bf16[8,48,512]{2,1,0:T(8,128)(2,1)S(1)}, bf16[8,48,512]{2,1,0:T(8,128)(2,1)S(1)}, u32[]{:S(2)}, u32[]{:S(2)}) collective-permute-start(bf16[8,48,512]{2,1,0:T(8,128)(2,1)S(1)} %all_to_all.15), channel_id=1, source_target_pairs={{0,0},{1,7},{2,6},{3,5},{4,4},{5,3},{6,2},{7,1},{8,9},{9,8},{10,15... | collective-permute-start | bytes 1179656 | tf_op jit(solution)/shard_map/ppermute | solution.py:307
  57.7 3.6 %collective-permute-start.5 = (bf16[512,512]{1,0:T(8,128)(2,1)S(1)}, bf16[512,512]{1,0:T(8,128)(2,1)S(1)}, u32[]{:S(2)}, u32[]{:S(2)}) collective-permute-start(bf16[512,512]{1,0:T(8,128)(2,1)S(1)} %copy-done.4), channel_id=1, source_target_pairs={{0,0},{1,7},{2,6},{3,5},{4,4},{5,3},{6,2},{7,1},{8,9},{9,8},{10,15... | collective-permute-start | bytes 1572872 | tf_op jit(solution)/shard_map/ppermute | solution.py:307
  61.4 7.6 %collective-permute-done.4.pre_ref = bf16[8,48,512]{2,1,0:T(8,128)(2,1)S(1)} collective-permute-done((bf16[8,48,512]{2,1,0:T(8,128)(2,1)S(1)}, bf16[8,48,512]{2,1,0:T(8,128)(2,1)S(1)}, u32[]{:S(2)}, u32[]{:S(2)}) %collective-permute-start.4) | collective-permute-done | bytes 393248 | tf_op jit(solution)/shard_map/ppermute | solution.py:307
  69.0 0.4 collective-permute-start.6
  69.3 3.0 %collective-permute-start.7 = (bf16[128,512]{1,0:T(8,128)(2,1)S(1)}, bf16[128,512]{1,0:T(8,128)(2,1)S(1)}, u32[]{:S(2)}, u32[]{:S(2)}) collective-permute-start(bf16[128,512]{1,0:T(8,128)(2,1)S(1)} %bitcast.33), channel_id=1, source_target_pairs={{0,192},{64,0},{128,64},{192,128},{1,193},{65,1},{129,65},{193,129... | collective-permute-start | bytes 393224 | tf_op jit(solution)/shard_map/ppermute | solution.py:298
  72.3 7.9 %collective-permute-done.5.root_ref = bf16[512,512]{1,0:T(8,128)(2,1)S(1)} collective-permute-done((bf16[512,512]{1,0:T(8,128)(2,1)S(1)}, bf16[512,512]{1,0:T(8,128)(2,1)S(1)}, u32[]{:S(2)}, u32[]{:S(2)}) %collective-permute-start.5) | collective-permute-done | bytes 524320 | tf_op jit(solution)/shard_map/ppermute | solution.py:307
  80.2 0.5 shard_map.81
  80.7 0.4 collective-permute-start.9
  81.1 3.0 %collective-permute-start.10 = (bf16[144,512]{1,0:T(8,128)(2,1)S(1)}, bf16[144,512]{1,0:T(8,128)(2,1)S(1)}, u32[]{:S(2)}, u32[]{:S(2)}) collective-permute-start(bf16[144,512]{1,0:T(8,128)(2,1)S(1)} %get-tuple-element.35.refs_0_), channel_id=1, source_target_pairs={{0,192},{64,0},{128,64},{192,128},{1,193},{65,1},{129,65},{193,129... | collective-permute-start | bytes 442376 | tf_op jit(solution)/shard_map/ppermute | solution.py:298
  84.0 7.0 %collective-permute-done.9.refs_1_ = bf16[144,512]{1,0:T(8,128)(2,1)S(1)} collective-permute-done((bf16[144,512]{1,0:T(8,128)(2,1)S(1)}, bf16[144,512]{1,0:T(8,128)(2,1)S(1)}, u32[]{:S(2)}, u32[]{:S(2)}) %collective-permute-start.9) | collective-permute-done | bytes 147488 | tf_op jit(solution)/shard_map/ppermute | solution.py:298
  91.1 1.2 shard_map.82
  92.2 3.3 %collective-permute-start.12 = (bf16[256,512]{1,0:T(8,128)(2,1)S(1)}, bf16[256,512]{1,0:T(8,128)(2,1)S(1)}, u32[]{:S(2)}, u32[]{:S(2)}) collective-permute-start(bf16[256,512]{1,0:T(8,128)(2,1)S(1)} %get-tuple-element.37), channel_id=1, source_target_pairs={{0,8},{8,16},{16,24},{24,32},{32,40},{40,48},{48,56},{56,0},{1,9},... | collective-permute-start | bytes 786440 | tf_op jit(solution)/shard_map/ppermute | solution.py:298
  95.6 1.9 %collective-permute-start.16 = (bf16[128,512]{1,0:T(8,128)(2,1)S(1)}, bf16[128,512]{1,0:T(8,128)(2,1)}, u32[]{:S(2)}, u32[]{:S(2)}) collective-permute-start(bf16[128,512]{1,0:T(8,128)(2,1)S(1)} %get-tuple-element.39), channel_id=1, source_target_pairs={{0,0},{1,7},{2,6},{3,5},{4,4},{5,3},{6,2},{7,1},{8,9},{9,8},{10,15... | collective-permute-start | bytes 393224 | tf_op jit(solution)/shard_map/ppermute | solution.py:307
  97.5 4.5 %collective-permute-done.16 = bf16[128,512]{1,0:T(8,128)(2,1)} collective-permute-done((bf16[128,512]{1,0:T(8,128)(2,1)S(1)}, bf16[128,512]{1,0:T(8,128)(2,1)}, u32[]{:S(2)}, u32[]{:S(2)}) %collective-permute-start.16) | collective-permute-done | bytes 131104 | tf_op jit(solution)/shard_map/ppermute | solution.py:307
  102.0 5.3 %collective-permute-start.17 = (bf16[256,512]{1,0:T(8,128)(2,1)S(1)}, bf16[256,512]{1,0:T(8,128)(2,1)S(1)}, u32[]{:S(2)}, u32[]{:S(2)}) collective-permute-start(bf16[256,512]{1,0:T(8,128)(2,1)S(1)} %collective-permute-done.12.refs_1_), channel_id=1, source_target_pairs={{0,8},{8,16},{16,24},{24,32},{32,40},{40,48},{48,56},{56,0},{1,9},... | collective-permute-start | bytes 786440 | tf_op jit(solution)/shard_map/ppermute | solution.py:298
  107.3 1.4 collective-permute-start.15
  108.7 2.5 %collective-permute-done.17.refs_5_ = bf16[256,512]{1,0:T(8,128)(2,1)S(1)} collective-permute-done((bf16[256,512]{1,0:T(8,128)(2,1)S(1)}, bf16[256,512]{1,0:T(8,128)(2,1)S(1)}, u32[]{:S(2)}, u32[]{:S(2)}) %collective-permute-start.17) | collective-permute-done | bytes 262176 | tf_op jit(solution)/shard_map/ppermute | solution.py:298
  111.2 3.7 %collective-permute-done.18.refs_6_ = bf16[256,512]{1,0:T(8,128)(2,1)S(1)} collective-permute-done((bf16[256,512]{1,0:T(8,128)(2,1)S(1)}, bf16[256,512]{1,0:T(8,128)(2,1)S(1)}, u32[]{:S(2)}, u32[]{:S(2)}) %collective-permute-start.18) | collective-permute-done | bytes 262176 | tf_op jit(solution)/shard_map/ppermute | solution.py:298
  114.9 1.3 collective-permute-start.20
  116.2 2.1 %collective-permute-start.21 = (bf16[256,512]{1,0:T(8,128)(2,1)S(1)}, bf16[256,512]{1,0:T(8,128)(2,1)S(1)}, u32[]{:S(2)}, u32[]{:S(2)}) collective-permute-start(bf16[256,512]{1,0:T(8,128)(2,1)S(1)} %collective-permute-done.17.refs_5_), channel_id=1, source_target_pairs={{0,8},{8,16},{16,24},{24,32},{32,40},{40,48},{48,56},{56,0},{1,9},... | collective-permute-start | bytes 786440 | tf_op jit(solution)/shard_map/ppermute | solution.py:298
  118.3 4.2 %collective-permute-done.20.refs_8_ = bf16[256,512]{1,0:T(8,128)(2,1)S(1)} collective-permute-done((bf16[256,512]{1,0:T(8,128)(2,1)S(1)}, bf16[256,512]{1,0:T(8,128)(2,1)S(1)}, u32[]{:S(2)}, u32[]{:S(2)}) %collective-permute-start.20) | collective-permute-done | bytes 262176 | tf_op jit(solution)/shard_map/ppermute | solution.py:302
  122.4 6.3 %all-to-all-start.2 = ((bf16[8,16,512]{2,1,0:T(8,128)(2,1)}), bf16[8,16,512]{2,1,0:T(8,128)(2,1)S(1)}, u32[]{:S(2)}, u32[]{:S(2)}) async-start(bf16[8,16,512]{2,1,0:T(8,128)(2,1)} %bitcast.10), calls=%async_computation.2 | async-start | bytes 262144 | tf_op jit(solution)/shard_map/all_to_all | solution.py:315
  128.7 2.7 %collective-permute-start.25 = (bf16[256,512]{1,0:T(8,128)(2,1)S(1)}, bf16[256,512]{1,0:T(8,128)(2,1)S(1)}, u32[]{:S(2)}, u32[]{:S(2)}) collective-permute-start(bf16[256,512]{1,0:T(8,128)(2,1)S(1)} %collective-permute-done.21.refs_9_), channel_id=1, source_target_pairs={{0,8},{8,16},{16,24},{24,32},{32,40},{40,48},{48,56},{56,0},{1,9},... | collective-permute-start | bytes 786440 | tf_op jit(solution)/shard_map/ppermute | solution.py:298
  131.4 0.4 collective-permute-start.23
  131.7 1.3 collective-permute-start.24
  133.0 1.8 %all-to-all-done.2.src_ref = bf16[8,16,512]{2,1,0:T(8,128)(2,1)S(1)} async-done(((bf16[8,16,512]{2,1,0:T(8,128)(2,1)}), bf16[8,16,512]{2,1,0:T(8,128)(2,1)S(1)}, u32[]{:S(2)}, u32[]{:S(2)}) %all-to-all-start.2) | async-done | bytes 131104 | tf_op jit(solution)/shard_map/all_to_all | solution.py:315
  134.8 1.7 %fusion.4 = (f32[8,16,1,512]{3,1,0,2:T(8,128)S(1)}, bf16[8,16,1,512]{3,1,2,0:T(8,128)(2,1)}) fusion(bf16[8,16,512]{2,1,0:T(8,128)(2,1)S(1)} %shard_map.84, f32[8,16,1,512]{3,2,1,0:T(1,128)} %param.7, bf16[8,16,1,512]{3,1,2,0:T(8,128)(2,1)} %param.6), kind=kLoop, calls=%fused_computation.6 | loop fusion | flops 655360 | bytes 917504 | tf_op jit(solution)/shard_map/add | solution.py:37
  136.6 1.0 copy.12
  137.5 0.3 collective-permute-done.23.refs_11_
  137.9 1.6 %collective-permute-done.24.refs_12_ = bf16[256,512]{1,0:T(8,128)(2,1)} collective-permute-done((bf16[256,512]{1,0:T(8,128)(2,1)S(1)}, bf16[256,512]{1,0:T(8,128)(2,1)}, u32[]{:S(2)}, u32[]{:S(2)}) %collective-permute-start.24) | collective-permute-done | bytes 262176 | tf_op jit(solution)/shard_map/ppermute | solution.py:302
  139.4 1.3 collective-permute-done.26.refs_14_
  140.7 3.2 %shard_map.83 = bf16[512,4096]{1,0:T(8,128)(2,1)} custom-call(s32[1]{0:T(128)} %bitcast.x_ref, s32[1]{0:T(128)} %bitcast.1.z_ref, s32[1]{0:T(128)} %bitcast.2.own_ref, bf16[512,512]{1,0:T(8,128)(2,1)S(1)} %get-tuple-element.36.refs_0_, bf16[256,512]{1,0:T(8,128)(2,1)S(1)} %collective-permute-done.12.refs_1_, ...), custom_call_target="tpu_custom_call" | custom-call | bytes 8388608 | tf_op jit(solution)/shard_map/pallas_call | solution.py:286
  (34 shorter events, 0.1 us)
Async XLA Ops:
  0.6 6.2 %copy-start.3 = (f32[8,16,1,512]{3,2,1,0:T(1,128)S(1)}, f32[8,16,1,512]{3,2,1,0:T(1,128)}, u32[]{:S(2)}) copy-start(f32[8,16,1,512]{3,2,1,0:T(1,128)} %param.7) | copy-start | bytes 786436
  3.1 25.6 %collective-permute-start = (bf16[2,128,2048]{2,1,0:T(8,128)(2,1)}, bf16[2,128,2048]{2,1,0:T(8,128)(2,1)S(1)}, u32[]{:S(2)}, u32[]{:S(2)}) collective-permute-start(bf16[2,128,2048]{2,1,0:T(8,128)(2,1)} %get-tuple-element.25), channel_id=1, source_target_pairs={{0,64},{64,0},{128,192},{192,128},{1,65},{65,1},{129,193},{193,129... | collective-permute-start | bytes 3145736 | tf_op jit(solution)/shard_map/ppermute | solution.py:302
  4.7 27.8 %collective-permute-start.2 = (bf16[2,128,2048]{2,1,0:T(8,128)(2,1)}, bf16[2,128,2048]{2,1,0:T(8,128)(2,1)S(1)}, u32[]{:S(2)}, u32[]{:S(2)}) collective-permute-start(bf16[2,128,2048]{2,1,0:T(8,128)(2,1)} %get-tuple-element.26.after_ref), channel_id=1, source_target_pairs={{0,192},{64,128},{128,64},{192,0},{1,193},{65,129},{129,65},{193,1... | collective-permute-start | bytes 3145736 | tf_op jit(solution)/shard_map/ppermute | solution.py:302
  10.1 36.3 %copy-start = (bf16[1,512,4096]{2,1,0:T(8,128)(2,1)S(1)}, bf16[1,512,4096]{2,1,0:T(8,128)(2,1)}, u32[]{:S(2)}) copy-start(bf16[1,512,4096]{2,1,0:T(8,128)(2,1)} %param.5) | copy-start | bytes 12582916
  28.7 1.0 copy-start.2
  30.1 13.7 %collective-permute-start.1 = (bf16[128,2048]{1,0:T(8,128)(2,1)S(1)}, bf16[128,2048]{1,0:T(8,128)(2,1)S(1)}, u32[]{:S(2)}, u32[]{:S(2)}) collective-permute-start(bf16[128,2048]{1,0:T(8,128)(2,1)S(1)} %shard_map.78), channel_id=1, source_target_pairs={{0,192},{64,128},{128,64},{192,0},{1,193},{65,129},{129,65},{193,1... | collective-permute-start | bytes 1572872 | tf_op jit(solution)/shard_map/ppermute | solution.py:302
  32.5 1.0 copy-start.1
  33.8 23.9 %copy-start.4 = (bf16[512,512]{1,0:T(8,128)(2,1)S(1)}, bf16[512,512]{1,0:T(8,128)(2,1)}, u32[]{:S(2)}) copy-start(bf16[512,512]{1,0:T(8,128)(2,1)} %get-tuple-element.33) | copy-start | bytes 1572868
  33.8 12.6 %collective-permute-start.3 = (bf16[128,2048]{1,0:T(8,128)(2,1)S(1)}, bf16[128,2048]{1,0:T(8,128)(2,1)S(1)}, u32[]{:S(2)}, u32[]{:S(2)}) collective-permute-start(bf16[128,2048]{1,0:T(8,128)(2,1)S(1)} %shard_map.79), channel_id=1, source_target_pairs={{0,64},{64,0},{128,192},{192,128},{1,65},{65,1},{129,193},{193,129... | collective-permute-start | bytes 1572872 | tf_op jit(solution)/shard_map/ppermute | solution.py:302
  48.2 32.1 %all-to-all-start.1 = ((bf16[8,128,512]{2,1,0:T(8,128)(2,1)}), bf16[8,128,512]{2,1,0:T(8,128)(2,1)S(1)}, u32[]{:S(2)}, u32[]{:S(2)}) async-start(bf16[8,128,512]{2,1,0:T(8,128)(2,1)} %shard_map.80), calls=%async_computation.1 | async-start | bytes 2097152 | tf_op jit(solution)/shard_map/all_to_all | solution.py:315
  55.8 13.2 %collective-permute-start.4 = (bf16[8,48,512]{2,1,0:T(8,128)(2,1)S(1)}, bf16[8,48,512]{2,1,0:T(8,128)(2,1)S(1)}, u32[]{:S(2)}, u32[]{:S(2)}) collective-permute-start(bf16[8,48,512]{2,1,0:T(8,128)(2,1)S(1)} %all_to_all.15), channel_id=1, source_target_pairs={{0,0},{1,7},{2,6},{3,5},{4,4},{5,3},{6,2},{7,1},{8,9},{9,8},{10,15... | collective-permute-start | bytes 1179656 | tf_op jit(solution)/shard_map/ppermute | solution.py:307
  57.7 22.5 %collective-permute-start.5 = (bf16[512,512]{1,0:T(8,128)(2,1)S(1)}, bf16[512,512]{1,0:T(8,128)(2,1)S(1)}, u32[]{:S(2)}, u32[]{:S(2)}) collective-permute-start(bf16[512,512]{1,0:T(8,128)(2,1)S(1)} %copy-done.4), channel_id=1, source_target_pairs={{0,0},{1,7},{2,6},{3,5},{4,4},{5,3},{6,2},{7,1},{8,9},{9,8},{10,15... | collective-permute-start | bytes 1572872 | tf_op jit(solution)/shard_map/ppermute | solution.py:307
  69.0 11.2 %collective-permute-start.6 = (bf16[128,512]{1,0:T(8,128)(2,1)S(1)}, bf16[128,512]{1,0:T(8,128)(2,1)S(1)}, u32[]{:S(2)}, u32[]{:S(2)}) collective-permute-start(bf16[128,512]{1,0:T(8,128)(2,1)S(1)} %bitcast.32), channel_id=1, source_target_pairs={{0,64},{64,128},{128,192},{192,0},{1,65},{65,129},{129,193},{193,1... | collective-permute-start | bytes 393224 | tf_op jit(solution)/shard_map/ppermute | solution.py:298
  69.3 10.9 %collective-permute-start.7 = (bf16[128,512]{1,0:T(8,128)(2,1)S(1)}, bf16[128,512]{1,0:T(8,128)(2,1)S(1)}, u32[]{:S(2)}, u32[]{:S(2)}) collective-permute-start(bf16[128,512]{1,0:T(8,128)(2,1)S(1)} %bitcast.33), channel_id=1, source_target_pairs={{0,192},{64,0},{128,64},{192,128},{1,193},{65,1},{129,65},{193,129... | collective-permute-start | bytes 393224 | tf_op jit(solution)/shard_map/ppermute | solution.py:298
  72.3 7.9 %collective-permute-start.8 = (bf16[128,512]{1,0:T(8,128)(2,1)S(1)}, bf16[128,512]{1,0:T(8,128)(2,1)S(1)}, u32[]{:S(2)}, u32[]{:S(2)}) collective-permute-start(bf16[128,512]{1,0:T(8,128)(2,1)S(1)} %bitcast.34), channel_id=1, source_target_pairs={{0,128},{64,192},{128,0},{192,64},{1,129},{65,193},{129,1},{193,65... | collective-permute-start | bytes 393224 | tf_op jit(solution)/shard_map/ppermute | solution.py:298
  80.7 10.3 %collective-permute-start.9 = (bf16[144,512]{1,0:T(8,128)(2,1)S(1)}, bf16[144,512]{1,0:T(8,128)(2,1)S(1)}, u32[]{:S(2)}, u32[]{:S(2)}) collective-permute-start(bf16[144,512]{1,0:T(8,128)(2,1)S(1)} %get-tuple-element.35.refs_0_), channel_id=1, source_target_pairs={{0,64},{64,128},{128,192},{192,0},{1,65},{65,129},{129,193},{193,1... | collective-permute-start | bytes 442376 | tf_op jit(solution)/shard_map/ppermute | solution.py:298
  81.1 10.0 %collective-permute-start.10 = (bf16[144,512]{1,0:T(8,128)(2,1)S(1)}, bf16[144,512]{1,0:T(8,128)(2,1)S(1)}, u32[]{:S(2)}, u32[]{:S(2)}) collective-permute-start(bf16[144,512]{1,0:T(8,128)(2,1)S(1)} %get-tuple-element.35.refs_0_), channel_id=1, source_target_pairs={{0,192},{64,0},{128,64},{192,128},{1,193},{65,1},{129,65},{193,129... | collective-permute-start | bytes 442376 | tf_op jit(solution)/shard_map/ppermute | solution.py:298
  84.0 7.0 %collective-permute-start.11 = (bf16[144,512]{1,0:T(8,128)(2,1)S(1)}, bf16[144,512]{1,0:T(8,128)(2,1)S(1)}, u32[]{:S(2)}, u32[]{:S(2)}) collective-permute-start(bf16[144,512]{1,0:T(8,128)(2,1)S(1)} %get-tuple-element.35.refs_0_), channel_id=1, source_target_pairs={{0,128},{64,192},{128,0},{192,64},{1,129},{65,193},{129,1},{193,65... | collective-permute-start | bytes 442376 | tf_op jit(solution)/shard_map/ppermute | solution.py:298
  92.2 9.7 %collective-permute-start.12 = (bf16[256,512]{1,0:T(8,128)(2,1)S(1)}, bf16[256,512]{1,0:T(8,128)(2,1)S(1)}, u32[]{:S(2)}, u32[]{:S(2)}) collective-permute-start(bf16[256,512]{1,0:T(8,128)(2,1)S(1)} %get-tuple-element.37), channel_id=1, source_target_pairs={{0,8},{8,16},{16,24},{24,32},{32,40},{40,48},{48,56},{56,0},{1,9},... | collective-permute-start | bytes 786440 | tf_op jit(solution)/shard_map/ppermute | solution.py:298
  95.6 11.7 %collective-permute-start.13 = (bf16[256,512]{1,0:T(8,128)(2,1)S(1)}, bf16[256,512]{1,0:T(8,128)(2,1)S(1)}, u32[]{:S(2)}, u32[]{:S(2)}) collective-permute-start(bf16[256,512]{1,0:T(8,128)(2,1)S(1)} %get-tuple-element.38), channel_id=1, source_target_pairs={{0,56},{8,0},{16,8},{24,16},{32,24},{40,32},{48,40},{56,48},{1,57}... | collective-permute-start | bytes 786440 | tf_op jit(solution)/shard_map/ppermute | solution.py:298
  95.6 6.4 %collective-permute-start.16 = (bf16[128,512]{1,0:T(8,128)(2,1)S(1)}, bf16[128,512]{1,0:T(8,128)(2,1)}, u32[]{:S(2)}, u32[]{:S(2)}) collective-permute-start(bf16[128,512]{1,0:T(8,128)(2,1)S(1)} %get-tuple-element.39), channel_id=1, source_target_pairs={{0,0},{1,7},{2,6},{3,5},{4,4},{5,3},{6,2},{7,1},{8,9},{9,8},{10,15... | collective-permute-start | bytes 393224 | tf_op jit(solution)/shard_map/ppermute | solution.py:307
  102.0 9.2 %collective-permute-start.17 = (bf16[256,512]{1,0:T(8,128)(2,1)S(1)}, bf16[256,512]{1,0:T(8,128)(2,1)S(1)}, u32[]{:S(2)}, u32[]{:S(2)}) collective-permute-start(bf16[256,512]{1,0:T(8,128)(2,1)S(1)} %collective-permute-done.12.refs_1_), channel_id=1, source_target_pairs={{0,8},{8,16},{16,24},{24,32},{32,40},{40,48},{48,56},{56,0},{1,9},... | collective-permute-start | bytes 786440 | tf_op jit(solution)/shard_map/ppermute | solution.py:298
  107.3 7.6 %collective-permute-start.18 = (bf16[256,512]{1,0:T(8,128)(2,1)S(1)}, bf16[256,512]{1,0:T(8,128)(2,1)S(1)}, u32[]{:S(2)}, u32[]{:S(2)}) collective-permute-start(bf16[256,512]{1,0:T(8,128)(2,1)S(1)} %collective-permute-done.13.refs_2_), channel_id=1, source_target_pairs={{0,56},{8,0},{16,8},{24,16},{32,24},{40,32},{48,40},{56,48},{1,57}... | collective-permute-start | bytes 786440 | tf_op jit(solution)/shard_map/ppermute | solution.py:298
  107.3 8.9 %collective-permute-start.14 = (bf16[256,512]{1,0:T(8,128)(2,1)S(1)}, bf16[256,512]{1,0:T(8,128)(2,1)S(1)}, u32[]{:S(2)}, u32[]{:S(2)}) collective-permute-start(bf16[256,512]{1,0:T(8,128)(2,1)S(1)} %collective-permute-done.12.refs_1_), channel_id=1, source_target_pairs={{0,64},{64,0},{128,192},{192,128},{1,65},{65,1},{129,193},{193,129... | collective-permute-start | bytes 786440 | tf_op jit(solution)/shard_map/ppermute | solution.py:302
  107.3 8.9 %collective-permute-start.15 = (bf16[256,512]{1,0:T(8,128)(2,1)S(1)}, bf16[256,512]{1,0:T(8,128)(2,1)S(1)}, u32[]{:S(2)}, u32[]{:S(2)}) collective-permute-start(bf16[256,512]{1,0:T(8,128)(2,1)S(1)} %collective-permute-done.13.refs_2_), channel_id=1, source_target_pairs={{0,192},{64,128},{128,64},{192,0},{1,193},{65,129},{129,65},{193,1... | collective-permute-start | bytes 786440 | tf_op jit(solution)/shard_map/ppermute | solution.py:302
  111.2 7.1 %collective-permute-start.19 = (bf16[256,512]{1,0:T(8,128)(2,1)S(1)}, bf16[256,512]{1,0:T(8,128)(2,1)S(1)}, u32[]{:S(2)}, u32[]{:S(2)}) collective-permute-start(bf16[256,512]{1,0:T(8,128)(2,1)S(1)} %collective-permute-done.17.refs_5_), channel_id=1, source_target_pairs={{0,64},{64,0},{128,192},{192,128},{1,65},{65,1},{129,193},{193,129... | collective-permute-start | bytes 786440 | tf_op jit(solution)/shard_map/ppermute | solution.py:302
  114.9 7.6 %collective-permute-start.20 = (bf16[256,512]{1,0:T(8,128)(2,1)S(1)}, bf16[256,512]{1,0:T(8,128)(2,1)S(1)}, u32[]{:S(2)}, u32[]{:S(2)}) collective-permute-start(bf16[256,512]{1,0:T(8,128)(2,1)S(1)} %collective-permute-done.18.refs_6_), channel_id=1, source_target_pairs={{0,192},{64,128},{128,64},{192,0},{1,193},{65,129},{129,65},{193,1... | collective-permute-start | bytes 786440 | tf_op jit(solution)/shard_map/ppermute | solution.py:302
  116.2 12.6 %collective-permute-start.21 = (bf16[256,512]{1,0:T(8,128)(2,1)S(1)}, bf16[256,512]{1,0:T(8,128)(2,1)S(1)}, u32[]{:S(2)}, u32[]{:S(2)}) collective-permute-start(bf16[256,512]{1,0:T(8,128)(2,1)S(1)} %collective-permute-done.17.refs_5_), channel_id=1, source_target_pairs={{0,8},{8,16},{16,24},{24,32},{32,40},{40,48},{48,56},{56,0},{1,9},... | collective-permute-start | bytes 786440 | tf_op jit(solution)/shard_map/ppermute | solution.py:298
  118.2 13.1 %collective-permute-start.22 = (bf16[256,512]{1,0:T(8,128)(2,1)S(1)}, bf16[256,512]{1,0:T(8,128)(2,1)S(1)}, u32[]{:S(2)}, u32[]{:S(2)}) collective-permute-start(bf16[256,512]{1,0:T(8,128)(2,1)S(1)} %collective-permute-done.18.refs_6_), channel_id=1, source_target_pairs={{0,56},{8,0},{16,8},{24,16},{32,24},{40,32},{48,40},{56,48},{1,57}... | collective-permute-start | bytes 786440 | tf_op jit(solution)/shard_map/ppermute | solution.py:298
  122.4 12.4 %all-to-all-start.2 = ((bf16[8,16,512]{2,1,0:T(8,128)(2,1)}), bf16[8,16,512]{2,1,0:T(8,128)(2,1)S(1)}, u32[]{:S(2)}, u32[]{:S(2)}) async-start(bf16[8,16,512]{2,1,0:T(8,128)(2,1)} %bitcast.10), calls=%async_computation.2 | async-start | bytes 262144 | tf_op jit(solution)/shard_map/all_to_all | solution.py:315
  128.7 10.7 %collective-permute-start.25 = (bf16[256,512]{1,0:T(8,128)(2,1)S(1)}, bf16[256,512]{1,0:T(8,128)(2,1)S(1)}, u32[]{:S(2)}, u32[]{:S(2)}) collective-permute-start(bf16[256,512]{1,0:T(8,128)(2,1)S(1)} %collective-permute-done.21.refs_9_), channel_id=1, source_target_pairs={{0,8},{8,16},{16,24},{24,32},{32,40},{40,48},{48,56},{56,0},{1,9},... | collective-permute-start | bytes 786440 | tf_op jit(solution)/shard_map/ppermute | solution.py:298
  131.4 6.5 %collective-permute-start.23 = (bf16[256,512]{1,0:T(8,128)(2,1)S(1)}, bf16[256,512]{1,0:T(8,128)(2,1)}, u32[]{:S(2)}, u32[]{:S(2)}) collective-permute-start(bf16[256,512]{1,0:T(8,128)(2,1)S(1)} %collective-permute-done.21.refs_9_), channel_id=1, source_target_pairs={{0,64},{64,0},{128,192},{192,128},{1,65},{65,1},{129,193},{193,129... | collective-permute-start | bytes 786440 | tf_op jit(solution)/shard_map/ppermute | solution.py:302
  131.7 7.7 %collective-permute-start.24 = (bf16[256,512]{1,0:T(8,128)(2,1)S(1)}, bf16[256,512]{1,0:T(8,128)(2,1)}, u32[]{:S(2)}, u32[]{:S(2)}) collective-permute-start(bf16[256,512]{1,0:T(8,128)(2,1)S(1)} %collective-permute-done.22.refs_10_), channel_id=1, source_target_pairs={{0,192},{64,128},{128,64},{192,0},{1,193},{65,129},{129,65},{193,1... | collective-permute-start | bytes 786440 | tf_op jit(solution)/shard_map/ppermute | solution.py:302
  133.0 7.7 %collective-permute-start.26 = (bf16[256,512]{1,0:T(8,128)(2,1)S(1)}, bf16[256,512]{1,0:T(8,128)(2,1)}, u32[]{:S(2)}, u32[]{:S(2)}) collective-permute-start(bf16[256,512]{1,0:T(8,128)(2,1)S(1)} %collective-permute-done.22.refs_10_), channel_id=1, source_target_pairs={{0,56},{8,0},{16,8},{24,16},{32,24},{40,32},{48,40},{56,48},{1,57}... | collective-permute-start | bytes 786440 | tf_op jit(solution)/shard_map/ppermute | solution.py:298

commit v4 on v3

--- a/solution.py
+++ b/solution.py
@@ -73,7 +73,7 @@
     )(x, grads)
 
 
-def pack_kernel(x_ref, z_ref, own_ref, after_ref, grads_ref, right_ref, *refs):
+def pack_kernel(x_ref, z_ref, own_ref, grads_ref, right_ref, *refs):
     states, (out_ref, root_ref, left_ref, rest_ref) = refs[:-8], refs[-8:-4]
     hold_ref, hold_root_ref, hold_kept_ref, sems = refs[-4:]
     loads = [
@@ -115,13 +115,13 @@
         store.wait()
 
 
-def pack(x, z, own, after, grads, right, *states):
+def pack(x, z, own, grads, right, *states):
     anywhere = pl.BlockSpec(memory_space=pl.ANY)
     smem = pl.BlockSpec(memory_space=pltpu.SMEM)
     shapes = [(NZ, len(states) * DROWS, BS), (BS, BS), (QROWS, HALF), (QROWS, HALF)]
     return pl.pallas_call(
         pack_kernel,
-        in_specs=[smem] * 3 + [anywhere] * (3 + len(states)),
+        in_specs=[smem] * 3 + [anywhere] * (2 + len(states)),
         out_specs=(anywhere,) * 4,
         out_shape=tuple(jax.ShapeDtypeStruct(shape, BF16) for shape in shapes),
         scratch_shapes=[
@@ -130,9 +130,9 @@
             pltpu.VMEM((2, QROWS, HALF), BF16),
             pltpu.SemaphoreType.DMA((2, NZ + 3)),
         ],
-        compiler_params=ALL_VMEM,
+        compiler_params=pltpu.CompilerParams(vmem_limit_bytes=48 * 1024 * 1024),
         cost_estimate=cost(0, 4 << 20),
-    )(x, z, own, after, grads, right, *states)
+    )(x, z, own, grads, right, *states)
 
 
 def add_kernel(kept_ref, got_ref, out_ref):
@@ -329,7 +329,7 @@
 
     low_second = after(second, sends[1])[:, :, 0].astype(BF16)
     states = left_roots[:, 0], momentum[:, :, 0], low_second
-    pre, root, *kept = pack(x, z, own, sends[1], quarters, right_roots[:, 0], *states)
+    pre, root, *kept = pack(x, z, own, quarters, right_roots[:, 0], *states)
     pre = exchange(pre, "z")
     firsts = [after(first, pre) for first in firsts]
     pre, root = mirror(pre), mirror(root)

time: 145 us -> 143 us (0.986)
  local copies, waits for them, and re-layouts: 3.76 us -> 1.02 us
  waiting for transfers between devices: 54.6 us -> 56.2 us
    unnamed x11 -> x9, local copies, waits for them, and re-layouts: 3.07 us -> 0.99 us
  transfers between devices with their start and end apart: 29 -> 29, of which waited for: 13 -> 14; matrix products, arithmetic and copies ran while one was open for 2% -> 2% of each run, Pallas kernels for 2% -> 2%
where the time goes in v4:
time: 143 us; the launch traced here: 142 us
  waiting for transfers between devices  56.2 us (39%)
  starting transfers between devices  52.4 us (37%)
  blocking collectives  18.5 us (13%)
  Pallas kernels  11.5 us (8%)
  other arithmetic  1.69 us (1%)
    ppermute x3, waiting for transfers between devices, mirror(): return lax.ppermute(value, ('z', *OWN), pairs)  20.2 us
    ppermute x14, starting transfers between devices, shift(): lax.ppermute(value, axis, [(k, (k + by) % size) for k in range(size)])  19.9 us
    ppermute x10, waiting for transfers between devices, partner(): return lax.ppermute(value, 'x', [(k, k ^ bits) for k in range(NX)])  19.3 us
    all_to_all x1, blocking collectives, exchange(): return lax.all_to_all(value, axis, split_axis=0, concat_axis=0, tiled=True)  18.5 us
    all_to_all x2, starting transfers between devices, exchange(): return lax.all_to_all(value, axis, split_axis=0, concat_axis=0, tiled=True)  14.5 us
    ppermute x14, waiting for transfers between devices, shift(): lax.ppermute(value, axis, [(k, (k + by) % size) for k in range(size)])  14.4 us
    ppermute x10, starting transfers between devices, partner(): return lax.ppermute(value, 'x', [(k, k ^ bits) for k in range(NX)])  10.6 us
    ppermute x3, starting transfers between devices, mirror(): return lax.ppermute(value, ('z', *OWN), pairs)  7.46 us
  transfers between devices with their start and end apart: 29, of which 14 were waited for; matrix products, arithmetic and copies ran while one was open for 2% of the time, Pallas kernels for 2%

profile of v4, /device:TPU:96, one launch (start us, length us, event | category | flops | bytes accessed | tf_op | source)
XLA Modules:
  0.0 142.3 jit_solution(17355885405920120473)
XLA Ops:
  0.6 0.0 copy-start.3
  0.7 2.5 %shard_map.76 = (bf16[2,128,2048]{2,1,0:T(8,128)(2,1)}, bf16[2,128,2048]{2,1,0:T(8,128)(2,1)}) custom-call(s32[1]{0:T(128)} %bitcast.x_ref, bf16[4,128,4096]{2,1,0:T(8,128)(2,1)} %bitcast.28), custom_call_target="tpu_custom_call" | custom-call | bytes 4194304 | tf_op jit(solution)/shard_map/pallas_call | solution.py:65
  3.2 1.6 %collective-permute-start = (bf16[2,128,2048]{2,1,0:T(8,128)(2,1)}, bf16[2,128,2048]{2,1,0:T(8,128)(2,1)S(1)}, u32[]{:S(2)}, u32[]{:S(2)}) collective-permute-start(bf16[2,128,2048]{2,1,0:T(8,128)(2,1)} %get-tuple-element.25), channel_id=1, source_target_pairs={{0,64},{64,0},{128,192},{192,128},{1,65},{65,1},{129,193},{193,129... | collective-permute-start | bytes 3145736 | tf_op jit(solution)/shard_map/ppermute | solution.py:302
  4.7 2.1 %collective-permute-start.2 = (bf16[2,128,2048]{2,1,0:T(8,128)(2,1)}, bf16[2,128,2048]{2,1,0:T(8,128)(2,1)S(1)}, u32[]{:S(2)}, u32[]{:S(2)}) collective-permute-start(bf16[2,128,2048]{2,1,0:T(8,128)(2,1)} %get-tuple-element.26), channel_id=1, source_target_pairs={{0,192},{64,128},{128,64},{192,0},{1,193},{65,129},{129,65},{193,1... | collective-permute-start | bytes 3145736 | tf_op jit(solution)/shard_map/ppermute | solution.py:302
  6.9 1.7 %shard_map.77 = (bf16[8,48,512]{2,1,0:T(8,128)(2,1)S(1)}, bf16[512,512]{1,0:T(8,128)(2,1)S(1)}, bf16[128,2048]{1,0:T(8,128)(2,1)S(1)}, bf16[128,2048]{1,0:T(8,128)(2,1)S(1)}) custom-call(s32[1]{0:T(128)} %bitcast.x_ref, s32[1]{0:T(128)} %bitcast.1.z_ref, s32[1]{0:T(128)} %bitcast.2.own_ref, bf16[4,128,4096]{2,1,0:T(8,128)(2,1)} %bitcast.29, ...), custom_call_target="tpu_custom_call" | custom-call | bytes 4194304 | tf_op jit(solution)/shard_map/pallas_call | solution.py:122
  8.6 0.0 copy-start
  8.6 18.5 %all_to_all.15 = bf16[8,48,512]{2,1,0:T(8,128)(2,1)} all-to-all(bf16[8,48,512]{2,1,0:T(8,128)(2,1)S(1)} %get-tuple-element.28), channel_id=1, replica_groups=mesh['x'=4,'z'=8,'y'=4,'core'=2] {'z'}, dimensions={0} | all-to-all | bytes 786432 | tf_op jit(solution)/shard_map/all_to_all | solution.py:315
  27.1 1.2 collective-permute-done.got_ref.refs_1_
  28.4 0.3 shard_map.78
  28.7 2.8 %collective-permute-start.1 = (bf16[128,2048]{1,0:T(8,128)(2,1)S(1)}, bf16[128,2048]{1,0:T(8,128)(2,1)S(1)}, u32[]{:S(2)}, u32[]{:S(2)}) collective-permute-start(bf16[128,2048]{1,0:T(8,128)(2,1)S(1)} %shard_map.78), channel_id=1, source_target_pairs={{0,192},{64,128},{128,64},{192,0},{1,193},{65,129},{129,65},{193,1... | collective-permute-start | bytes 1572872 | tf_op jit(solution)/shard_map/ppermute | solution.py:302
  31.5 0.3 shard_map.79
  31.8 0.3 collective-permute-start.3
  32.1 10.6 %collective-permute-done.1.refs_2_ = bf16[128,2048]{1,0:T(8,128)(2,1)S(1)} collective-permute-done((bf16[128,2048]{1,0:T(8,128)(2,1)S(1)}, bf16[128,2048]{1,0:T(8,128)(2,1)S(1)}, u32[]{:S(2)}, u32[]{:S(2)}) %collective-permute-start.1) | collective-permute-done | bytes 524320 | tf_op jit(solution)/shard_map/ppermute | solution.py:302
  42.7 1.6 %collective-permute-done.3.refs_5_ = bf16[128,2048]{1,0:T(8,128)(2,1)S(1)} collective-permute-done((bf16[128,2048]{1,0:T(8,128)(2,1)S(1)}, bf16[128,2048]{1,0:T(8,128)(2,1)S(1)}, u32[]{:S(2)}, u32[]{:S(2)}) %collective-permute-start.3) | collective-permute-done | bytes 524320 | tf_op jit(solution)/shard_map/ppermute | solution.py:302
  44.4 1.7 %shard_map.80 = bf16[8,128,512]{2,1,0:T(8,128)(2,1)} custom-call(s32[1]{0:T(128)} %bitcast.x_ref, s32[1]{0:T(128)} %bitcast.2.own_ref, bf16[4,128,4096]{2,1,0:T(8,128)(2,1)S(1)} %bitcast.30, bf16[2,128,2048]{2,1,0:T(8,128)(2,1)S(1)} %collective-permute-done.got_ref.refs_1_, bf16[128,2048]{1,0:T(8,128)(2,1)S(1)} %collective-permute-done.1.refs_2_, ...), custom_call_target="tpu_custom_call" | custom-call | flops 1048576 | bytes 4194304 | tf_op jit(solution)/shard_map/pallas_call | solution.py:172
  46.1 7.7 %all-to-all-start.1 = ((bf16[8,128,512]{2,1,0:T(8,128)(2,1)}), bf16[8,128,512]{2,1,0:T(8,128)(2,1)S(1)}, u32[]{:S(2)}, u32[]{:S(2)}) async-start(bf16[8,128,512]{2,1,0:T(8,128)(2,1)} %shard_map.80), calls=%async_computation.1 | async-start | bytes 2097152 | tf_op jit(solution)/shard_map/all_to_all | solution.py:315
  53.8 1.9 %collective-permute-start.4 = (bf16[8,48,512]{2,1,0:T(8,128)(2,1)}, bf16[8,48,512]{2,1,0:T(8,128)(2,1)S(1)}, u32[]{:S(2)}, u32[]{:S(2)}) collective-permute-start(bf16[8,48,512]{2,1,0:T(8,128)(2,1)} %all_to_all.15), channel_id=1, source_target_pairs={{0,0},{1,7},{2,6},{3,5},{4,4},{5,3},{6,2},{7,1},{8,9},{9,8},{10,15... | collective-permute-start | bytes 1179656 | tf_op jit(solution)/shard_map/ppermute | solution.py:307
  55.7 3.6 %collective-permute-start.5 = (bf16[512,512]{1,0:T(8,128)(2,1)S(1)}, bf16[512,512]{1,0:T(8,128)(2,1)S(1)}, u32[]{:S(2)}, u32[]{:S(2)}) collective-permute-start(bf16[512,512]{1,0:T(8,128)(2,1)S(1)} %get-tuple-element.33), channel_id=1, source_target_pairs={{0,0},{1,7},{2,6},{3,5},{4,4},{5,3},{6,2},{7,1},{8,9},{9,8},{10,15... | collective-permute-start | bytes 1572872 | tf_op jit(solution)/shard_map/ppermute | solution.py:307
  59.3 7.8 %collective-permute-done.4.pre_ref = bf16[8,48,512]{2,1,0:T(8,128)(2,1)S(1)} collective-permute-done((bf16[8,48,512]{2,1,0:T(8,128)(2,1)}, bf16[8,48,512]{2,1,0:T(8,128)(2,1)S(1)}, u32[]{:S(2)}, u32[]{:S(2)}) %collective-permute-start.4) | collective-permute-done | bytes 393248 | tf_op jit(solution)/shard_map/ppermute | solution.py:307
  67.1 0.4 collective-permute-start.6
  67.5 3.0 %collective-permute-start.7 = (bf16[128,512]{1,0:T(8,128)(2,1)S(1)}, bf16[128,512]{1,0:T(8,128)(2,1)S(1)}, u32[]{:S(2)}, u32[]{:S(2)}) collective-permute-start(bf16[128,512]{1,0:T(8,128)(2,1)S(1)} %bitcast.35), channel_id=1, source_target_pairs={{0,192},{64,0},{128,64},{192,128},{1,193},{65,1},{129,65},{193,129... | collective-permute-start | bytes 393224 | tf_op jit(solution)/shard_map/ppermute | solution.py:298
  70.5 7.9 %collective-permute-done.5.root_ref = bf16[512,512]{1,0:T(8,128)(2,1)S(1)} collective-permute-done((bf16[512,512]{1,0:T(8,128)(2,1)S(1)}, bf16[512,512]{1,0:T(8,128)(2,1)S(1)}, u32[]{:S(2)}, u32[]{:S(2)}) %collective-permute-start.5) | collective-permute-done | bytes 524320 | tf_op jit(solution)/shard_map/ppermute | solution.py:307
  78.4 0.5 shard_map.81
  78.9 0.4 collective-permute-start.9
  79.2 3.0 %collective-permute-start.10 = (bf16[144,512]{1,0:T(8,128)(2,1)S(1)}, bf16[144,512]{1,0:T(8,128)(2,1)S(1)}, u32[]{:S(2)}, u32[]{:S(2)}) collective-permute-start(bf16[144,512]{1,0:T(8,128)(2,1)S(1)} %get-tuple-element.35.refs_0_), channel_id=1, source_target_pairs={{0,192},{64,0},{128,64},{192,128},{1,193},{65,1},{129,65},{193,129... | collective-permute-start | bytes 442376 | tf_op jit(solution)/shard_map/ppermute | solution.py:298
  82.2 7.0 %collective-permute-done.9.refs_1_ = bf16[144,512]{1,0:T(8,128)(2,1)S(1)} collective-permute-done((bf16[144,512]{1,0:T(8,128)(2,1)S(1)}, bf16[144,512]{1,0:T(8,128)(2,1)S(1)}, u32[]{:S(2)}, u32[]{:S(2)}) %collective-permute-start.9) | collective-permute-done | bytes 147488 | tf_op jit(solution)/shard_map/ppermute | solution.py:298
  89.2 1.2 shard_map.82
  90.4 3.2 %collective-permute-start.12 = (bf16[256,512]{1,0:T(8,128)(2,1)S(1)}, bf16[256,512]{1,0:T(8,128)(2,1)S(1)}, u32[]{:S(2)}, u32[]{:S(2)}) collective-permute-start(bf16[256,512]{1,0:T(8,128)(2,1)S(1)} %get-tuple-element.37), channel_id=1, source_target_pairs={{0,8},{8,16},{16,24},{24,32},{32,40},{40,48},{48,56},{56,0},{1,9},... | collective-permute-start | bytes 786440 | tf_op jit(solution)/shard_map/ppermute | solution.py:298
  93.6 1.9 %collective-permute-start.16 = (bf16[128,512]{1,0:T(8,128)(2,1)S(1)}, bf16[128,512]{1,0:T(8,128)(2,1)}, u32[]{:S(2)}, u32[]{:S(2)}) collective-permute-start(bf16[128,512]{1,0:T(8,128)(2,1)S(1)} %get-tuple-element.39), channel_id=1, source_target_pairs={{0,0},{1,7},{2,6},{3,5},{4,4},{5,3},{6,2},{7,1},{8,9},{9,8},{10,15... | collective-permute-start | bytes 393224 | tf_op jit(solution)/shard_map/ppermute | solution.py:307
  95.6 4.5 %collective-permute-done.16 = bf16[128,512]{1,0:T(8,128)(2,1)} collective-permute-done((bf16[128,512]{1,0:T(8,128)(2,1)S(1)}, bf16[128,512]{1,0:T(8,128)(2,1)}, u32[]{:S(2)}, u32[]{:S(2)}) %collective-permute-start.16) | collective-permute-done | bytes 131104 | tf_op jit(solution)/shard_map/ppermute | solution.py:307
  100.0 5.3 %collective-permute-start.17 = (bf16[256,512]{1,0:T(8,128)(2,1)S(1)}, bf16[256,512]{1,0:T(8,128)(2,1)S(1)}, u32[]{:S(2)}, u32[]{:S(2)}) collective-permute-start(bf16[256,512]{1,0:T(8,128)(2,1)S(1)} %collective-permute-done.12.refs_1_), channel_id=1, source_target_pairs={{0,8},{8,16},{16,24},{24,32},{32,40},{40,48},{48,56},{56,0},{1,9},... | collective-permute-start | bytes 786440 | tf_op jit(solution)/shard_map/ppermute | solution.py:298
  105.4 1.4 collective-permute-start.15
  106.7 2.5 %collective-permute-done.17.refs_5_ = bf16[256,512]{1,0:T(8,128)(2,1)S(1)} collective-permute-done((bf16[256,512]{1,0:T(8,128)(2,1)S(1)}, bf16[256,512]{1,0:T(8,128)(2,1)S(1)}, u32[]{:S(2)}, u32[]{:S(2)}) %collective-permute-start.17) | collective-permute-done | bytes 262176 | tf_op jit(solution)/shard_map/ppermute | solution.py:298
  109.2 3.7 %collective-permute-done.18.refs_6_ = bf16[256,512]{1,0:T(8,128)(2,1)S(1)} collective-permute-done((bf16[256,512]{1,0:T(8,128)(2,1)S(1)}, bf16[256,512]{1,0:T(8,128)(2,1)S(1)}, u32[]{:S(2)}, u32[]{:S(2)}) %collective-permute-start.18) | collective-permute-done | bytes 262176 | tf_op jit(solution)/shard_map/ppermute | solution.py:298
  112.9 1.3 collective-permute-start.20
  114.2 1.9 %collective-permute-start.21 = (bf16[256,512]{1,0:T(8,128)(2,1)S(1)}, bf16[256,512]{1,0:T(8,128)(2,1)S(1)}, u32[]{:S(2)}, u32[]{:S(2)}) collective-permute-start(bf16[256,512]{1,0:T(8,128)(2,1)S(1)} %collective-permute-done.17.refs_5_), channel_id=1, source_target_pairs={{0,8},{8,16},{16,24},{24,32},{32,40},{40,48},{48,56},{56,0},{1,9},... | collective-permute-start | bytes 786440 | tf_op jit(solution)/shard_map/ppermute | solution.py:298
  116.2 0.1 collective-permute-start.22
  116.3 4.3 %collective-permute-done.20.refs_8_ = bf16[256,512]{1,0:T(8,128)(2,1)S(1)} collective-permute-done((bf16[256,512]{1,0:T(8,128)(2,1)S(1)}, bf16[256,512]{1,0:T(8,128)(2,1)S(1)}, u32[]{:S(2)}, u32[]{:S(2)}) %collective-permute-start.20) | collective-permute-done | bytes 262176 | tf_op jit(solution)/shard_map/ppermute | solution.py:302
  120.5 6.8 %all-to-all-start.2 = ((bf16[8,16,512]{2,1,0:T(8,128)(2,1)}), bf16[8,16,512]{2,1,0:T(8,128)(2,1)S(1)}, u32[]{:S(2)}, u32[]{:S(2)}) async-start(bf16[8,16,512]{2,1,0:T(8,128)(2,1)} %bitcast.10), calls=%async_computation.2 | async-start | bytes 262144 | tf_op jit(solution)/shard_map/all_to_all | solution.py:315
  127.3 2.7 %collective-permute-start.25 = (bf16[256,512]{1,0:T(8,128)(2,1)S(1)}, bf16[256,512]{1,0:T(8,128)(2,1)}, u32[]{:S(2)}, u32[]{:S(2)}) collective-permute-start(bf16[256,512]{1,0:T(8,128)(2,1)S(1)} %collective-permute-done.21.refs_9_), channel_id=1, source_target_pairs={{0,8},{8,16},{16,24},{24,32},{32,40},{40,48},{48,56},{56,0},{1,9},... | collective-permute-start | bytes 786440 | tf_op jit(solution)/shard_map/ppermute | solution.py:298
  130.0 1.1 collective-permute-start.24
  131.1 2.4 %all-to-all-done.2.src_ref = bf16[8,16,512]{2,1,0:T(8,128)(2,1)S(1)} async-done(((bf16[8,16,512]{2,1,0:T(8,128)(2,1)}), bf16[8,16,512]{2,1,0:T(8,128)(2,1)S(1)}, u32[]{:S(2)}, u32[]{:S(2)}) %all-to-all-start.2) | async-done | bytes 131104 | tf_op jit(solution)/shard_map/all_to_all | solution.py:315
  133.5 1.7 %fusion.4 = (f32[8,16,1,512]{3,1,0,2:T(8,128)S(1)}, bf16[8,16,1,512]{3,1,2,0:T(8,128)(2,1)}) fusion(bf16[8,16,512]{2,1,0:T(8,128)(2,1)S(1)} %shard_map.84, f32[8,16,1,512]{3,2,1,0:T(1,128)} %param.7, bf16[8,16,1,512]{3,1,2,0:T(8,128)(2,1)S(1)} %copy-done.1), kind=kLoop, calls=%fused_computation.6 | loop fusion | flops 655360 | bytes 917504 | tf_op jit(solution)/shard_map/add | solution.py:37
  135.2 1.0 copy.12
  136.2 0.3 collective-permute-done.23.refs_11_
  136.5 1.2 collective-permute-done.24.refs_12_
  137.7 1.2 collective-permute-done.26.refs_14_
  138.9 3.3 %shard_map.83 = bf16[512,4096]{1,0:T(8,128)(2,1)} custom-call(s32[1]{0:T(128)} %bitcast.x_ref, s32[1]{0:T(128)} %bitcast.1.z_ref, s32[1]{0:T(128)} %bitcast.2.own_ref, bf16[512,512]{1,0:T(8,128)(2,1)S(1)} %get-tuple-element.36.refs_0_, bf16[256,512]{1,0:T(8,128)(2,1)S(1)} %collective-permute-done.12.refs_1_, ...), custom_call_target="tpu_custom_call" | custom-call | bytes 8388608 | tf_op jit(solution)/shard_map/pallas_call | solution.py:286
  (32 shorter events, 0.1 us)
Async XLA Ops:
  0.6 6.2 %copy-start.3 = (f32[8,16,1,512]{3,2,1,0:T(1,128)S(1)}, f32[8,16,1,512]{3,2,1,0:T(1,128)}, u32[]{:S(2)}) copy-start(f32[8,16,1,512]{3,2,1,0:T(1,128)} %param.7) | copy-start | bytes 786436
  0.6 6.2 %copy-start.2 = (bf16[8,1,16,512]{3,2,1,0:T(8,128)(2,1)S(1)}, bf16[8,1,16,512]{3,2,1,0:T(8,128)(2,1)}, u32[]{:S(2)}) copy-start(bf16[8,1,16,512]{3,2,1,0:T(8,128)(2,1)} %param.8) | copy-start | bytes 393220
  0.7 6.2 %copy-start.1 = (bf16[8,16,1,512]{3,1,2,0:T(8,128)(2,1)S(1)}, bf16[8,16,1,512]{3,1,2,0:T(8,128)(2,1)}, u32[]{:S(2)}) copy-start(bf16[8,16,1,512]{3,1,2,0:T(8,128)(2,1)} %param.6) | copy-start | bytes 393220
  3.2 25.2 %collective-permute-start = (bf16[2,128,2048]{2,1,0:T(8,128)(2,1)}, bf16[2,128,2048]{2,1,0:T(8,128)(2,1)S(1)}, u32[]{:S(2)}, u32[]{:S(2)}) collective-permute-start(bf16[2,128,2048]{2,1,0:T(8,128)(2,1)} %get-tuple-element.25), channel_id=1, source_target_pairs={{0,64},{64,0},{128,192},{192,128},{1,65},{65,1},{129,193},{193,129... | collective-permute-start | bytes 3145736 | tf_op jit(solution)/shard_map/ppermute | solution.py:302
  4.7 26.8 %collective-permute-start.2 = (bf16[2,128,2048]{2,1,0:T(8,128)(2,1)}, bf16[2,128,2048]{2,1,0:T(8,128)(2,1)S(1)}, u32[]{:S(2)}, u32[]{:S(2)}) collective-permute-start(bf16[2,128,2048]{2,1,0:T(8,128)(2,1)} %get-tuple-element.26), channel_id=1, source_target_pairs={{0,192},{64,128},{128,64},{192,0},{1,193},{65,129},{129,65},{193,1... | collective-permute-start | bytes 3145736 | tf_op jit(solution)/shard_map/ppermute | solution.py:302
  8.6 35.8 %copy-start = (bf16[1,512,4096]{2,1,0:T(8,128)(2,1)S(1)}, bf16[1,512,4096]{2,1,0:T(8,128)(2,1)}, u32[]{:S(2)}) copy-start(bf16[1,512,4096]{2,1,0:T(8,128)(2,1)} %param.5) | copy-start | bytes 12582916
  28.7 14.1 %collective-permute-start.1 = (bf16[128,2048]{1,0:T(8,128)(2,1)S(1)}, bf16[128,2048]{1,0:T(8,128)(2,1)S(1)}, u32[]{:S(2)}, u32[]{:S(2)}) collective-permute-start(bf16[128,2048]{1,0:T(8,128)(2,1)S(1)} %shard_map.78), channel_id=1, source_target_pairs={{0,192},{64,128},{128,64},{192,0},{1,193},{65,129},{129,65},{193,1... | collective-permute-start | bytes 1572872 | tf_op jit(solution)/shard_map/ppermute | solution.py:302
  31.8 12.6 %collective-permute-start.3 = (bf16[128,2048]{1,0:T(8,128)(2,1)S(1)}, bf16[128,2048]{1,0:T(8,128)(2,1)S(1)}, u32[]{:S(2)}, u32[]{:S(2)}) collective-permute-start(bf16[128,2048]{1,0:T(8,128)(2,1)S(1)} %shard_map.79), channel_id=1, source_target_pairs={{0,64},{64,0},{128,192},{192,128},{1,65},{65,1},{129,193},{193,129... | collective-permute-start | bytes 1572872 | tf_op jit(solution)/shard_map/ppermute | solution.py:302
  46.1 32.3 %all-to-all-start.1 = ((bf16[8,128,512]{2,1,0:T(8,128)(2,1)}), bf16[8,128,512]{2,1,0:T(8,128)(2,1)S(1)}, u32[]{:S(2)}, u32[]{:S(2)}) async-start(bf16[8,128,512]{2,1,0:T(8,128)(2,1)} %shard_map.80), calls=%async_computation.1 | async-start | bytes 2097152 | tf_op jit(solution)/shard_map/all_to_all | solution.py:315
  53.8 13.4 %collective-permute-start.4 = (bf16[8,48,512]{2,1,0:T(8,128)(2,1)}, bf16[8,48,512]{2,1,0:T(8,128)(2,1)S(1)}, u32[]{:S(2)}, u32[]{:S(2)}) collective-permute-start(bf16[8,48,512]{2,1,0:T(8,128)(2,1)} %all_to_all.15), channel_id=1, source_target_pairs={{0,0},{1,7},{2,6},{3,5},{4,4},{5,3},{6,2},{7,1},{8,9},{9,8},{10,15... | collective-permute-start | bytes 1179656 | tf_op jit(solution)/shard_map/ppermute | solution.py:307
  55.7 22.7 %collective-permute-start.5 = (bf16[512,512]{1,0:T(8,128)(2,1)S(1)}, bf16[512,512]{1,0:T(8,128)(2,1)S(1)}, u32[]{:S(2)}, u32[]{:S(2)}) collective-permute-start(bf16[512,512]{1,0:T(8,128)(2,1)S(1)} %get-tuple-element.33), channel_id=1, source_target_pairs={{0,0},{1,7},{2,6},{3,5},{4,4},{5,3},{6,2},{7,1},{8,9},{9,8},{10,15... | collective-permute-start | bytes 1572872 | tf_op jit(solution)/shard_map/ppermute | solution.py:307
  67.1 11.2 %collective-permute-start.6 = (bf16[128,512]{1,0:T(8,128)(2,1)S(1)}, bf16[128,512]{1,0:T(8,128)(2,1)S(1)}, u32[]{:S(2)}, u32[]{:S(2)}) collective-permute-start(bf16[128,512]{1,0:T(8,128)(2,1)S(1)} %bitcast.34), channel_id=1, source_target_pairs={{0,64},{64,128},{128,192},{192,0},{1,65},{65,129},{129,193},{193,1... | collective-permute-start | bytes 393224 | tf_op jit(solution)/shard_map/ppermute | solution.py:298
  67.5 10.9 %collective-permute-start.7 = (bf16[128,512]{1,0:T(8,128)(2,1)S(1)}, bf16[128,512]{1,0:T(8,128)(2,1)S(1)}, u32[]{:S(2)}, u32[]{:S(2)}) collective-permute-start(bf16[128,512]{1,0:T(8,128)(2,1)S(1)} %bitcast.35), channel_id=1, source_target_pairs={{0,192},{64,0},{128,64},{192,128},{1,193},{65,1},{129,65},{193,129... | collective-permute-start | bytes 393224 | tf_op jit(solution)/shard_map/ppermute | solution.py:298
  70.5 7.9 %collective-permute-start.8 = (bf16[128,512]{1,0:T(8,128)(2,1)S(1)}, bf16[128,512]{1,0:T(8,128)(2,1)S(1)}, u32[]{:S(2)}, u32[]{:S(2)}) collective-permute-start(bf16[128,512]{1,0:T(8,128)(2,1)S(1)} %bitcast.36), channel_id=1, source_target_pairs={{0,128},{64,192},{128,0},{192,64},{1,129},{65,193},{129,1},{193,65... | collective-permute-start | bytes 393224 | tf_op jit(solution)/shard_map/ppermute | solution.py:298
  78.9 10.3 %collective-permute-start.9 = (bf16[144,512]{1,0:T(8,128)(2,1)S(1)}, bf16[144,512]{1,0:T(8,128)(2,1)S(1)}, u32[]{:S(2)}, u32[]{:S(2)}) collective-permute-start(bf16[144,512]{1,0:T(8,128)(2,1)S(1)} %get-tuple-element.35.refs_0_), channel_id=1, source_target_pairs={{0,64},{64,128},{128,192},{192,0},{1,65},{65,129},{129,193},{193,1... | collective-permute-start | bytes 442376 | tf_op jit(solution)/shard_map/ppermute | solution.py:298
  79.2 10.0 %collective-permute-start.10 = (bf16[144,512]{1,0:T(8,128)(2,1)S(1)}, bf16[144,512]{1,0:T(8,128)(2,1)S(1)}, u32[]{:S(2)}, u32[]{:S(2)}) collective-permute-start(bf16[144,512]{1,0:T(8,128)(2,1)S(1)} %get-tuple-element.35.refs_0_), channel_id=1, source_target_pairs={{0,192},{64,0},{128,64},{192,128},{1,193},{65,1},{129,65},{193,129... | collective-permute-start | bytes 442376 | tf_op jit(solution)/shard_map/ppermute | solution.py:298
  82.2 7.0 %collective-permute-start.11 = (bf16[144,512]{1,0:T(8,128)(2,1)S(1)}, bf16[144,512]{1,0:T(8,128)(2,1)S(1)}, u32[]{:S(2)}, u32[]{:S(2)}) collective-permute-start(bf16[144,512]{1,0:T(8,128)(2,1)S(1)} %get-tuple-element.35.refs_0_), channel_id=1, source_target_pairs={{0,128},{64,192},{128,0},{192,64},{1,129},{65,193},{129,1},{193,65... | collective-permute-start | bytes 442376 | tf_op jit(solution)/shard_map/ppermute | solution.py:298
  90.4 9.6 %collective-permute-start.12 = (bf16[256,512]{1,0:T(8,128)(2,1)S(1)}, bf16[256,512]{1,0:T(8,128)(2,1)S(1)}, u32[]{:S(2)}, u32[]{:S(2)}) collective-permute-start(bf16[256,512]{1,0:T(8,128)(2,1)S(1)} %get-tuple-element.37), channel_id=1, source_target_pairs={{0,8},{8,16},{16,24},{24,32},{32,40},{40,48},{48,56},{56,0},{1,9},... | collective-permute-start | bytes 786440 | tf_op jit(solution)/shard_map/ppermute | solution.py:298
  93.6 11.7 %collective-permute-start.13 = (bf16[256,512]{1,0:T(8,128)(2,1)S(1)}, bf16[256,512]{1,0:T(8,128)(2,1)S(1)}, u32[]{:S(2)}, u32[]{:S(2)}) collective-permute-start(bf16[256,512]{1,0:T(8,128)(2,1)S(1)} %get-tuple-element.38), channel_id=1, source_target_pairs={{0,56},{8,0},{16,8},{24,16},{32,24},{40,32},{48,40},{56,48},{1,57}... | collective-permute-start | bytes 786440 | tf_op jit(solution)/shard_map/ppermute | solution.py:298
  93.6 6.4 %collective-permute-start.16 = (bf16[128,512]{1,0:T(8,128)(2,1)S(1)}, bf16[128,512]{1,0:T(8,128)(2,1)}, u32[]{:S(2)}, u32[]{:S(2)}) collective-permute-start(bf16[128,512]{1,0:T(8,128)(2,1)S(1)} %get-tuple-element.39), channel_id=1, source_target_pairs={{0,0},{1,7},{2,6},{3,5},{4,4},{5,3},{6,2},{7,1},{8,9},{9,8},{10,15... | collective-permute-start | bytes 393224 | tf_op jit(solution)/shard_map/ppermute | solution.py:307
  100.0 9.2 %collective-permute-start.17 = (bf16[256,512]{1,0:T(8,128)(2,1)S(1)}, bf16[256,512]{1,0:T(8,128)(2,1)S(1)}, u32[]{:S(2)}, u32[]{:S(2)}) collective-permute-start(bf16[256,512]{1,0:T(8,128)(2,1)S(1)} %collective-permute-done.12.refs_1_), channel_id=1, source_target_pairs={{0,8},{8,16},{16,24},{24,32},{32,40},{40,48},{48,56},{56,0},{1,9},... | collective-permute-start | bytes 786440 | tf_op jit(solution)/shard_map/ppermute | solution.py:298
  105.3 7.6 %collective-permute-start.18 = (bf16[256,512]{1,0:T(8,128)(2,1)S(1)}, bf16[256,512]{1,0:T(8,128)(2,1)S(1)}, u32[]{:S(2)}, u32[]{:S(2)}) collective-permute-start(bf16[256,512]{1,0:T(8,128)(2,1)S(1)} %collective-permute-done.13.refs_2_), channel_id=1, source_target_pairs={{0,56},{8,0},{16,8},{24,16},{32,24},{40,32},{48,40},{56,48},{1,57}... | collective-permute-start | bytes 786440 | tf_op jit(solution)/shard_map/ppermute | solution.py:298
  105.3 8.9 %collective-permute-start.14 = (bf16[256,512]{1,0:T(8,128)(2,1)S(1)}, bf16[256,512]{1,0:T(8,128)(2,1)S(1)}, u32[]{:S(2)}, u32[]{:S(2)}) collective-permute-start(bf16[256,512]{1,0:T(8,128)(2,1)S(1)} %collective-permute-done.12.refs_1_), channel_id=1, source_target_pairs={{0,64},{64,0},{128,192},{192,128},{1,65},{65,1},{129,193},{193,129... | collective-permute-start | bytes 786440 | tf_op jit(solution)/shard_map/ppermute | solution.py:302
  105.4 8.9 %collective-permute-start.15 = (bf16[256,512]{1,0:T(8,128)(2,1)S(1)}, bf16[256,512]{1,0:T(8,128)(2,1)S(1)}, u32[]{:S(2)}, u32[]{:S(2)}) collective-permute-start(bf16[256,512]{1,0:T(8,128)(2,1)S(1)} %collective-permute-done.13.refs_2_), channel_id=1, source_target_pairs={{0,192},{64,128},{128,64},{192,0},{1,193},{65,129},{129,65},{193,1... | collective-permute-start | bytes 786440 | tf_op jit(solution)/shard_map/ppermute | solution.py:302
  109.2 7.0 %collective-permute-start.19 = (bf16[256,512]{1,0:T(8,128)(2,1)S(1)}, bf16[256,512]{1,0:T(8,128)(2,1)S(1)}, u32[]{:S(2)}, u32[]{:S(2)}) collective-permute-start(bf16[256,512]{1,0:T(8,128)(2,1)S(1)} %collective-permute-done.17.refs_5_), channel_id=1, source_target_pairs={{0,64},{64,0},{128,192},{192,128},{1,65},{65,1},{129,193},{193,129... | collective-permute-start | bytes 786440 | tf_op jit(solution)/shard_map/ppermute | solution.py:302
  112.9 7.6 %collective-permute-start.20 = (bf16[256,512]{1,0:T(8,128)(2,1)S(1)}, bf16[256,512]{1,0:T(8,128)(2,1)S(1)}, u32[]{:S(2)}, u32[]{:S(2)}) collective-permute-start(bf16[256,512]{1,0:T(8,128)(2,1)S(1)} %collective-permute-done.18.refs_6_), channel_id=1, source_target_pairs={{0,192},{64,128},{128,64},{192,0},{1,193},{65,129},{129,65},{193,1... | collective-permute-start | bytes 786440 | tf_op jit(solution)/shard_map/ppermute | solution.py:302
  114.2 13.1 %collective-permute-start.21 = (bf16[256,512]{1,0:T(8,128)(2,1)S(1)}, bf16[256,512]{1,0:T(8,128)(2,1)S(1)}, u32[]{:S(2)}, u32[]{:S(2)}) collective-permute-start(bf16[256,512]{1,0:T(8,128)(2,1)S(1)} %collective-permute-done.17.refs_5_), channel_id=1, source_target_pairs={{0,8},{8,16},{16,24},{24,32},{32,40},{40,48},{48,56},{56,0},{1,9},... | collective-permute-start | bytes 786440 | tf_op jit(solution)/shard_map/ppermute | solution.py:298
  116.2 13.8 %collective-permute-start.22 = (bf16[256,512]{1,0:T(8,128)(2,1)S(1)}, bf16[256,512]{1,0:T(8,128)(2,1)S(1)}, u32[]{:S(2)}, u32[]{:S(2)}) collective-permute-start(bf16[256,512]{1,0:T(8,128)(2,1)S(1)} %collective-permute-done.18.refs_6_), channel_id=1, source_target_pairs={{0,56},{8,0},{16,8},{24,16},{32,24},{40,32},{48,40},{56,48},{1,57}... | collective-permute-start | bytes 786440 | tf_op jit(solution)/shard_map/ppermute | solution.py:298
  120.5 13.0 %all-to-all-start.2 = ((bf16[8,16,512]{2,1,0:T(8,128)(2,1)}), bf16[8,16,512]{2,1,0:T(8,128)(2,1)S(1)}, u32[]{:S(2)}, u32[]{:S(2)}) async-start(bf16[8,16,512]{2,1,0:T(8,128)(2,1)} %bitcast.10), calls=%async_computation.2 | async-start | bytes 262144 | tf_op jit(solution)/shard_map/all_to_all | solution.py:315
  127.3 10.4 %collective-permute-start.25 = (bf16[256,512]{1,0:T(8,128)(2,1)S(1)}, bf16[256,512]{1,0:T(8,128)(2,1)}, u32[]{:S(2)}, u32[]{:S(2)}) collective-permute-start(bf16[256,512]{1,0:T(8,128)(2,1)S(1)} %collective-permute-done.21.refs_9_), channel_id=1, source_target_pairs={{0,8},{8,16},{16,24},{24,32},{32,40},{40,48},{48,56},{56,0},{1,9},... | collective-permute-start | bytes 786440 | tf_op jit(solution)/shard_map/ppermute | solution.py:298
  130.0 6.5 %collective-permute-start.23 = (bf16[256,512]{1,0:T(8,128)(2,1)S(1)}, bf16[256,512]{1,0:T(8,128)(2,1)}, u32[]{:S(2)}, u32[]{:S(2)}) collective-permute-start(bf16[256,512]{1,0:T(8,128)(2,1)S(1)} %collective-permute-done.21.refs_9_), channel_id=1, source_target_pairs={{0,64},{64,0},{128,192},{192,128},{1,65},{65,1},{129,193},{193,129... | collective-permute-start | bytes 786440 | tf_op jit(solution)/shard_map/ppermute | solution.py:302
  130.0 7.7 %collective-permute-start.24 = (bf16[256,512]{1,0:T(8,128)(2,1)S(1)}, bf16[256,512]{1,0:T(8,128)(2,1)}, u32[]{:S(2)}, u32[]{:S(2)}) collective-permute-start(bf16[256,512]{1,0:T(8,128)(2,1)S(1)} %collective-permute-done.22.refs_10_), channel_id=1, source_target_pairs={{0,192},{64,128},{128,64},{192,0},{1,193},{65,129},{129,65},{193,1... | collective-permute-start | bytes 786440 | tf_op jit(solution)/shard_map/ppermute | solution.py:302
  131.1 7.8 %collective-permute-start.26 = (bf16[256,512]{1,0:T(8,128)(2,1)S(1)}, bf16[256,512]{1,0:T(8,128)(2,1)}, u32[]{:S(2)}, u32[]{:S(2)}) collective-permute-start(bf16[256,512]{1,0:T(8,128)(2,1)S(1)} %collective-permute-done.22.refs_10_), channel_id=1, source_target_pairs={{0,56},{8,0},{16,8},{24,16},{32,24},{40,32},{48,40},{56,48},{1,57}... | collective-permute-start | bytes 786440 | tf_op jit(solution)/shard_map/ppermute | solution.py:298
